TPU v7x, 512 devices: a whole 4x8x8 slice. The times are simulated.
512 devices in a mesh: dp: 16 (over z, x_hi), vocab: 32 (over x_lo, y, core).
Axes of the slice: x: 4 (x_hi: 2, x_lo: 2; x = x_hi * 2 + x_lo), y: 8, z: 8, core: 2. Of those that a mesh axis runs over, the one named last changes fastest.
Arguments:
- hidden: bfloat16 [1024, 4608], P('dp'), may hold values from -300 to 300
- labels: int32 [1024], P('dp'), may hold values from 0 to 131071
- unembed: bfloat16 [4608, 131072], P(None, ('dp', 'vocab')), may hold values from -0.09375 to 0.09375
- in_proj: bfloat16 [4608, 64], replicated, may hold values from -0.09375 to 0.09375
- out_proj: float32 [131072, 64], P(('dp', 'vocab')), may hold values from -6 to 6
- left_inv: float32 [64, 64], replicated, may hold values from -1 to 4
- right_inv: float32 [64, 64], replicated, may hold values from -1 to 4
- queries: float32 [16, 256, 4096], P('dp', 'vocab'), may hold values from -0.012 to 0.012
Outputs:
- scores: float32 [16, 16, 256], P('dp', None, 'vocab')
All inputs are finite; a program needn't handle non-finite values.
Results may differ from a plain program's by a relative error of at most 0.00065.
Values may be sent and summed in bfloat16 or wider, within the bound.
No kernel may reach another device: no remote copies, remote signals or barrier semaphores. Data moves between devices by JAX's collectives and lax.ppermute only.
A program may use at most 128 MiB of HBM per device.

v0:
```python
import jax
import jax.numpy as jnp
from jax import lax
from jax.sharding import PartitionSpec as P

PRECISE = lax.Precision.HIGHEST


def shifted(value, axis, by):
    devices = lax.axis_size(axis)
    return lax.ppermute(value, axis, [(i, (i + by) % devices) for i in range(devices)])


def local(hidden, labels, unembed, in_proj, out_proj, left_inv, right_inv, queries):
    every_hidden, every_label = (
        lax.all_gather(hidden, "dp", axis=0, tiled=True),
        lax.all_gather(labels, "dp", axis=0, tiled=True),
    )
    logits = jnp.dot(every_hidden, unembed, preferred_element_type=jnp.float32)
    columns_dev = unembed.shape[1]
    seq_rows = hidden.shape[0]
    shard_index = lax.axis_index("dp") * lax.axis_size("vocab") + lax.axis_index("vocab")
    column_ids = shard_index * columns_dev + lax.iota(jnp.int32, columns_dev)
    label_mask = (every_label[:, None] == column_ids[None, :]).astype(jnp.float32)
    label_term = jnp.dot(label_mask, out_proj, precision=PRECISE)
    row_offset = lax.axis_index("dp") * seq_rows
    largest = lax.pmax(jnp.max(logits, axis=1), ("dp", "vocab"))
    exponent = jnp.exp(logits - largest[:, None])
    partial_sums = lax.psum(
        (jnp.sum(exponent, axis=1), jnp.dot(exponent, out_proj, precision=PRECISE), label_term),
        "vocab",
    )
    totals, spread, label_sum = lax.psum((partial_sums[0], partial_sums[1], partial_sums[2]), "dp")
    totals = lax.dynamic_slice_in_dim(totals, row_offset, seq_rows, 0)
    spread = lax.dynamic_slice_in_dim(spread, row_offset, seq_rows, 0)
    label_sum = lax.dynamic_slice_in_dim(label_sum, row_offset, seq_rows, 0)
    projected = spread / totals[:, None] - label_sum
    mapped = jnp.dot(hidden, in_proj, preferred_element_type=jnp.float32)
    feature = jnp.dot(mapped.T, projected, precision=PRECISE)
    precond = jnp.dot(jnp.dot(left_inv, feature, precision=PRECISE), right_inv, precision=PRECISE)
    flattened = precond.reshape(-1)
    group_count = lax.axis_size("dp")
    own_group = lax.axis_index("dp")
    query_block = queries[0]

    def place_scores(scores, block_now, source):
        row_scores = jnp.dot(block_now, flattened, precision=PRECISE)
        return lax.dynamic_update_slice_in_dim(scores, row_scores[None, :], source, 0)

    scores = jnp.zeros((group_count, query_block.shape[0]), jnp.float32)
    scores = place_scores(scores, query_block, own_group)

    def turn(turn_index, carry):
        scores_now, block_now = carry
        block_now = shifted(block_now, "dp", 1)
        source = (own_group - turn_index - 1) % group_count
        return (place_scores(scores_now, block_now, source), block_now)

    scores, query_block = lax.fori_loop(0, group_count - 1, turn, (scores, query_block))
    result = scores[None]
    return result


def solution(mesh):
    in_specs = (
        P("dp", None),
        P("dp"),
        P(None, ("dp", "vocab")),
        P(),
        P(("dp", "vocab"), None),
        P(),
        P(),
        P("dp", "vocab", None),
    )
    out_specs = P("dp", None, "vocab")
    return jax.shard_map(local, mesh=mesh, in_specs=in_specs, out_specs=out_specs, check_vma=False)
```

profile of v0, /device:TPU:16, one launch (start us, length us, event | category | flops | bytes accessed | tf_op | source)
XLA Modules:
  0.0 843.5 jit_solution(11562273559999551611)
XLA Ops:
  6.5 1.1 copy.27
  7.7 1.3 dynamic-slice
  9.6 0.9 dynamic-update-slice
  10.5 23.4 %all-reduce = s32[1024]{0:T(1024)S(1)} all-reduce(s32[1024]{0:T(1024)S(1)} %dynamic-update-slice), channel_id=1, replica_groups=mesh['dp'=16,'vocab'=32] {'dp'}, use_global_device_ids=true, to_apply=%add | all-reduce | flops 1024 | bytes 8192
  33.9 2.3 fusion
  36.2 131.6 %all-gather.2.cloned.1.call-done = bf16[1024,4608]{1,0:T(8,128)(2,1)} async-done(((bf16[64,4608]{1,0:T(8,128)(2,1)}), bf16[1024,4608]{1,0:T(8,128)(2,1)}) %all-gather.2.cloned.1.call-update) | async-done | bytes 9437200 | tf_op jit(solution)/shard_map/all_gather | solution.py:16
  167.7 5.2 fusion.16
  173.0 94.3 %pmax.7 = f32[1024]{0:T(1024)S(1)} all-reduce(f32[1024]{0:T(1024)S(1)} %get-tuple-element.154), channel_id=1, replica_groups=mesh['dp'=16,'vocab'=32] {'dp','vocab'}, use_global_device_ids=true, to_apply=%region_1.0 | all-reduce | flops 1024 | bytes 8192 | tf_op jit(solution)/shard_map/pmax | solution.py:27
  267.3 3.5 fusion.3
  270.8 221.6 %all-reduce.6.cloned.1.call-done = (f32[1024,64]{1,0:T(8,128)}, f32[1024,64]{1,0:T(8,128)}) async-done(((f32[1024,64]{1,0:T(8,128)}, f32[1024,64]{1,0:T(8,128)}), (f32[1024,64]{1,0:T(8,128)}, f32[1024,64]{1,0:T(8,128)})) %all-reduce.6.cloned.1.call-update) | async-done | bytes 524304 | tf_op jit(solution)/shard_map/psum | solution.py:29
  492.5 2.1 fusion.18
  494.8 55.4 %psum.44 = f32[1024]{0:T(1024)S(1)} all-reduce(f32[1024]{0:T(1024)S(1)} %fusion.2), channel_id=1, replica_groups=mesh['dp'=16,'vocab'=32] {'vocab'}, use_global_device_ids=true, to_apply=%region_5.0 | all-reduce | flops 1024 | bytes 8192 | tf_op jit(solution)/shard_map/psum | solution.py:29
  550.2 42.8 %psum.45 = f32[1024]{0:T(1024)S(1)} all-reduce(f32[1024]{0:T(1024)S(1)} %psum.44), channel_id=1, replica_groups=mesh['dp'=16,'vocab'=32] {'dp'}, use_global_device_ids=true, to_apply=%region_6.0 | all-reduce | flops 1024 | bytes 8192 | tf_op jit(solution)/shard_map/psum | solution.py:33
  593.1 74.0 %all-reduce.8.cloned.1.call-done = (f32[1024,64]{1,0:T(8,128)}, f32[1024,64]{1,0:T(8,128)}) async-done(((f32[1024,64]{1,0:T(8,128)}, f32[1024,64]{1,0:T(8,128)}), (f32[1024,64]{1,0:T(8,128)}, f32[1024,64]{1,0:T(8,128)})) %all-reduce.8.cloned.1.call-update) | async-done | bytes 524304 | tf_op jit(solution)/shard_map/psum | solution.py:33
  667.1 1.0 fusion.7
  668.1 1.0 fusion.19
  669.1 1.0 fusion.20
  670.7 165.6 %while.17 = (s32[]{:T(128)}, f32[16,8]{1,0:T(8,128)S(1)}, f32[8,4096]{1,0:T(8,128)S(1)}, f32[4096]{0:T(1024)S(1)}, s32[]{:T(128)}, /*index=5*/s32[]{:T(128)}, s32[]{:T(128)}, s32[]{:T(128)}, s32[]{:T(128)}, s32[]{:T(128)}) while((s32[]{:T(128)}, f32[16,8]{1,0:T(8,128)S(1)}, f32[8,4096]{1,0:T(8,128)S(1)}, f32[4096]{0:T(1024)S(1)}, ...), condition=%wide.region_10.11_spmd, body=%wide.region_9.10_spmd.sunk | while | flops 393234 | bytes 934296 | solution.py:59
  670.8 4.3 collective-permute-start
  675.1 6.1 collective-permute-done
  681.7 2.2 collective-permute-start
  683.9 8.2 collective-permute-done
  692.6 1.9 collective-permute-start
  694.6 8.5 %collective-permute-done = f32[8,4096]{1,0:T(8,128)S(1)} collective-permute-done((f32[8,4096]{1,0:T(8,128)S(1)}, f32[8,4096]{1,0:T(8,128)S(1)}, u32[]{:S(2)}, u32[]{:S(2)}) %collective-permute-start) | collective-permute-done | bytes 131104 | tf_op jit(solution)/shard_map/while/body/eval_jaxpr/ppermute | solution.py:11
  703.5 1.9 collective-permute-start
  705.5 8.5 %collective-permute-done = f32[8,4096]{1,0:T(8,128)S(1)} collective-permute-done((f32[8,4096]{1,0:T(8,128)S(1)}, f32[8,4096]{1,0:T(8,128)S(1)}, u32[]{:S(2)}, u32[]{:S(2)}) %collective-permute-start) | collective-permute-done | bytes 131104 | tf_op jit(solution)/shard_map/while/body/eval_jaxpr/ppermute | solution.py:11
  714.5 1.9 collective-permute-start
  716.4 8.5 %collective-permute-done = f32[8,4096]{1,0:T(8,128)S(1)} collective-permute-done((f32[8,4096]{1,0:T(8,128)S(1)}, f32[8,4096]{1,0:T(8,128)S(1)}, u32[]{:S(2)}, u32[]{:S(2)}) %collective-permute-start) | collective-permute-done | bytes 131104 | tf_op jit(solution)/shard_map/while/body/eval_jaxpr/ppermute | solution.py:11
  725.4 1.9 collective-permute-start
  727.4 8.5 %collective-permute-done = f32[8,4096]{1,0:T(8,128)S(1)} collective-permute-done((f32[8,4096]{1,0:T(8,128)S(1)}, f32[8,4096]{1,0:T(8,128)S(1)}, u32[]{:S(2)}, u32[]{:S(2)}) %collective-permute-start) | collective-permute-done | bytes 131104 | tf_op jit(solution)/shard_map/while/body/eval_jaxpr/ppermute | solution.py:11
  736.3 1.9 collective-permute-start
  738.3 8.5 %collective-permute-done = f32[8,4096]{1,0:T(8,128)S(1)} collective-permute-done((f32[8,4096]{1,0:T(8,128)S(1)}, f32[8,4096]{1,0:T(8,128)S(1)}, u32[]{:S(2)}, u32[]{:S(2)}) %collective-permute-start) | collective-permute-done | bytes 131104 | tf_op jit(solution)/shard_map/while/body/eval_jaxpr/ppermute | solution.py:11
  747.3 1.9 collective-permute-start
  749.2 9.6 %collective-permute-done = f32[8,4096]{1,0:T(8,128)S(1)} collective-permute-done((f32[8,4096]{1,0:T(8,128)S(1)}, f32[8,4096]{1,0:T(8,128)S(1)}, u32[]{:S(2)}, u32[]{:S(2)}) %collective-permute-start) | collective-permute-done | bytes 131104 | tf_op jit(solution)/shard_map/while/body/eval_jaxpr/ppermute | solution.py:11
  759.3 1.9 collective-permute-start
  761.3 9.1 %collective-permute-done = f32[8,4096]{1,0:T(8,128)S(1)} collective-permute-done((f32[8,4096]{1,0:T(8,128)S(1)}, f32[8,4096]{1,0:T(8,128)S(1)}, u32[]{:S(2)}, u32[]{:S(2)}) %collective-permute-start) | collective-permute-done | bytes 131104 | tf_op jit(solution)/shard_map/while/body/eval_jaxpr/ppermute | solution.py:11
  770.8 1.9 collective-permute-start
  772.7 8.5 %collective-permute-done = f32[8,4096]{1,0:T(8,128)S(1)} collective-permute-done((f32[8,4096]{1,0:T(8,128)S(1)}, f32[8,4096]{1,0:T(8,128)S(1)}, u32[]{:S(2)}, u32[]{:S(2)}) %collective-permute-start) | collective-permute-done | bytes 131104 | tf_op jit(solution)/shard_map/while/body/eval_jaxpr/ppermute | solution.py:11
  781.7 1.9 collective-permute-start
  783.7 8.5 %collective-permute-done = f32[8,4096]{1,0:T(8,128)S(1)} collective-permute-done((f32[8,4096]{1,0:T(8,128)S(1)}, f32[8,4096]{1,0:T(8,128)S(1)}, u32[]{:S(2)}, u32[]{:S(2)}) %collective-permute-start) | collective-permute-done | bytes 131104 | tf_op jit(solution)/shard_map/while/body/eval_jaxpr/ppermute | solution.py:11
  792.6 1.9 collective-permute-start
  794.6 8.5 %collective-permute-done = f32[8,4096]{1,0:T(8,128)S(1)} collective-permute-done((f32[8,4096]{1,0:T(8,128)S(1)}, f32[8,4096]{1,0:T(8,128)S(1)}, u32[]{:S(2)}, u32[]{:S(2)}) %collective-permute-start) | collective-permute-done | bytes 131104 | tf_op jit(solution)/shard_map/while/body/eval_jaxpr/ppermute | solution.py:11
  803.6 1.9 collective-permute-start
  805.5 8.5 %collective-permute-done = f32[8,4096]{1,0:T(8,128)S(1)} collective-permute-done((f32[8,4096]{1,0:T(8,128)S(1)}, f32[8,4096]{1,0:T(8,128)S(1)}, u32[]{:S(2)}, u32[]{:S(2)}) %collective-permute-start) | collective-permute-done | bytes 131104 | tf_op jit(solution)/shard_map/while/body/eval_jaxpr/ppermute | solution.py:11
  814.5 1.9 collective-permute-start
  816.4 8.5 %collective-permute-done = f32[8,4096]{1,0:T(8,128)S(1)} collective-permute-done((f32[8,4096]{1,0:T(8,128)S(1)}, f32[8,4096]{1,0:T(8,128)S(1)}, u32[]{:S(2)}, u32[]{:S(2)}) %collective-permute-start) | collective-permute-done | bytes 131104 | tf_op jit(solution)/shard_map/while/body/eval_jaxpr/ppermute | solution.py:11
  825.4 1.9 collective-permute-start
  827.4 8.5 %collective-permute-done = f32[8,4096]{1,0:T(8,128)S(1)} collective-permute-done((f32[8,4096]{1,0:T(8,128)S(1)}, f32[8,4096]{1,0:T(8,128)S(1)}, u32[]{:S(2)}, u32[]{:S(2)}) %collective-permute-start) | collective-permute-done | bytes 131104 | tf_op jit(solution)/shard_map/while/body/eval_jaxpr/ppermute | solution.py:11
  (63 shorter events, 8.0 us)
Async XLA Ops:
  6.5 161.2 %copy-start = (bf16[4608,256]{1,0:T(8,128)(2,1)S(1)}, bf16[4608,256]{1,0:T(8,128)(2,1)}, u32[]{:S(2)}) copy-start(bf16[4608,256]{1,0:T(8,128)(2,1)} %param.12) | copy-start | bytes 7077892
  6.5 161.2 %all-gather.2.cloned.1.call-start = ((), (), s32[]{:S(2)}) async-start(), calls=%async_computation | async-start | bytes 10027008 | tf_op jit(solution)/shard_map/all_gather | solution.py:16
  7.6 484.8 %all-reduce.6.cloned.1.call-start = ((), (), s32[]{:S(2)}) async-start(), calls=%async_computation.1 | async-start | bytes 2097152 | tf_op jit(solution)/shard_map/psum | solution.py:29
  270.8 396.3 %all-reduce.8.cloned.1.call-start = ((), (), s32[]{:S(2)}) async-start(), calls=%async_computation.2 | async-start | bytes 2097152 | tf_op jit(solution)/shard_map/psum | solution.py:33
  670.8 10.5 %collective-permute-start = (f32[8,4096]{1,0:T(8,128)S(1)}, f32[8,4096]{1,0:T(8,128)S(1)}, u32[]{:S(2)}, u32[]{:S(2)}) collective-permute-start(f32[8,4096]{1,0:T(8,128)S(1)} %get-tuple-element.199), channel_id=1, source_target_pairs={{0,32},{32,64},{64,96},{96,128},{128,160},{160,192},{192,224},{224... | collective-permute-start | bytes 393224 | tf_op jit(solution)/shard_map/while/body/eval_jaxpr/ppermute | solution.py:11
  681.7 10.5 %collective-permute-start = (f32[8,4096]{1,0:T(8,128)S(1)}, f32[8,4096]{1,0:T(8,128)S(1)}, u32[]{:S(2)}, u32[]{:S(2)}) collective-permute-start(f32[8,4096]{1,0:T(8,128)S(1)} %get-tuple-element.199), channel_id=1, source_target_pairs={{0,32},{32,64},{64,96},{96,128},{128,160},{160,192},{192,224},{224... | collective-permute-start | bytes 393224 | tf_op jit(solution)/shard_map/while/body/eval_jaxpr/ppermute | solution.py:11
  692.6 10.5 %collective-permute-start = (f32[8,4096]{1,0:T(8,128)S(1)}, f32[8,4096]{1,0:T(8,128)S(1)}, u32[]{:S(2)}, u32[]{:S(2)}) collective-permute-start(f32[8,4096]{1,0:T(8,128)S(1)} %get-tuple-element.199), channel_id=1, source_target_pairs={{0,32},{32,64},{64,96},{96,128},{128,160},{160,192},{192,224},{224... | collective-permute-start | bytes 393224 | tf_op jit(solution)/shard_map/while/body/eval_jaxpr/ppermute | solution.py:11
  703.5 10.5 %collective-permute-start = (f32[8,4096]{1,0:T(8,128)S(1)}, f32[8,4096]{1,0:T(8,128)S(1)}, u32[]{:S(2)}, u32[]{:S(2)}) collective-permute-start(f32[8,4096]{1,0:T(8,128)S(1)} %get-tuple-element.199), channel_id=1, source_target_pairs={{0,32},{32,64},{64,96},{96,128},{128,160},{160,192},{192,224},{224... | collective-permute-start | bytes 393224 | tf_op jit(solution)/shard_map/while/body/eval_jaxpr/ppermute | solution.py:11
  714.5 10.5 %collective-permute-start = (f32[8,4096]{1,0:T(8,128)S(1)}, f32[8,4096]{1,0:T(8,128)S(1)}, u32[]{:S(2)}, u32[]{:S(2)}) collective-permute-start(f32[8,4096]{1,0:T(8,128)S(1)} %get-tuple-element.199), channel_id=1, source_target_pairs={{0,32},{32,64},{64,96},{96,128},{128,160},{160,192},{192,224},{224... | collective-permute-start | bytes 393224 | tf_op jit(solution)/shard_map/while/body/eval_jaxpr/ppermute | solution.py:11
  725.4 10.5 %collective-permute-start = (f32[8,4096]{1,0:T(8,128)S(1)}, f32[8,4096]{1,0:T(8,128)S(1)}, u32[]{:S(2)}, u32[]{:S(2)}) collective-permute-start(f32[8,4096]{1,0:T(8,128)S(1)} %get-tuple-element.199), channel_id=1, source_target_pairs={{0,32},{32,64},{64,96},{96,128},{128,160},{160,192},{192,224},{224... | collective-permute-start | bytes 393224 | tf_op jit(solution)/shard_map/while/body/eval_jaxpr/ppermute | solution.py:11
  736.3 10.5 %collective-permute-start = (f32[8,4096]{1,0:T(8,128)S(1)}, f32[8,4096]{1,0:T(8,128)S(1)}, u32[]{:S(2)}, u32[]{:S(2)}) collective-permute-start(f32[8,4096]{1,0:T(8,128)S(1)} %get-tuple-element.199), channel_id=1, source_target_pairs={{0,32},{32,64},{64,96},{96,128},{128,160},{160,192},{192,224},{224... | collective-permute-start | bytes 393224 | tf_op jit(solution)/shard_map/while/body/eval_jaxpr/ppermute | solution.py:11
  747.3 11.6 %collective-permute-start = (f32[8,4096]{1,0:T(8,128)S(1)}, f32[8,4096]{1,0:T(8,128)S(1)}, u32[]{:S(2)}, u32[]{:S(2)}) collective-permute-start(f32[8,4096]{1,0:T(8,128)S(1)} %get-tuple-element.199), channel_id=1, source_target_pairs={{0,32},{32,64},{64,96},{96,128},{128,160},{160,192},{192,224},{224... | collective-permute-start | bytes 393224 | tf_op jit(solution)/shard_map/while/body/eval_jaxpr/ppermute | solution.py:11
  759.3 11.0 %collective-permute-start = (f32[8,4096]{1,0:T(8,128)S(1)}, f32[8,4096]{1,0:T(8,128)S(1)}, u32[]{:S(2)}, u32[]{:S(2)}) collective-permute-start(f32[8,4096]{1,0:T(8,128)S(1)} %get-tuple-element.199), channel_id=1, source_target_pairs={{0,32},{32,64},{64,96},{96,128},{128,160},{160,192},{192,224},{224... | collective-permute-start | bytes 393224 | tf_op jit(solution)/shard_map/while/body/eval_jaxpr/ppermute | solution.py:11
  770.8 10.5 %collective-permute-start = (f32[8,4096]{1,0:T(8,128)S(1)}, f32[8,4096]{1,0:T(8,128)S(1)}, u32[]{:S(2)}, u32[]{:S(2)}) collective-permute-start(f32[8,4096]{1,0:T(8,128)S(1)} %get-tuple-element.199), channel_id=1, source_target_pairs={{0,32},{32,64},{64,96},{96,128},{128,160},{160,192},{192,224},{224... | collective-permute-start | bytes 393224 | tf_op jit(solution)/shard_map/while/body/eval_jaxpr/ppermute | solution.py:11
  781.7 10.5 %collective-permute-start = (f32[8,4096]{1,0:T(8,128)S(1)}, f32[8,4096]{1,0:T(8,128)S(1)}, u32[]{:S(2)}, u32[]{:S(2)}) collective-permute-start(f32[8,4096]{1,0:T(8,128)S(1)} %get-tuple-element.199), channel_id=1, source_target_pairs={{0,32},{32,64},{64,96},{96,128},{128,160},{160,192},{192,224},{224... | collective-permute-start | bytes 393224 | tf_op jit(solution)/shard_map/while/body/eval_jaxpr/ppermute | solution.py:11
  792.6 10.5 %collective-permute-start = (f32[8,4096]{1,0:T(8,128)S(1)}, f32[8,4096]{1,0:T(8,128)S(1)}, u32[]{:S(2)}, u32[]{:S(2)}) collective-permute-start(f32[8,4096]{1,0:T(8,128)S(1)} %get-tuple-element.199), channel_id=1, source_target_pairs={{0,32},{32,64},{64,96},{96,128},{128,160},{160,192},{192,224},{224... | collective-permute-start | bytes 393224 | tf_op jit(solution)/shard_map/while/body/eval_jaxpr/ppermute | solution.py:11
  803.6 10.5 %collective-permute-start = (f32[8,4096]{1,0:T(8,128)S(1)}, f32[8,4096]{1,0:T(8,128)S(1)}, u32[]{:S(2)}, u32[]{:S(2)}) collective-permute-start(f32[8,4096]{1,0:T(8,128)S(1)} %get-tuple-element.199), channel_id=1, source_target_pairs={{0,32},{32,64},{64,96},{96,128},{128,160},{160,192},{192,224},{224... | collective-permute-start | bytes 393224 | tf_op jit(solution)/shard_map/while/body/eval_jaxpr/ppermute | solution.py:11
  814.5 10.5 %collective-permute-start = (f32[8,4096]{1,0:T(8,128)S(1)}, f32[8,4096]{1,0:T(8,128)S(1)}, u32[]{:S(2)}, u32[]{:S(2)}) collective-permute-start(f32[8,4096]{1,0:T(8,128)S(1)} %get-tuple-element.199), channel_id=1, source_target_pairs={{0,32},{32,64},{64,96},{96,128},{128,160},{160,192},{192,224},{224... | collective-permute-start | bytes 393224 | tf_op jit(solution)/shard_map/while/body/eval_jaxpr/ppermute | solution.py:11
  825.4 10.5 %collective-permute-start = (f32[8,4096]{1,0:T(8,128)S(1)}, f32[8,4096]{1,0:T(8,128)S(1)}, u32[]{:S(2)}, u32[]{:S(2)}) collective-permute-start(f32[8,4096]{1,0:T(8,128)S(1)} %get-tuple-element.199), channel_id=1, source_target_pairs={{0,32},{32,64},{64,96},{96,128},{128,160},{160,192},{192,224},{224... | collective-permute-start | bytes 393224 | tf_op jit(solution)/shard_map/while/body/eval_jaxpr/ppermute | solution.py:11
Sparse Core Ops, SparseCore 0:
  10.5 157.1 all-gather.1
  270.9 221.5 all-reduce.5
  495.7 171.3 all-reduce.7
where the time goes:
time: 845 us; the launch traced here: 844 us
  waiting for transfers between devices  554 us (66%)
  blocking collectives  216 us (26%)
  starting transfers between devices  31.6 us (4%)
  matrix products  21.9 us (3%)
  between operations  13.8 us (2%)
    psum x1, waiting for transfers between devices, local(): lax.psum((jnp.sum(exponent, axis=1), jnp.dot(exponent, out_proj, precisio...  222 us
    all_gather x1, waiting for transfers between devices, local(): lax.all_gather(hidden, 'dp', axis=0, tiled=True)  132 us
    ppermute x15, waiting for transfers between devices, shifted(): lax.ppermute(value, axis, [(i, (i + by) % devices) for i in range(devices)])  127 us
    pmax x1, blocking collectives, local(): largest = lax.pmax(jnp.max(logits, axis=1), ('dp', 'vocab'))  94.3 us
    psum x1, waiting for transfers between devices, local(): lax.psum((partial_sums[0], partial_sums[1], partial_sums[2]), 'dp')  74 us
    psum x1, blocking collectives, local(): lax.psum((jnp.sum(exponent, axis=1), jnp.dot(exponent, out_proj, precisio...  55.4 us
    psum x1, blocking collectives, local(): lax.psum((partial_sums[0], partial_sums[1], partial_sums[2]), 'dp')  42.8 us
    ppermute x15, starting transfers between devices, shifted(): lax.ppermute(value, axis, [(i, (i + by) % devices) for i in range(devices)])  31.5 us
  transfers between devices with their start and end apart: 18, of which 18 were waited for; matrix products, arithmetic and copies ran while one was open for 1% of the time, Pallas kernels for 0%

commit v1 on v0

v1 whole, which is shorter than its diff:
```python
import jax
import jax.numpy as jnp
from jax import lax
from jax.sharding import Mesh, PartitionSpec as P

PRECISE = lax.Precision.HIGHEST
EVERY = ("z", "xh", "xl", "yh", "yl", "core")
DP = ("z", "xh")
VOC = ("xl", "yh", "yl", "core")
SWAP = [(0, 1), (1, 0)]


def exchange(blocks, axes):
    return lax.all_to_all(blocks, axes, split_axis=0, concat_axis=0, tiled=True)


def spread_out(block, axes, count):
    return exchange(jnp.broadcast_to(block[None], (count,) + block.shape), axes)


def both_ways(value, axes, count):
    pairs = [(2 * i, 2 * ((i + 1) % count)) for i in range(count)]
    pairs += [(2 * i + 1, 2 * ((i - 1) % count) + 1) for i in range(count)]
    return lax.ppermute(value, axes + ("core",), pairs)


def local(hidden, labels, unembed, in_proj, out_proj, left_inv, right_inv, queries):
    core, xl, xh = lax.axis_index("core"), lax.axis_index("xl"), lax.axis_index("xh")
    y = lax.axis_index("yh") * 2 + lax.axis_index("yl")
    rows = 16 * (2 * lax.axis_index("yl") + core)
    z = lax.axis_index("z")

    chosen = lax.dynamic_slice(hidden, (rows, 2304 * xl), (16, 2304))
    picked = lax.dynamic_slice(labels, (rows,), (16,))
    digits = jnp.stack([picked // 65536, (picked // 256) % 256, picked % 256], axis=1)
    digits = jnp.pad(digits, ((0, 0), (0, 125))).astype(jnp.bfloat16)
    own0 = spread_out(jnp.concatenate([chosen[:, :1152], digits], axis=1), DP, 16).reshape(256, 1280)
    own1 = spread_out(chosen[:, 1152:], DP, 16).reshape(256, 1152)
    digits, own0 = own0[:, 1152:].astype(jnp.int32), own0[:, :1152]
    every_label = digits[:, 0:1] * 65536 + digits[:, 1:2] * 256 + digits[:, 2:3]
    rest0 = both_ways(own0, ("xh", "xl"), 4)
    rest1 = both_ways(own1, ("xh", "xl"), 4)

    query_pair = jnp.stack([queries[0], lax.ppermute(queries[0], "xh", SWAP)])
    query_pair, _ = lax.optimization_barrier((query_pair, own0))
    every_query = lax.all_gather(query_pair, "z", axis=0)

    weights = [unembed, both_ways(unembed, ("yh", "yl"), 8)]
    weights += [lax.ppermute(block, "core", SWAP) for block in weights]
    tables = jnp.concatenate([out_proj, both_ways(out_proj, ("yh", "yl"), 8)], axis=0)
    table = jnp.concatenate([tables, lax.ppermute(tables, "core", SWAP)], axis=0)

    def block_start(at_y, at_core):
        return (((z * 2 + xh) * 2 + xl) * 16 + at_y * 2 + at_core) * 256

    below, above = (y + 7) % 8, (y + 1) % 8
    starts = [
        block_start(y, core),
        block_start(jnp.where(core == 0, below, above), core),
        block_start(y, 1 - core),
        block_start(jnp.where(core == 0, above, below), 1 - core),
    ]
    ids = lax.iota(jnp.int32, 256)
    column_ids = jnp.concatenate([start + ids for start in starts])
    mask = (every_label == column_ids[None, :]).astype(jnp.float32)
    label_rows = jnp.dot(mask, table, precision=PRECISE)
    mapped = jnp.dot(hidden, in_proj, preferred_element_type=jnp.float32)

    def product(values, weight, start):
        part = lax.dynamic_slice(weight, (start, 0), (1152, 256))
        return jnp.dot(values, part, preferred_element_type=jnp.float32)

    here, there = 2304 * xl, 2304 * (1 - xl)
    logits = [
        product(own0, weight, here)
        + product(own1, weight, here + 1152)
        + product(rest0, weight, there)
        + product(rest1, weight, there + 1152)
        for weight in weights
    ]
    logits = jnp.concatenate(logits, axis=1)
    largest = jnp.max(logits, axis=1, keepdims=True)
    exponent = jnp.exp(logits - largest)
    totals = jnp.sum(exponent, axis=1, keepdims=True)
    sums = jnp.dot(exponent, table, precision=PRECISE)

    ends = jnp.pad(jnp.concatenate([largest, totals], axis=1), ((0, 0), (0, 126)))
    packed = jnp.concatenate([sums, label_rows, ends], axis=1)

    def merge(parts, axis):
        sums, label_rows = parts[..., :64], parts[..., 64:128]
        largest, totals = parts[..., 128:129], parts[..., 129:130]
        top = jnp.max(largest, axis=axis, keepdims=True)
        scaled = jnp.exp(largest - top)
        sums = jnp.sum(sums * scaled, axis=axis)
        return sums, jnp.sum(label_rows, axis=axis), jnp.squeeze(top, axis), jnp.sum(totals * scaled, axis=axis)

    merged = merge(exchange(packed.reshape(32, 8, 256), ("z", "xh", "xl")), 0)
    packed = jnp.pad(jnp.concatenate(merged, axis=-1), ((0, 0), (0, 126)))
    parts = spread_out(packed, VOC, 32).reshape(2, 4, 2, 2, 8, 256)
    sums, label_rows, _, totals = merge(parts, 1)
    projected = sums / totals - label_rows
    projected = jnp.transpose(projected, (1, 2, 0, 3, 4)).reshape(64, 64)

    feature = jnp.dot(mapped.T, projected, precision=PRECISE)
    precond = jnp.dot(jnp.dot(left_inv, feature, precision=PRECISE), right_inv, precision=PRECISE)
    scores = jnp.sum(every_query * precond.reshape(1, 1, 1, 4096), axis=3)
    scores = jnp.where(xh == 0, scores, scores[:, ::-1])
    return scores.reshape(1, 16, 8)


def solution(mesh):
    fine = Mesh(mesh.devices.reshape(8, 2, 2, 4, 2, 2), EVERY)
    in_specs = (
        P(DP, None),
        P(DP),
        P(None, EVERY),
        P(),
        P(EVERY, None),
        P(),
        P(),
        P(DP, VOC, None),
    )
    out_specs = P(DP, None, VOC)
    return jax.shard_map(local, mesh=fine, in_specs=in_specs, out_specs=out_specs, check_vma=False)
```

time: 845 us -> 153 us (0.18)
  the two profiles are of different devices: /device:TPU:16 before, /device:TPU:1 now
where the time goes in v1:
time: 153 us; the launch traced here: 152 us
  starting transfers between devices  58.8 us (38%)
  waiting for transfers between devices  24.4 us (16%)
  blocking collectives  22.9 us (15%)
  matrix products  18.5 us (12%)
  between operations  13.9 us (9%)
  local copies, waits for them, and re-layouts  7.81 us (5%)
  other arithmetic  5.6 us (4%)
    all_to_all x3, starting transfers between devices, exchange(): return lax.all_to_all(blocks, axes, split_axis=0, concat_axis=0, tiled=True)  27.8 us
    all_to_all x1, blocking collectives, exchange(): return lax.all_to_all(blocks, axes, split_axis=0, concat_axis=0, tiled=True)  22.9 us
    all_to_all x3, waiting for transfers between devices, exchange(): return lax.all_to_all(blocks, axes, split_axis=0, concat_axis=0, tiled=True)  16.1 us
    dot_general x16, matrix products, product(): return jnp.dot(values, part, preferred_element_type=jnp.float32)  16 us
    ppermute x4, starting transfers between devices, both_ways(): return lax.ppermute(value, axes + ('core',), pairs)  14.8 us
    ppermute x4, waiting for transfers between devices, both_ways(): return lax.ppermute(value, axes + ('core',), pairs)  8.09 us
    ppermute x2, starting transfers between devices, local(): weights += [lax.ppermute(block, 'core', SWAP) for block in weights]  7.19 us
    ppermute x1, starting transfers between devices, local(): query_pair = jnp.stack([queries[0], lax.ppermute(queries[0], 'xh', SWAP)])  4.94 us
  transfers between devices with their start and end apart: 12, of which 6 were waited for; matrix products, arithmetic and copies ran while one was open for 18% of the time, Pallas kernels for 0%

profile of v1, /device:TPU:1, one launch (start us, length us, event | category | flops | bytes accessed | tf_op | source)
XLA Modules:
  0.0 151.9 jit_solution(1843808117662247916)
XLA Ops:
  6.5 0.9 fusion.75
  7.4 0.9 broadcast_in_dim.9
  8.3 13.4 %all-to-all-start.1 = ((bf16[16,16,1152]{2,1,0:T(8,128)(2,1)}), bf16[16,16,1152]{2,1,0:T(8,128)(2,1)S(1)}, u32[]{:S(2)}, u32[]{:S(2)}) async-start(bf16[16,16,1152]{2,1,0:T(8,128)(2,1)} %broadcast_in_dim.9), calls=%async_computation.1 | async-start | bytes 1179648 | tf_op jit(solution)/shard_map/all_to_all | solution.py:14
  21.7 5.1 %collective-permute-start.3 = (bf16[4608,256]{1,0:T(8,128)(2,1)}, bf16[4608,256]{1,0:T(8,128)(2,1)}, u32[]{:S(2)}, u32[]{:S(2)}) collective-permute-start(bf16[4608,256]{1,0:T(8,128)(2,1)} %param.10), channel_id=1, source_target_pairs={{0,2},{2,4},{4,6},{6,8},{8,10},{10,12},{12,14},{14,0},{1,15},{3,1}... | collective-permute-start | bytes 7077896 | tf_op jit(solution)/shard_map/ppermute | solution.py:24
  26.8 1.9 %collective-permute-start.4 = (bf16[4608,256]{1,0:T(8,128)(2,1)}, bf16[4608,256]{1,0:T(8,128)(2,1)}, u32[]{:S(2)}, u32[]{:S(2)}) collective-permute-start(bf16[4608,256]{1,0:T(8,128)(2,1)} %param.10), channel_id=1, source_target_pairs={{0,1},{1,0},{2,3},{3,2},{4,5},{5,4},{6,7},{7,6},{8,9},{9,8},{10,11... | collective-permute-start | bytes 7077896 | tf_op jit(solution)/shard_map/ppermute | solution.py:49
  28.8 3.0 %collective-permute-start.6 = (f32[256,64]{0,1:T(8,128)}, f32[256,64]{0,1:T(8,128)S(1)}, u32[]{:S(2)}, u32[]{:S(2)}) collective-permute-start(f32[256,64]{0,1:T(8,128)} %param.12), channel_id=1, source_target_pairs={{0,2},{2,4},{4,6},{6,8},{8,10},{10,12},{12,14},{14,0},{1,15},{3,1}... | collective-permute-start | bytes 196616 | tf_op jit(solution)/shard_map/ppermute | solution.py:24
  31.8 4.9 %collective-permute-start = (f32[8,4096]{1,0:T(8,128)}, f32[8,4096]{1,0:T(8,128)S(1)}, u32[]{:S(2)}, u32[]{:S(2)}) collective-permute-start(f32[8,4096]{1,0:T(8,128)} %bitcast.69), channel_id=1, source_target_pairs={{0,32},{32,0},{1,33},{33,1},{2,34},{34,2},{3,35},{35,3},{4,36},{36... | collective-permute-start | bytes 393224 | tf_op jit(solution)/shard_map/ppermute | solution.py:44
  36.7 0.8 fusion.66
  37.6 2.5 %all-to-all-done.1 = bf16[16,16,1152]{2,1,0:T(8,128)(2,1)S(1)} async-done(((bf16[16,16,1152]{2,1,0:T(8,128)(2,1)}), bf16[16,16,1152]{2,1,0:T(8,128)(2,1)S(1)}, u32[]{:S(2)}, u32[]{:S(2)}) %all-to-all-start.1) | async-done | bytes 589856 | tf_op jit(solution)/shard_map/all_to_all | solution.py:14
  40.1 0.9 broadcast_in_dim.8
  41.0 4.9 %all-to-all-start = ((bf16[16,16,1280]{2,1,0:T(8,128)(2,1)}), bf16[16,16,1280]{2,1,0:T(8,128)(2,1)S(1)}, u32[]{:S(2)}, u32[]{:S(2)}) async-start(bf16[16,16,1280]{2,1,0:T(8,128)(2,1)} %broadcast_in_dim.8), calls=%async_computation | async-start | bytes 1310720 | tf_op jit(solution)/shard_map/all_to_all | solution.py:14
  46.1 7.6 %collective-permute-done.6 = f32[256,64]{0,1:T(8,128)S(1)} collective-permute-done((f32[256,64]{0,1:T(8,128)}, f32[256,64]{0,1:T(8,128)S(1)}, u32[]{:S(2)}, u32[]{:S(2)}) %collective-permute-start.6) | collective-permute-done | bytes 65568 | tf_op jit(solution)/shard_map/ppermute | solution.py:24
  53.6 4.1 %collective-permute-start.7 = (f32[512,64]{0,1:T(8,128)S(1)}, f32[512,64]{0,1:T(8,128)S(1)}, u32[]{:S(2)}, u32[]{:S(2)}) collective-permute-start(f32[512,64]{0,1:T(8,128)S(1)} %pad_maximum_fusion.2), channel_id=1, source_target_pairs={{0,1},{1,0},{2,3},{3,2},{4,5},{5,4},{6,7},{7,6},{8,9},{9,8},{10,11... | collective-permute-start | bytes 393224 | tf_op jit(solution)/shard_map/ppermute | solution.py:51
  57.8 0.7 pad_maximum_fusion
  58.7 4.8 %collective-permute-start.2 = (bf16[256,1152]{1,0:T(8,128)(2,1)S(1)}, bf16[256,1152]{1,0:T(8,128)(2,1)S(1)}, u32[]{:S(2)}, u32[]{:S(2)}) collective-permute-start(bf16[256,1152]{1,0:T(8,128)(2,1)S(1)} %bitcast.59), channel_id=1, source_target_pairs={{0,16},{16,32},{32,48},{48,0},{1,49},{17,1},{33,17},{49,33},{2,18}... | collective-permute-start | bytes 1769480 | tf_op jit(solution)/shard_map/ppermute | solution.py:24
  63.5 2.0 %all-to-all-done = bf16[16,16,1280]{2,1,0:T(8,128)(2,1)S(1)} async-done(((bf16[16,16,1280]{2,1,0:T(8,128)(2,1)}), bf16[16,16,1280]{2,1,0:T(8,128)(2,1)S(1)}, u32[]{:S(2)}, u32[]{:S(2)}) %all-to-all-start) | async-done | bytes 655392 | tf_op jit(solution)/shard_map/all_to_all | solution.py:14
  65.5 0.9 slice.60
  66.3 1.9 %collective-permute-start.1 = (bf16[256,1152]{1,0:T(8,128)(2,1)}, bf16[256,1152]{1,0:T(8,128)(2,1)S(1)}, u32[]{:S(2)}, u32[]{:S(2)}) collective-permute-start(bf16[256,1152]{1,0:T(8,128)(2,1)} %slice.60), channel_id=1, source_target_pairs={{0,16},{16,32},{32,48},{48,0},{1,49},{17,1},{33,17},{49,33},{2,18}... | collective-permute-start | bytes 1769480 | tf_op jit(solution)/shard_map/ppermute | solution.py:24
  68.3 1.6 %fusion.35 = f32[256,256]{0,1:T(8,128)S(1)} fusion(bf16[4608,256]{1,0:T(8,128)(2,1)} %param.10, s32[]{:T(128)S(6)} %select_n.74, bf16[256,1280]{1,0:T(8,128)(2,1)S(1)} %bitcast.55), kind=kOutput, calls=%fused_computation.43 | convolution fusion | flops 150994944 | bytes 1441796 | tf_op jit(solution)/shard_map/dot_general | solution.py:71
  70.1 0.7 fusion.8
  70.8 0.4 convolution_add_fusion.4
  71.2 5.3 %collective-permute-start.5 = (bf16[4608,256]{1,0:T(8,128)(2,1)}, bf16[4608,256]{1,0:T(8,128)(2,1)S(1)}, u32[]{:S(2)}, u32[]{:S(2)}) collective-permute-start(bf16[4608,256]{1,0:T(8,128)(2,1)} %collective-permute-done.3), channel_id=1, source_target_pairs={{0,1},{1,0},{2,3},{3,2},{4,5},{5,4},{6,7},{7,6},{8,9},{9,8},{10,11... | collective-permute-start | bytes 7077896 | tf_op jit(solution)/shard_map/ppermute | solution.py:49
  76.5 0.4 fusion.31
  76.9 0.5 collective-permute-done.1
  77.5 0.4 fusion.80
  77.9 1.4 fusion.26
  79.3 1.4 fusion.24
  80.8 1.4 fusion.28
  82.2 1.4 fusion.19
  83.7 1.4 fusion.17
  85.1 1.4 fusion.21
  86.6 1.5 fusion.81
  88.1 1.5 fusion.79
  89.6 0.4 fusion.12
  89.9 0.4 fusion.10
  90.3 0.4 fusion.14
  90.7 0.4 fusion.78
  91.2 0.8 fusion.40
  92.4 22.9 %all_to_all.20 = f32[32,8,256]{2,1,0:T(8,128)S(1)} all-to-all(f32[32,8,256]{2,1,0:T(8,128)S(1)} %bitcast.67), channel_id=1, replica_groups=mesh['z'=8,'xh'=2,'xl'=2,'yh'=4,'yl'=2,'core'=2] {'z','xh','xl'}, dimensions={0} | all-to-all | bytes 524288 | tf_op jit(solution)/shard_map/all_to_all | solution.py:14
  116.3 0.7 broadcast_in_dim.11
  117.1 9.5 %all-to-all-start.3 = ((f32[32,8,256]{2,1,0:T(8,128)}), f32[32,8,256]{2,1,0:T(8,128)S(1)}, u32[]{:S(2)}, u32[]{:S(2)}) async-start(f32[32,8,256]{2,1,0:T(8,128)} %broadcast_in_dim.11), calls=%async_computation.3 | async-start | bytes 524288 | tf_op jit(solution)/shard_map/all_to_all | solution.py:14
  126.6 0.3 fusion.82
  126.9 11.6 %all-to-all-done.3 = f32[32,8,256]{2,1,0:T(8,128)S(1)} async-done(((f32[32,8,256]{2,1,0:T(8,128)}), f32[32,8,256]{2,1,0:T(8,128)S(1)}, u32[]{:S(2)}, u32[]{:S(2)}) %all-to-all-start.3) | async-done | bytes 262176 | tf_op jit(solution)/shard_map/all_to_all | solution.py:14
  138.8 0.3 copy.66
  139.2 1.1 copy.64
  140.6 0.7 multiply_reduce_fusion.1
  142.5 1.8 %multiply_reduce_fusion = f32[8,2,8]{2,1,0:T(2,128)S(1)} fusion(f32[8,2,8,4096]{3,2,1,0:T(8,128)} %bitcast.66, f32[4096]{0:T(1024)S(1)} %mul.131), kind=kLoop, calls=%fused_computation | loop fusion | flops 1048448 | bytes 2114048 | tf_op jit(solution)/shard_map/reduce_sum | solution.py:107
  144.4 0.7 copy.61
  (63 shorter events, 4.1 us)
Async XLA Ops:
  6.5 120.0 %copy-start = (bf16[4608,64]{0,1:T(8,128)(2,1)S(1)}, bf16[4608,64]{0,1:T(8,128)(2,1)}, u32[]{:S(2)}) copy-start(bf16[4608,64]{0,1:T(8,128)(2,1)} %param.11) | copy-start | bytes 1769476
  6.5 39.5 %copy-start.3 = (f32[256,64]{0,1:T(8,128)S(1)}, f32[256,64]{0,1:T(8,128)}, u32[]{:S(2)}) copy-start(f32[256,64]{0,1:T(8,128)} %param.12) | copy-start | bytes 196612
  6.5 51.2 %copy-start.4 = (f32[1,8,4096]{2,1,0:T(8,128)S(1)}, f32[1,8,4096]{2,1,0:T(8,128)}, u32[]{:S(2)}) copy-start(f32[1,8,4096]{2,1,0:T(8,128)} %param.15) | copy-start | bytes 393220
  8.3 31.8 %all-to-all-start.1 = ((bf16[16,16,1152]{2,1,0:T(8,128)(2,1)}), bf16[16,16,1152]{2,1,0:T(8,128)(2,1)S(1)}, u32[]{:S(2)}, u32[]{:S(2)}) async-start(bf16[16,16,1152]{2,1,0:T(8,128)(2,1)} %broadcast_in_dim.9), calls=%async_computation.1 | async-start | bytes 1179648 | tf_op jit(solution)/shard_map/all_to_all | solution.py:14
  21.7 49.5 %collective-permute-start.3 = (bf16[4608,256]{1,0:T(8,128)(2,1)}, bf16[4608,256]{1,0:T(8,128)(2,1)}, u32[]{:S(2)}, u32[]{:S(2)}) collective-permute-start(bf16[4608,256]{1,0:T(8,128)(2,1)} %param.10), channel_id=1, source_target_pairs={{0,2},{2,4},{4,6},{6,8},{8,10},{10,12},{12,14},{14,0},{1,15},{3,1}... | collective-permute-start | bytes 7077896 | tf_op jit(solution)/shard_map/ppermute | solution.py:24
  26.8 55.4 %collective-permute-start.4 = (bf16[4608,256]{1,0:T(8,128)(2,1)}, bf16[4608,256]{1,0:T(8,128)(2,1)}, u32[]{:S(2)}, u32[]{:S(2)}) collective-permute-start(bf16[4608,256]{1,0:T(8,128)(2,1)} %param.10), channel_id=1, source_target_pairs={{0,1},{1,0},{2,3},{3,2},{4,5},{5,4},{6,7},{7,6},{8,9},{9,8},{10,11... | collective-permute-start | bytes 7077896 | tf_op jit(solution)/shard_map/ppermute | solution.py:49
  28.8 24.9 %collective-permute-start.6 = (f32[256,64]{0,1:T(8,128)}, f32[256,64]{0,1:T(8,128)S(1)}, u32[]{:S(2)}, u32[]{:S(2)}) collective-permute-start(f32[256,64]{0,1:T(8,128)} %param.12), channel_id=1, source_target_pairs={{0,2},{2,4},{4,6},{6,8},{8,10},{10,12},{12,14},{14,0},{1,15},{3,1}... | collective-permute-start | bytes 196616 | tf_op jit(solution)/shard_map/ppermute | solution.py:24
  31.8 26.0 %collective-permute-start = (f32[8,4096]{1,0:T(8,128)}, f32[8,4096]{1,0:T(8,128)S(1)}, u32[]{:S(2)}, u32[]{:S(2)}) collective-permute-start(f32[8,4096]{1,0:T(8,128)} %bitcast.69), channel_id=1, source_target_pairs={{0,32},{32,0},{1,33},{33,1},{2,34},{34,2},{3,35},{35,3},{4,36},{36... | collective-permute-start | bytes 393224 | tf_op jit(solution)/shard_map/ppermute | solution.py:44
  41.0 24.4 %all-to-all-start = ((bf16[16,16,1280]{2,1,0:T(8,128)(2,1)}), bf16[16,16,1280]{2,1,0:T(8,128)(2,1)S(1)}, u32[]{:S(2)}, u32[]{:S(2)}) async-start(bf16[16,16,1280]{2,1,0:T(8,128)(2,1)} %broadcast_in_dim.8), calls=%async_computation | async-start | bytes 1310720 | tf_op jit(solution)/shard_map/all_to_all | solution.py:14
  45.9 96.6 %all-gather.3.cloned.1.call-start = ((), (), s32[]{:S(2)}) async-start(), calls=%async_computation.4 | async-start | bytes 2359296 | tf_op jit(solution)/shard_map/all_gather | solution.py:46
  53.6 5.1 %collective-permute-start.7 = (f32[512,64]{0,1:T(8,128)S(1)}, f32[512,64]{0,1:T(8,128)S(1)}, u32[]{:S(2)}, u32[]{:S(2)}) collective-permute-start(f32[512,64]{0,1:T(8,128)S(1)} %pad_maximum_fusion.2), channel_id=1, source_target_pairs={{0,1},{1,0},{2,3},{3,2},{4,5},{5,4},{6,7},{7,6},{8,9},{9,8},{10,11... | collective-permute-start | bytes 393224 | tf_op jit(solution)/shard_map/ppermute | solution.py:51
  58.7 17.8 %collective-permute-start.2 = (bf16[256,1152]{1,0:T(8,128)(2,1)S(1)}, bf16[256,1152]{1,0:T(8,128)(2,1)S(1)}, u32[]{:S(2)}, u32[]{:S(2)}) collective-permute-start(bf16[256,1152]{1,0:T(8,128)(2,1)S(1)} %bitcast.59), channel_id=1, source_target_pairs={{0,16},{16,32},{32,48},{48,0},{1,49},{17,1},{33,17},{49,33},{2,18}... | collective-permute-start | bytes 1769480 | tf_op jit(solution)/shard_map/ppermute | solution.py:24
  66.3 11.1 %collective-permute-start.1 = (bf16[256,1152]{1,0:T(8,128)(2,1)}, bf16[256,1152]{1,0:T(8,128)(2,1)S(1)}, u32[]{:S(2)}, u32[]{:S(2)}) collective-permute-start(bf16[256,1152]{1,0:T(8,128)(2,1)} %slice.60), channel_id=1, source_target_pairs={{0,16},{16,32},{32,48},{48,0},{1,49},{17,1},{33,17},{49,33},{2,18}... | collective-permute-start | bytes 1769480 | tf_op jit(solution)/shard_map/ppermute | solution.py:24
  68.3 2.6 %copy-start.1 = (bf16[4608,256]{1,0:T(8,128)(2,1)S(1)}, bf16[4608,256]{1,0:T(8,128)(2,1)}, u32[]{:S(2)}) copy-start(bf16[4608,256]{1,0:T(8,128)(2,1)} %param.10) | copy-start | bytes 7077892
  71.2 18.3 %collective-permute-start.5 = (bf16[4608,256]{1,0:T(8,128)(2,1)}, bf16[4608,256]{1,0:T(8,128)(2,1)S(1)}, u32[]{:S(2)}, u32[]{:S(2)}) collective-permute-start(bf16[4608,256]{1,0:T(8,128)(2,1)} %collective-permute-done.3), channel_id=1, source_target_pairs={{0,1},{1,0},{2,3},{3,2},{4,5},{5,4},{6,7},{7,6},{8,9},{9,8},{10,11... | collective-permute-start | bytes 7077896 | tf_op jit(solution)/shard_map/ppermute | solution.py:49
  92.0 34.6 %copy-start.2 = (bf16[64,4608]{1,0:T(8,128)(2,1)S(1)}, bf16[64,4608]{1,0:T(8,128)(2,1)}, u32[]{:S(2)}) copy-start(bf16[64,4608]{1,0:T(8,128)(2,1)} %param.8) | copy-start | bytes 1769476
  117.1 21.4 %all-to-all-start.3 = ((f32[32,8,256]{2,1,0:T(8,128)}), f32[32,8,256]{2,1,0:T(8,128)S(1)}, u32[]{:S(2)}, u32[]{:S(2)}) async-start(f32[32,8,256]{2,1,0:T(8,128)} %broadcast_in_dim.11), calls=%async_computation.3 | async-start | bytes 524288 | tf_op jit(solution)/shard_map/all_to_all | solution.py:14
  138.6 3.4 %copy-start.5 = (f32[64,64]{1,0:T(8,128)S(1)}, f32[64,64]{1,0:T(8,128)}, u32[]{:S(2)}) copy-start(f32[64,64]{1,0:T(8,128)} %param.13) | copy-start | bytes 49156
  138.8 3.4 %copy-start.6 = (f32[64,64]{1,0:T(8,128)S(1)}, f32[64,64]{1,0:T(8,128)}, u32[]{:S(2)}) copy-start(f32[64,64]{1,0:T(8,128)} %param.14) | copy-start | bytes 49156
Sparse Core Ops, SparseCore 0:
  68.4 45.1 all-gather.2

commit v2 on v1

v2 whole, which is shorter than its diff:
```python
import jax
import jax.numpy as jnp
from jax import lax
from jax.experimental import pallas as pl
from jax.experimental.pallas import tpu as pltpu
from jax.sharding import Mesh, PartitionSpec as P

PRECISE = lax.Precision.HIGHEST
EVERY = ("zh", "zl", "xh", "xl", "yh", "yl", "core")
DP = ("zh", "zl", "xh")
VOC = ("xl", "yh", "yl", "core")
SWAP = [(0, 1), (1, 0)]
STEPS = 3
DEPTH = 2304 // STEPS
ROWS = 128


def exchange(blocks, axes):
    return lax.all_to_all(blocks, axes, split_axis=0, concat_axis=0, tiled=True)


def spread_out(block, axes, count):
    return exchange(jnp.broadcast_to(block[None], (count,) + block.shape), axes)


def both_ways(value, axes, count):
    pairs = [(2 * i, 2 * ((i + 1) % count)) for i in range(count)]
    pairs += [(2 * i + 1, 2 * ((i - 1) % count) + 1) for i in range(count)]
    return lax.ppermute(value, axes + ("core",), pairs)


def add_products(near_ref, far_ref, weight_refs, acc_ref):
    for block, weight in enumerate(weight_refs):
        columns = pl.ds(256 * block, 256)
        for start, rows in ((0, near_ref), (ROWS, far_ref)):
            acc_ref[pl.ds(start, ROWS), columns] += jnp.dot(
                rows[...], weight[...], preferred_element_type=jnp.float32
            )


def first_kernel(where_ref, near_ref, far_ref, w0, w1, w2, w3, acc_ref):
    @pl.when(pl.program_id(0) == 0)
    def _():
        acc_ref[...] = jnp.zeros_like(acc_ref)

    add_products(near_ref, far_ref, (w0, w1, w2, w3), acc_ref)


def last_kernel(where_ref, near_ref, far_ref, w0, w1, w2, w3, begun_ref, table_ref, label_ref, out_ref, acc_ref):
    step = pl.program_id(0)

    @pl.when(step == 0)
    def _():
        acc_ref[...] = begun_ref[...]

    add_products(near_ref, far_ref, (w0, w1, w2, w3), acc_ref)

    @pl.when(step == STEPS - 1)
    def _():
        logits = acc_ref[...]
        largest = jnp.max(logits, axis=1, keepdims=True)
        exponent = jnp.exp(logits - largest)
        totals = jnp.sum(exponent, axis=1, keepdims=True)
        sums = jnp.dot(exponent, table_ref[...], precision=PRECISE, preferred_element_type=jnp.float32)
        left = jnp.concatenate([sums, label_ref[...]], axis=1)
        lane = lax.broadcasted_iota(jnp.int32, (2 * ROWS, 128), 1)
        right = jnp.where(lane == 0, largest, jnp.where(lane == 1, totals, 0.0))
        parity = where_ref[1]
        for start, place in ((0, parity), (ROWS, 1 - parity)):
            out_ref[:, pl.ds(place, 1), :, 0:128] = left[start : start + ROWS].reshape(4, 1, 32, 128)
            out_ref[:, pl.ds(place, 1), :, 128:256] = right[start : start + ROWS].reshape(4, 1, 32, 128)


def product_specs():
    rows = pl.BlockSpec((ROWS, DEPTH), lambda step, where: (0, step))
    weight = pl.BlockSpec((DEPTH, 256), lambda step, where: (where[0] * STEPS + step, 0))
    return [rows, rows] + [weight] * 4


def whole(shape):
    return pl.BlockSpec(shape, lambda step, where: (0,) * len(shape))


COST = dict(flops=2 * 256 * 2304 * 1024, bytes_accessed=7_000_000)


def first_products(where, near, far, weights):
    return pl.pallas_call(
        first_kernel,
        out_shape=jax.ShapeDtypeStruct((256, 1024), jnp.float32),
        grid_spec=pltpu.PrefetchScalarGridSpec(
            num_scalar_prefetch=1,
            grid=(STEPS,),
            in_specs=product_specs(),
            out_specs=whole((256, 1024)),
        ),
        compiler_params=pltpu.CompilerParams(vmem_limit_bytes=24 << 20),
        cost_estimate=pl.CostEstimate(transcendentals=0, **COST),
    )(where, near, far, *weights)


def last_products(where, near, far, weights, begun, table, label_rows):
    return pl.pallas_call(
        last_kernel,
        out_shape=jax.ShapeDtypeStruct((4, 2, 32, 256), jnp.float32),
        grid_spec=pltpu.PrefetchScalarGridSpec(
            num_scalar_prefetch=1,
            grid=(STEPS,),
            in_specs=product_specs() + [whole((256, 1024)), whole((1024, 64)), whole((256, 64))],
            out_specs=whole((4, 2, 32, 256)),
            scratch_shapes=[pltpu.VMEM((256, 1024), jnp.float32)],
        ),
        compiler_params=pltpu.CompilerParams(vmem_limit_bytes=24 << 20),
        cost_estimate=pl.CostEstimate(transcendentals=256 * 1024, **COST),
    )(where, near, far, *weights, begun, table, label_rows)


def local(hidden, labels, unembed, in_proj, out_proj, left_inv, right_inv, queries):
    core, xl, xh, zl = [lax.axis_index(name) for name in ("core", "xl", "xh", "zl")]
    y = lax.axis_index("yh") * 2 + lax.axis_index("yl")
    rows = 16 * (2 * lax.axis_index("yl") + core)
    z = lax.axis_index("zh") * 2 + zl

    chosen = lax.dynamic_slice(hidden, (rows, 2304 * xl), (16, 2304))
    picked = lax.dynamic_slice(labels, (rows,), (16,))
    digits = jnp.stack([picked // 65536, (picked // 256) % 256, picked % 256], axis=1)
    digits = jnp.pad(digits, ((0, 0), (0, 125))).astype(jnp.bfloat16)
    chosen = jnp.concatenate([chosen, digits], axis=1)
    near = spread_out(chosen, ("zh", "xh"), 8).reshape(ROWS, 2432)
    far = both_ways(near, ("zh", "zl"), 8)
    near_x = both_ways(near, ("xh", "xl"), 4)
    far_x = both_ways(far, ("xh", "xl"), 4)

    query_pair = jnp.stack([queries[0], lax.ppermute(queries[0], "xh", SWAP)])
    query_pair, _ = lax.optimization_barrier((query_pair, near))
    every_query = lax.all_gather(query_pair, ("zh", "zl"), axis=0)

    weights = [unembed, both_ways(unembed, ("yh", "yl"), 8)]
    weights += [lax.ppermute(block, "core", SWAP) for block in weights]
    tables = jnp.concatenate([out_proj, both_ways(out_proj, ("yh", "yl"), 8)], axis=0)
    table = jnp.concatenate([tables, lax.ppermute(tables, "core", SWAP)], axis=0)

    def block_start(at_y, at_core):
        return (((z * 2 + xh) * 2 + xl) * 16 + at_y * 2 + at_core) * 256

    below, above = (y + 7) % 8, (y + 1) % 8
    starts = [
        block_start(y, core),
        block_start(jnp.where(core == 0, below, above), core),
        block_start(y, 1 - core),
        block_start(jnp.where(core == 0, above, below), 1 - core),
    ]
    ids = lax.iota(jnp.int32, 256)
    column_ids = jnp.concatenate([start + ids for start in starts])
    digits = jnp.concatenate([near[:, 2304:], far[:, 2304:]], axis=0).astype(jnp.int32)
    every_label = digits[:, 0:1] * 65536 + digits[:, 1:2] * 256 + digits[:, 2:3]
    mask = (every_label == column_ids[None, :]).astype(jnp.float32)
    label_rows = jnp.dot(mask, table, precision=PRECISE)
    mapped = jnp.dot(hidden, in_proj, preferred_element_type=jnp.float32)

    begun = first_products(jnp.stack([xl, zl]), near, far, weights)
    packed = last_products(jnp.stack([1 - xl, zl]), near_x, far_x, weights, begun, table, label_rows)

    def merge(parts, axis):
        sums, label_rows = parts[..., :64], parts[..., 64:128]
        largest, totals = parts[..., 128:129], parts[..., 129:130]
        top = jnp.max(largest, axis=axis, keepdims=True)
        scaled = jnp.exp(largest - top)
        sums = jnp.sum(sums * scaled, axis=axis)
        return sums, jnp.sum(label_rows, axis=axis), jnp.squeeze(top, axis), jnp.sum(totals * scaled, axis=axis)

    merged = merge(exchange(packed.reshape(32, 8, 256), ("zh", "zl", "xh", "xl")), 0)
    packed = jnp.pad(jnp.concatenate(merged, axis=-1), ((0, 0), (0, 126)))
    parts = spread_out(packed, VOC, 32).reshape(2, 4, 2, 2, 8, 256)
    sums, label_rows, _, totals = merge(parts, 1)
    projected = sums / totals - label_rows
    projected = jnp.transpose(projected, (1, 2, 0, 3, 4)).reshape(64, 64)

    feature = jnp.dot(mapped.T, projected, precision=PRECISE)
    precond = jnp.dot(jnp.dot(left_inv, feature, precision=PRECISE), right_inv, precision=PRECISE)
    scores = jnp.sum(every_query * precond.reshape(1, 1, 1, 4096), axis=3)
    scores = jnp.where(xh == 0, scores, scores[:, ::-1])
    return scores.reshape(1, 16, 8)


def solution(mesh):
    fine = Mesh(mesh.devices.reshape(4, 2, 2, 2, 4, 2, 2), EVERY)
    in_specs = (
        P(DP, None),
        P(DP),
        P(None, EVERY),
        P(),
        P(EVERY, None),
        P(),
        P(),
        P(DP, VOC, None),
    )
    out_specs = P(DP, None, VOC)
    return jax.shard_map(local, mesh=fine, in_specs=in_specs, out_specs=out_specs, check_vma=False)
```

time: 153 us -> 147 us (0.961)
  matrix products: 18.5 us -> 2.72 us
  Pallas kernels: 0 us -> 10.7 us
  blocking collectives: 22.9 us -> 17.8 us
  starting transfers between devices: 58.8 us -> 60.8 us
  other arithmetic: 5.6 us -> 7.49 us
    dot_general x17 -> x0, matrix products: 16.8 us -> none  [the longest x16 16 us: product(): return jnp.dot(values, part, preferred_element_type=jnp.float32)]
    pallas_call x0 -> x2, Pallas kernels: none -> 10.7 us  [the longest x1 5.96 us: last_products(): pl.pallas_call(last_kernel, out_shape=jax.ShapeDtypeStruct((4, 2, 32, 256...]
    ppermute x4 -> x5, starting transfers between devices: 14.8 us -> 23.5 us  [both_ways(): return lax.ppermute(value, axes + ('core',), pairs)]
    all_to_all x3 -> x2, starting transfers between devices: 27.8 us -> 22.4 us  [exchange(): return lax.all_to_all(blocks, axes, split_axis=0, concat_axis=0, tiled=True)]
    all_to_all x1, blocking collectives: 22.9 us -> 17.8 us  [exchange(): return lax.all_to_all(blocks, axes, split_axis=0, concat_axis=0, tiled=True)]
    all_to_all x3 -> x2, waiting for transfers between devices: 16.1 us -> 11.6 us  [exchange(): return lax.all_to_all(blocks, axes, split_axis=0, concat_axis=0, tiled=True)]
    ppermute x4 -> x5, waiting for transfers between devices: 8.09 us -> 12.1 us  [both_ways(): return lax.ppermute(value, axes + ('core',), pairs)]
    ppermute x2, starting transfers between devices: 7.19 us -> 11.1 us  [local(): weights += [lax.ppermute(block, 'core', SWAP) for block in weights]]
  transfers between devices with their start and end apart: 12 -> 12, of which waited for: 6 -> 4; matrix products, arithmetic and copies ran while one was open for 18% -> 11% of each run, Pallas kernels for 0% -> 7%
where the time goes in v2:
time: 147 us; the launch traced here: 146 us
  starting transfers between devices  60.8 us (41%)
  waiting for transfers between devices  23.7 us (16%)
  blocking collectives  17.8 us (12%)
  between operations  13.8 us (9%)
  Pallas kernels  10.7 us (7%)
  local copies, waits for them, and re-layouts  8.38 us (6%)
  other arithmetic  7.49 us (5%)
  matrix products  2.72 us (2%)
    ppermute x5, starting transfers between devices, both_ways(): return lax.ppermute(value, axes + ('core',), pairs)  23.5 us
    all_to_all x2, starting transfers between devices, exchange(): return lax.all_to_all(blocks, axes, split_axis=0, concat_axis=0, tiled=True)  22.4 us
    all_to_all x1, blocking collectives, exchange(): return lax.all_to_all(blocks, axes, split_axis=0, concat_axis=0, tiled=True)  17.8 us
    ppermute x5, waiting for transfers between devices, both_ways(): return lax.ppermute(value, axes + ('core',), pairs)  12.1 us
    all_to_all x2, waiting for transfers between devices, exchange(): return lax.all_to_all(blocks, axes, split_axis=0, concat_axis=0, tiled=True)  11.6 us
    ppermute x2, starting transfers between devices, local(): weights += [lax.ppermute(block, 'core', SWAP) for block in weights]  11.1 us
    pallas_call x1, Pallas kernels, last_products(): pl.pallas_call(last_kernel, out_shape=jax.ShapeDtypeStruct((4, 2, 32, 256...  5.96 us
    pallas_call x1, Pallas kernels, first_products(): pl.pallas_call(first_kernel, out_shape=jax.ShapeDtypeStruct((256, 1024),...  4.75 us
  transfers between devices with their start and end apart: 12, of which 4 were waited for; matrix products, arithmetic and copies ran while one was open for 11% of the time, Pallas kernels for 7%

profile of v2, /device:TPU:1, one launch (start us, length us, event | category | flops | bytes accessed | tf_op | source)
XLA Modules:
  0.0 145.5 jit_solution(7173336448275375737)
XLA Ops:
  6.5 6.0 %collective-permute-start.4 = (bf16[4608,256]{1,0:T(8,128)(2,1)}, bf16[4608,256]{1,0:T(8,128)(2,1)}, u32[]{:S(2)}, u32[]{:S(2)}) collective-permute-start(bf16[4608,256]{1,0:T(8,128)(2,1)} %w0.3), channel_id=1, source_target_pairs={{0,2},{2,4},{4,6},{6,8},{8,10},{10,12},{12,14},{14,0},{1,15},{3,1}... | collective-permute-start | bytes 7077896 | tf_op jit(solution)/shard_map/ppermute | solution.py:29
  12.6 0.7 fusion.12
  13.5 0.9 dynamic_slice.6
  14.4 0.9 broadcast_in_dim.4
  15.3 12.5 %all-to-all-start = ((bf16[8,16,2432]{2,1,0:T(8,128)(2,1)}), bf16[8,16,2432]{2,1,0:T(8,128)(2,1)}, u32[]{:S(2)}, u32[]{:S(2)}) async-start(bf16[8,16,2432]{2,1,0:T(8,128)(2,1)} %broadcast_in_dim.4), calls=%async_computation | async-start | bytes 1245184 | tf_op jit(solution)/shard_map/all_to_all | solution.py:19
  27.8 2.1 %collective-permute-start.5 = (bf16[4608,256]{1,0:T(8,128)(2,1)}, bf16[4608,256]{1,0:T(8,128)(2,1)}, u32[]{:S(2)}, u32[]{:S(2)}) collective-permute-start(bf16[4608,256]{1,0:T(8,128)(2,1)} %w0.3), channel_id=1, source_target_pairs={{0,1},{1,0},{2,3},{3,2},{4,5},{5,4},{6,7},{7,6},{8,9},{9,8},{10,11... | collective-permute-start | bytes 7077896 | tf_op jit(solution)/shard_map/ppermute | solution.py:139
  29.9 8.8 %collective-permute-done.4.w1 = bf16[4608,256]{1,0:T(8,128)(2,1)} collective-permute-done((bf16[4608,256]{1,0:T(8,128)(2,1)}, bf16[4608,256]{1,0:T(8,128)(2,1)}, u32[]{:S(2)}, u32[]{:S(2)}) %collective-permute-start.4) | collective-permute-done | bytes 2359328 | tf_op jit(solution)/shard_map/ppermute | solution.py:29
  38.7 9.0 %collective-permute-start.6 = (bf16[4608,256]{1,0:T(8,128)(2,1)}, bf16[4608,256]{1,0:T(8,128)(2,1)}, u32[]{:S(2)}, u32[]{:S(2)}) collective-permute-start(bf16[4608,256]{1,0:T(8,128)(2,1)} %collective-permute-done.4.w1), channel_id=1, source_target_pairs={{0,1},{1,0},{2,3},{3,2},{4,5},{5,4},{6,7},{7,6},{8,9},{9,8},{10,11... | collective-permute-start | bytes 7077896 | tf_op jit(solution)/shard_map/ppermute | solution.py:139
  47.7 0.9 copy.27
  48.7 1.9 %collective-permute-start.7 = (f32[256,64]{1,0:T(8,128)S(1)}, f32[256,64]{1,0:T(8,128)S(1)}, u32[]{:S(2)}, u32[]{:S(2)}) collective-permute-start(f32[256,64]{1,0:T(8,128)S(1)} %copy.27), channel_id=1, source_target_pairs={{0,2},{2,4},{4,6},{6,8},{8,10},{10,12},{12,14},{14,0},{1,15},{3,1}... | collective-permute-start | bytes 196616 | tf_op jit(solution)/shard_map/ppermute | solution.py:29
  50.6 1.9 %collective-permute-start = (f32[8,4096]{1,0:T(8,128)}, f32[8,4096]{1,0:T(8,128)}, u32[]{:S(2)}, u32[]{:S(2)}) collective-permute-start(f32[8,4096]{1,0:T(8,128)} %bitcast), channel_id=1, source_target_pairs={{0,32},{32,0},{1,33},{33,1},{2,34},{34,2},{3,35},{35,3},{4,36},{36... | collective-permute-start | bytes 393224 | tf_op jit(solution)/shard_map/ppermute | solution.py:134
  52.6 10.0 %collective-permute-start.2 = (bf16[128,2432]{1,0:T(8,128)(2,1)}, bf16[128,2432]{1,0:T(8,128)(2,1)}, u32[]{:S(2)}, u32[]{:S(2)}) collective-permute-start(bf16[128,2432]{1,0:T(8,128)(2,1)} %bitcast.5.near_ref), channel_id=1, source_target_pairs={{0,64},{64,128},{128,192},{192,256},{256,320},{320,384},{384,448},... | collective-permute-start | bytes 1867784 | tf_op jit(solution)/shard_map/ppermute | solution.py:29
  62.7 1.9 %collective-permute-start.8 = (f32[512,64]{1,0:T(8,128)S(1)}, f32[512,64]{1,0:T(8,128)}, u32[]{:S(2)}, u32[]{:S(2)}) collective-permute-start(f32[512,64]{1,0:T(8,128)S(1)} %pad_maximum_fusion.2), channel_id=1, source_target_pairs={{0,1},{1,0},{2,3},{3,2},{4,5},{5,4},{6,7},{7,6},{8,9},{9,8},{10,11... | collective-permute-start | bytes 393224 | tf_op jit(solution)/shard_map/ppermute | solution.py:141
  64.7 1.7 %pad_maximum_fusion.1 = f32[2,8,4096]{2,1,0:T(8,128)} fusion(f32[1,8,4096]{2,1,0:T(8,128)} %bitcast.1, f32[1,8,4096]{2,1,0:T(8,128)} %param.15), kind=kLoop, calls=%fused_computation.8 | loop fusion | flops 65536 | bytes 524288 | tf_op jit(solution)/shard_map/stack | solution.py:134
  66.4 2.8 %collective-permute-start.1 = (bf16[128,2432]{1,0:T(8,128)(2,1)}, bf16[128,2432]{1,0:T(8,128)(2,1)}, u32[]{:S(2)}, u32[]{:S(2)}) collective-permute-start(bf16[128,2432]{1,0:T(8,128)(2,1)} %bitcast.5.near_ref), channel_id=1, source_target_pairs={{0,16},{16,32},{32,48},{48,0},{1,49},{17,1},{33,17},{49,33},{2,18}... | collective-permute-start | bytes 1867784 | tf_op jit(solution)/shard_map/ppermute | solution.py:29
  69.1 1.0 collective-permute-done.2.far_ref
  70.1 2.8 %collective-permute-start.3 = (bf16[128,2432]{1,0:T(8,128)(2,1)}, bf16[128,2432]{1,0:T(8,128)(2,1)}, u32[]{:S(2)}, u32[]{:S(2)}) collective-permute-start(bf16[128,2432]{1,0:T(8,128)(2,1)} %collective-permute-done.2.far_ref), channel_id=1, source_target_pairs={{0,16},{16,32},{32,48},{48,0},{1,49},{17,1},{33,17},{49,33},{2,18}... | collective-permute-start | bytes 1867784 | tf_op jit(solution)/shard_map/ppermute | solution.py:29
  72.9 1.1 pad_maximum_fusion.table_ref
  74.0 0.8 slice.52
  74.8 0.8 slice.53
  75.5 0.2 fusion.6
  75.8 1.7 %fusion.label_ref = f32[256,64]{1,0:T(8,128)S(1)} fusion(s32[1024]{0:T(1024)S(1)} %pad_add_fusion, s32[256]{0:T(256)S(1)} %fusion.6, f32[512,64]{1,0:T(8,128)} %collective-permute-done.8, f32[256,64]{1,0:T(8,128)} %copy-done.4, f32[256,64]{1,0:T(8,128)} %copy-done.2), kind=kOutput, calls=%fused_computation.2 | convolution fusion | flops 201719808 | bytes 332800 | tf_op jit(solution)/shard_map/dot_general | solution.py:158
  77.5 4.7 %shard_map.82.begun_ref = f32[256,1024]{1,0:T(8,128)S(1)} custom-call(s32[2]{0:T(128)S(1)} %get-tuple-element.25.where_ref, bf16[128,2432]{1,0:T(8,128)(2,1)} %bitcast.5.near_ref, bf16[128,2432]{1,0:T(8,128)(2,1)} %collective-permute-done.2.far_ref, bf16[4608,256]{1,0:T(8,128)(2,1)S(1)} %copy-done.1, bf16[4608,256]{1,0:T(8,128)(2,1)} %collective-permute-done.4.w1, ...), custom_call_target="tpu_custom_call" | custom-call | flops 1207959552 | bytes 7000000 | tf_op jit(solution)/shard_map/pallas_call | solution.py:88
  82.3 2.3 %collective-permute-done.3.far_ref = bf16[128,2432]{1,0:T(8,128)(2,1)} collective-permute-done((bf16[128,2432]{1,0:T(8,128)(2,1)}, bf16[128,2432]{1,0:T(8,128)(2,1)}, u32[]{:S(2)}, u32[]{:S(2)}) %collective-permute-start.3) | collective-permute-done | bytes 622624 | tf_op jit(solution)/shard_map/ppermute | solution.py:29
  84.6 6.0 %shard_map.83 = f32[4,2,32,256]{3,2,1,0:T(8,128)S(1)} custom-call(s32[2]{0:T(128)S(1)} %get-tuple-element.24.where_ref, bf16[128,2432]{1,0:T(8,128)(2,1)} %collective-permute-done.1.near_ref, bf16[128,2432]{1,0:T(8,128)(2,1)} %collective-permute-done.3.far_ref, bf16[4608,256]{1,0:T(8,128)(2,1)S(1)} %copy-done.1, ...), custom_call_target="tpu_custom_call" | custom-call | flops 1207959552 | bytes 7000000 | tf_op jit(solution)/shard_map/pallas_call | solution.py:103
  90.6 17.8 %all_to_all.15 = f32[32,8,256]{2,1,0:T(8,128)S(1)} all-to-all(f32[32,8,256]{2,1,0:T(8,128)S(1)} %bitcast.39), channel_id=1, replica_groups=mesh['zh'=4,'zl'=2,'xh'=2,'xl'=2,'yh'=4,'yl'=2,'core'=2] {'zh','zl','xh'..., dimensions={0} | all-to-all | bytes 524288 | tf_op jit(solution)/shard_map/all_to_all | solution.py:19
  108.4 0.2 slice_reduce_fusion.3
  108.6 0.1 copy.41
  108.7 0.1 copy.42
  108.8 0.2 fusion.10
  109.3 0.1 fusion.5
  109.5 0.7 broadcast_in_dim.5
  110.2 9.9 %all-to-all-start.2 = ((f32[32,8,256]{2,1,0:T(8,128)}), f32[32,8,256]{2,1,0:T(8,128)S(1)}, u32[]{:S(2)}, u32[]{:S(2)}) async-start(f32[32,8,256]{2,1,0:T(8,128)} %broadcast_in_dim.5), calls=%async_computation.2 | async-start | bytes 524288 | tf_op jit(solution)/shard_map/all_to_all | solution.py:19
  120.2 0.3 fusion.18
  120.5 11.6 %all-to-all-done.2 = f32[32,8,256]{2,1,0:T(8,128)S(1)} async-done(((f32[32,8,256]{2,1,0:T(8,128)}), f32[32,8,256]{2,1,0:T(8,128)S(1)}, u32[]{:S(2)}, u32[]{:S(2)}) %all-to-all-start.2) | async-done | bytes 262176 | tf_op jit(solution)/shard_map/all_to_all | solution.py:19
  132.1 0.1 fusion.16
  132.2 0.3 copy.44
  132.5 0.3 copy.45
  132.9 1.1 copy.43
  134.0 0.2 copy.50
  134.2 0.7 multiply_reduce_fusion.1
  135.0 0.2 divide_subtract_fusion
  135.1 0.2 copy.38
  135.3 0.2 fusion.19
  135.6 0.2 fusion.20
  135.8 0.2 fusion.21
  136.2 1.8 %multiply_reduce_fusion = f32[8,2,8]{2,1,0:T(2,128)S(1)} fusion(f32[8,2,8,4096]{3,2,1,0:T(8,128)} %bitcast.42, f32[4096]{0:T(1024)S(1)} %mul.126), kind=kLoop, calls=%fused_computation | loop fusion | flops 1048448 | bytes 2114048 | tf_op jit(solution)/shard_map/reduce_sum | solution.py:181
  138.0 0.7 copy.39
  (43 shorter events, 0.9 us)
Async XLA Ops:
  6.5 113.6 %copy-start = (bf16[4608,64]{0,1:T(8,128)(2,1)S(1)}, bf16[4608,64]{0,1:T(8,128)(2,1)}, u32[]{:S(2)}) copy-start(bf16[4608,64]{0,1:T(8,128)(2,1)} %param.11) | copy-start | bytes 1769476
  6.5 32.1 %collective-permute-start.4 = (bf16[4608,256]{1,0:T(8,128)(2,1)}, bf16[4608,256]{1,0:T(8,128)(2,1)}, u32[]{:S(2)}, u32[]{:S(2)}) collective-permute-start(bf16[4608,256]{1,0:T(8,128)(2,1)} %w0.3), channel_id=1, source_target_pairs={{0,2},{2,4},{4,6},{6,8},{8,10},{10,12},{12,14},{14,0},{1,15},{3,1}... | collective-permute-start | bytes 7077896 | tf_op jit(solution)/shard_map/ppermute | solution.py:29
  15.3 37.4 %all-to-all-start = ((bf16[8,16,2432]{2,1,0:T(8,128)(2,1)}), bf16[8,16,2432]{2,1,0:T(8,128)(2,1)}, u32[]{:S(2)}, u32[]{:S(2)}) async-start(bf16[8,16,2432]{2,1,0:T(8,128)(2,1)} %broadcast_in_dim.4), calls=%async_computation | async-start | bytes 1245184 | tf_op jit(solution)/shard_map/all_to_all | solution.py:19
  27.7 49.8 %copy-start.1 = (bf16[4608,256]{1,0:T(8,128)(2,1)S(1)}, bf16[4608,256]{1,0:T(8,128)(2,1)}, u32[]{:S(2)}) copy-start(bf16[4608,256]{1,0:T(8,128)(2,1)} %w0.3) | copy-start | bytes 7077892
  27.7 108.4 %all-gather.3.cloned.1.call-start = ((), (), s32[]{:S(2)}) async-start(), calls=%async_computation.3 | async-start | bytes 2359296 | tf_op jit(solution)/shard_map/all_gather | solution.py:136
  27.8 49.7 %collective-permute-start.5 = (bf16[4608,256]{1,0:T(8,128)(2,1)}, bf16[4608,256]{1,0:T(8,128)(2,1)}, u32[]{:S(2)}, u32[]{:S(2)}) collective-permute-start(bf16[4608,256]{1,0:T(8,128)(2,1)} %w0.3), channel_id=1, source_target_pairs={{0,1},{1,0},{2,3},{3,2},{4,5},{5,4},{6,7},{7,6},{8,9},{9,8},{10,11... | collective-permute-start | bytes 7077896 | tf_op jit(solution)/shard_map/ppermute | solution.py:139
  38.7 38.8 %collective-permute-start.6 = (bf16[4608,256]{1,0:T(8,128)(2,1)}, bf16[4608,256]{1,0:T(8,128)(2,1)}, u32[]{:S(2)}, u32[]{:S(2)}) collective-permute-start(bf16[4608,256]{1,0:T(8,128)(2,1)} %collective-permute-done.4.w1), channel_id=1, source_target_pairs={{0,1},{1,0},{2,3},{3,2},{4,5},{5,4},{6,7},{7,6},{8,9},{9,8},{10,11... | collective-permute-start | bytes 7077896 | tf_op jit(solution)/shard_map/ppermute | solution.py:139
  48.6 24.2 %copy-start.2 = (f32[256,64]{1,0:T(8,128)}, f32[256,64]{1,0:T(8,128)S(1)}, u32[]{:S(2)}) copy-start(f32[256,64]{1,0:T(8,128)S(1)} %copy.27) | copy-start | bytes 196612
  48.7 14.0 %collective-permute-start.7 = (f32[256,64]{1,0:T(8,128)S(1)}, f32[256,64]{1,0:T(8,128)S(1)}, u32[]{:S(2)}, u32[]{:S(2)}) collective-permute-start(f32[256,64]{1,0:T(8,128)S(1)} %copy.27), channel_id=1, source_target_pairs={{0,2},{2,4},{4,6},{6,8},{8,10},{10,12},{12,14},{14,0},{1,15},{3,1}... | collective-permute-start | bytes 196616 | tf_op jit(solution)/shard_map/ppermute | solution.py:29
  50.6 14.1 %collective-permute-start = (f32[8,4096]{1,0:T(8,128)}, f32[8,4096]{1,0:T(8,128)}, u32[]{:S(2)}, u32[]{:S(2)}) collective-permute-start(f32[8,4096]{1,0:T(8,128)} %bitcast), channel_id=1, source_target_pairs={{0,32},{32,0},{1,33},{33,1},{2,34},{34,2},{3,35},{35,3},{4,36},{36... | collective-permute-start | bytes 393224 | tf_op jit(solution)/shard_map/ppermute | solution.py:134
  52.6 17.5 %collective-permute-start.2 = (bf16[128,2432]{1,0:T(8,128)(2,1)}, bf16[128,2432]{1,0:T(8,128)(2,1)}, u32[]{:S(2)}, u32[]{:S(2)}) collective-permute-start(bf16[128,2432]{1,0:T(8,128)(2,1)} %bitcast.5.near_ref), channel_id=1, source_target_pairs={{0,64},{64,128},{128,192},{192,256},{256,320},{320,384},{384,448},... | collective-permute-start | bytes 1867784 | tf_op jit(solution)/shard_map/ppermute | solution.py:29
  62.7 10.2 %copy-start.4 = (f32[256,64]{1,0:T(8,128)}, f32[256,64]{1,0:T(8,128)S(1)}, u32[]{:S(2)}) copy-start(f32[256,64]{1,0:T(8,128)S(1)} %collective-permute-done.7) | copy-start | bytes 196612
  62.7 10.2 %collective-permute-start.8 = (f32[512,64]{1,0:T(8,128)S(1)}, f32[512,64]{1,0:T(8,128)}, u32[]{:S(2)}, u32[]{:S(2)}) collective-permute-start(f32[512,64]{1,0:T(8,128)S(1)} %pad_maximum_fusion.2), channel_id=1, source_target_pairs={{0,1},{1,0},{2,3},{3,2},{4,5},{5,4},{6,7},{7,6},{8,9},{9,8},{10,11... | collective-permute-start | bytes 393224 | tf_op jit(solution)/shard_map/ppermute | solution.py:141
  66.4 15.9 %collective-permute-start.1 = (bf16[128,2432]{1,0:T(8,128)(2,1)}, bf16[128,2432]{1,0:T(8,128)(2,1)}, u32[]{:S(2)}, u32[]{:S(2)}) collective-permute-start(bf16[128,2432]{1,0:T(8,128)(2,1)} %bitcast.5.near_ref), channel_id=1, source_target_pairs={{0,16},{16,32},{32,48},{48,0},{1,49},{17,1},{33,17},{49,33},{2,18}... | collective-permute-start | bytes 1867784 | tf_op jit(solution)/shard_map/ppermute | solution.py:29
  70.1 14.5 %collective-permute-start.3 = (bf16[128,2432]{1,0:T(8,128)(2,1)}, bf16[128,2432]{1,0:T(8,128)(2,1)}, u32[]{:S(2)}, u32[]{:S(2)}) collective-permute-start(bf16[128,2432]{1,0:T(8,128)(2,1)} %collective-permute-done.2.far_ref), channel_id=1, source_target_pairs={{0,16},{16,32},{32,48},{48,0},{1,49},{17,1},{33,17},{49,33},{2,18}... | collective-permute-start | bytes 1867784 | tf_op jit(solution)/shard_map/ppermute | solution.py:29
  90.6 29.6 %copy-start.3 = (bf16[64,4608]{1,0:T(8,128)(2,1)S(1)}, bf16[64,4608]{1,0:T(8,128)(2,1)}, u32[]{:S(2)}) copy-start(bf16[64,4608]{1,0:T(8,128)(2,1)} %param.8) | copy-start | bytes 1769476
  110.2 21.8 %all-to-all-start.2 = ((f32[32,8,256]{2,1,0:T(8,128)}), f32[32,8,256]{2,1,0:T(8,128)S(1)}, u32[]{:S(2)}, u32[]{:S(2)}) async-start(f32[32,8,256]{2,1,0:T(8,128)} %broadcast_in_dim.5), calls=%async_computation.2 | async-start | bytes 524288 | tf_op jit(solution)/shard_map/all_to_all | solution.py:19
  132.2 3.4 %copy-start.5 = (f32[64,64]{1,0:T(8,128)S(1)}, f32[64,64]{1,0:T(8,128)}, u32[]{:S(2)}) copy-start(f32[64,64]{1,0:T(8,128)} %param.13) | copy-start | bytes 49156
  132.5 3.4 %copy-start.6 = (f32[64,64]{1,0:T(8,128)S(1)}, f32[64,64]{1,0:T(8,128)}, u32[]{:S(2)}) copy-start(f32[64,64]{1,0:T(8,128)} %param.14) | copy-start | bytes 49156
Sparse Core Ops, SparseCore 0:
  74.9 43.2 all-gather.2

commit v3 on v2

--- a/solution.py
+++ b/solution.py
@@ -1,3 +1,4 @@
+import functools
 import jax
 import jax.numpy as jnp
 from jax import lax
@@ -71,6 +72,48 @@
             out_ref[:, pl.ds(place, 1), :, 128:256] = right[start : start + ROWS].reshape(4, 1, 32, 128)
 
 
+def merge_kernel(parts_ref, out_ref):
+    left, right = parts_ref[:, :, 0:128], parts_ref[:, :, 128:256]
+    largest = right[:, :, 0:1]
+    top = jnp.max(largest, axis=0, keepdims=True)
+    scaled = jnp.exp(largest - top)
+    lane = lax.broadcasted_iota(jnp.int32, (1, 8, 128), 2)
+    sums = jnp.sum(left * scaled, axis=0, keepdims=True)
+    label_rows = jnp.sum(left, axis=0, keepdims=True)
+    totals = jnp.sum(right[:, :, 1:2] * scaled, axis=0, keepdims=True)
+    left = jnp.where(lane < 64, sums, label_rows)
+    right = jnp.where(lane == 0, top, jnp.where(lane == 1, totals, 0.0))
+    out_ref[:, :, 0:128] = jnp.broadcast_to(left, (32, 8, 128))
+    out_ref[:, :, 128:256] = jnp.broadcast_to(right, (32, 8, 128))
+
+
+def end_kernel(half_ref, parts_ref, mapped_ref, even_ref, odd_ref, right_ref, queries_ref, out_ref):
+    def precise(first, second):
+        return jnp.dot(first, second, precision=PRECISE, preferred_element_type=jnp.float32)
+
+    parts = [parts_ref[:, part].reshape(64, 256) for part in range(4)]
+    largest = [part[:, 128:129] for part in parts]
+    top = functools.reduce(jnp.maximum, largest)
+    scaled = [jnp.exp(value - top) for value in largest]
+    totals = sum(part[:, 129:130] * scale for part, scale in zip(parts, scaled))
+    sums = sum(part[:, 0:64] * scale for part, scale in zip(parts, scaled))
+    projected = sums / totals - sum(part[:, 64:128] for part in parts)
+    feature = precise(mapped_ref[...], projected)
+    even = precise(precise(even_ref[...], feature), right_ref[...])
+    odd = precise(precise(odd_ref[...], feature), right_ref[...])
+    flat = jnp.concatenate([even, odd], axis=1)
+    products = jnp.zeros((128, 128), jnp.float32)
+    for pair in range(32):
+        products += queries_ref[:, 128 * pair : 128 * pair + 128] * flat[pair : pair + 1, :]
+    lane = lax.broadcasted_iota(jnp.int32, (8, 16), 1)
+    scores = jnp.zeros((8, 16), jnp.float32)
+    for block in range(16):
+        group = block // 2 * 2 + jnp.where(half_ref[0] == 0, block % 2, 1 - block % 2)
+        column = jnp.sum(products[8 * block : 8 * block + 8], axis=1, keepdims=True)
+        scores = jnp.where(lane == group, column, scores)
+    out_ref[...] = scores
+
+
 def product_specs():
     rows = pl.BlockSpec((ROWS, DEPTH), lambda step, where: (0, step))
     weight = pl.BlockSpec((DEPTH, 256), lambda step, where: (where[0] * STEPS + step, 0))
@@ -131,13 +174,14 @@
     near_x = both_ways(near, ("xh", "xl"), 4)
     far_x = both_ways(far, ("xh", "xl"), 4)
 
-    query_pair = jnp.stack([queries[0], lax.ppermute(queries[0], "xh", SWAP)])
-    query_pair, _ = lax.optimization_barrier((query_pair, near))
+    late_query, _ = lax.optimization_barrier((queries[0], near))
+    query_pair = jnp.stack([late_query, lax.ppermute(late_query, "xh", SWAP)])
     every_query = lax.all_gather(query_pair, ("zh", "zl"), axis=0)
 
     weights = [unembed, both_ways(unembed, ("yh", "yl"), 8)]
-    weights += [lax.ppermute(block, "core", SWAP) for block in weights]
     tables = jnp.concatenate([out_proj, both_ways(out_proj, ("yh", "yl"), 8)], axis=0)
+    late_weight, tables, _, _ = lax.optimization_barrier((weights[1], tables, far, near_x))
+    weights += [lax.ppermute(block, "core", SWAP) for block in (unembed, late_weight)]
     table = jnp.concatenate([tables, lax.ppermute(tables, "core", SWAP)], axis=0)
 
     def block_start(at_y, at_core):
@@ -161,26 +205,22 @@
     begun = first_products(jnp.stack([xl, zl]), near, far, weights)
     packed = last_products(jnp.stack([1 - xl, zl]), near_x, far_x, weights, begun, table, label_rows)
 
-    def merge(parts, axis):
-        sums, label_rows = parts[..., :64], parts[..., 64:128]
-        largest, totals = parts[..., 128:129], parts[..., 129:130]
-        top = jnp.max(largest, axis=axis, keepdims=True)
-        scaled = jnp.exp(largest - top)
-        sums = jnp.sum(sums * scaled, axis=axis)
-        return sums, jnp.sum(label_rows, axis=axis), jnp.squeeze(top, axis), jnp.sum(totals * scaled, axis=axis)
-
-    merged = merge(exchange(packed.reshape(32, 8, 256), ("zh", "zl", "xh", "xl")), 0)
-    packed = jnp.pad(jnp.concatenate(merged, axis=-1), ((0, 0), (0, 126)))
-    parts = spread_out(packed, VOC, 32).reshape(2, 4, 2, 2, 8, 256)
-    sums, label_rows, _, totals = merge(parts, 1)
-    projected = sums / totals - label_rows
-    projected = jnp.transpose(projected, (1, 2, 0, 3, 4)).reshape(64, 64)
-
-    feature = jnp.dot(mapped.T, projected, precision=PRECISE)
-    precond = jnp.dot(jnp.dot(left_inv, feature, precision=PRECISE), right_inv, precision=PRECISE)
-    scores = jnp.sum(every_query * precond.reshape(1, 1, 1, 4096), axis=3)
-    scores = jnp.where(xh == 0, scores, scores[:, ::-1])
-    return scores.reshape(1, 16, 8)
+    parts = exchange(packed.reshape(32, 8, 256), ("zh", "zl", "xh", "xl"))
+    merged = pl.pallas_call(
+        merge_kernel,
+        out_shape=jax.ShapeDtypeStruct((32, 8, 256), jnp.float32),
+        cost_estimate=pl.CostEstimate(flops=300_000, bytes_accessed=600_000, transcendentals=256),
+    )(parts)
+    parts = exchange(merged, VOC).reshape(2, 4, 4, 8, 256)
+    mapped = jnp.transpose(mapped.reshape(4, 2, 8, 64), (3, 1, 0, 2)).reshape(64, 64)
+    scores = pl.pallas_call(
+        end_kernel,
+        out_shape=jax.ShapeDtypeStruct((8, 16), jnp.float32),
+        in_specs=[pl.BlockSpec(memory_space=pltpu.SMEM)] + [pl.BlockSpec(memory_space=pltpu.VMEM)] * 6,
+        cost_estimate=pl.CostEstimate(flops=2_000_000, bytes_accessed=2_500_000, transcendentals=256),
+        compiler_params=pltpu.CompilerParams(vmem_limit_bytes=24 << 20),
+    )(xh.reshape(1), parts, mapped, left_inv[0::2], left_inv[1::2], right_inv, every_query.reshape(128, 4096))
+    return scores.T[None]
 
 
 def solution(mesh):

time: 147 us -> 140 us (0.952)
  blocking collectives: 17.8 us -> 50.1 us
  starting transfers between devices: 60.8 us -> 38.8 us
  waiting for transfers between devices: 23.7 us -> 13.2 us
  other arithmetic: 7.49 us -> 1.85 us
  Pallas kernels: 10.7 us -> 14.1 us
  matrix products: 2.72 us -> 0.94 us
  local copies, waits for them, and re-layouts: 8.38 us -> 6.75 us
    all_to_all x1 -> x2, blocking collectives: 17.8 us -> 50.1 us  [exchange(): return lax.all_to_all(blocks, axes, split_axis=0, concat_axis=0, tiled=True)]
    all_to_all x2 -> x1, starting transfers between devices: 22.4 us -> 6.55 us  [exchange(): return lax.all_to_all(blocks, axes, split_axis=0, concat_axis=0, tiled=True)]
    ppermute x5, waiting for transfers between devices: 12.1 us -> 1.9 us  [both_ways(): return lax.ppermute(value, axes + ('core',), pairs)]
    ppermute x5, starting transfers between devices: 23.5 us -> 19.3 us  [both_ways(): return lax.ppermute(value, axes + ('core',), pairs)]
    pallas_call x0 -> x2, Pallas kernels: none -> 3.45 us  [the longest x1 1.84 us: local(): pl.pallas_call(merge_kernel, out_shape=jax.ShapeDtypeStruct((32, 8, 256),...]
    reduce_sum x4 -> x0, other arithmetic: 2.73 us -> none  [the longest x1 1.83 us: local(): scores = jnp.sum(every_query * precond.reshape(1, 1, 1, 4096), axis=3)]
    ppermute x3, starting transfers between devices: 13 us -> 11.1 us  [the longest x2 6.69 us: local(): lax.ppermute(block, 'core', SWAP)]
    all_to_all x2 -> x1, waiting for transfers between devices: 11.6 us -> 9.97 us  [exchange(): return lax.all_to_all(blocks, axes, split_axis=0, concat_axis=0, tiled=True)]
  transfers between devices with their start and end apart: 12 -> 11, of which waited for: 4 -> 4; matrix products, arithmetic and copies ran while one was open for 11% -> 6% of each run, Pallas kernels for 7% -> 9%
where the time goes in v3:
time: 140 us; the launch traced here: 139 us
  blocking collectives  50.1 us (36%)
  starting transfers between devices  38.8 us (28%)
  Pallas kernels  14.1 us (10%)
  between operations  13.7 us (10%)
  waiting for transfers between devices  13.2 us (9%)
  local copies, waits for them, and re-layouts  6.75 us (5%)
  other arithmetic  1.85 us (1%)
    all_to_all x2, blocking collectives, exchange(): return lax.all_to_all(blocks, axes, split_axis=0, concat_axis=0, tiled=True)  50.1 us
    ppermute x5, starting transfers between devices, both_ways(): return lax.ppermute(value, axes + ('core',), pairs)  19.3 us
    all_to_all x1, waiting for transfers between devices, exchange(): return lax.all_to_all(blocks, axes, split_axis=0, concat_axis=0, tiled=True)  9.97 us
    ppermute x2, starting transfers between devices, local(): lax.ppermute(block, 'core', SWAP)  6.69 us
    all_to_all x1, starting transfers between devices, exchange(): return lax.all_to_all(blocks, axes, split_axis=0, concat_axis=0, tiled=True)  6.55 us
    pallas_call x1, Pallas kernels, last_products(): pl.pallas_call(last_kernel, out_shape=jax.ShapeDtypeStruct((4, 2, 32, 256...  5.81 us
    pallas_call x1, Pallas kernels, first_products(): pl.pallas_call(first_kernel, out_shape=jax.ShapeDtypeStruct((256, 1024),...  4.81 us
    ppermute x1, starting transfers between devices, local(): query_pair = jnp.stack([late_query, lax.ppermute(late_query, 'xh', SWAP)])  4.37 us
  transfers between devices with their start and end apart: 11, of which 4 were waited for; matrix products, arithmetic and copies ran while one was open for 6% of the time, Pallas kernels for 9%

profile of v3, /device:TPU:1, one launch (start us, length us, event | category | flops | bytes accessed | tf_op | source)
XLA Modules:
  0.0 139.4 jit_solution(4322957870811223696)
XLA Ops:
  6.5 0.0 copy-start
  6.5 0.0 all-gather.3.cloned.1.call-start
  6.5 6.0 %collective-permute-start.3 = (bf16[4608,256]{1,0:T(8,128)(2,1)}, bf16[4608,256]{1,0:T(8,128)(2,1)}, u32[]{:S(2)}, u32[]{:S(2)}) collective-permute-start(bf16[4608,256]{1,0:T(8,128)(2,1)} %w0.3), channel_id=1, source_target_pairs={{0,2},{2,4},{4,6},{6,8},{8,10},{10,12},{12,14},{14,0},{1,15},{3,1}... | collective-permute-start | bytes 7077896 | tf_op jit(solution)/shard_map/ppermute | solution.py:30
  12.6 0.7 fusion.9
  13.4 0.1 copy.27
  13.5 0.9 dynamic_slice.6
  14.4 31.6 %all_to_all.15 = bf16[8,16,2432]{2,1,0:T(8,128)(2,1)} all-to-all(bf16[8,16,2432]{2,1,0:T(8,128)(2,1)S(1)} %broadcast_in_dim.4), channel_id=1, replica_groups=mesh['zh'=4,'zl'=2,'xh'=2,'xl'=2,'yh'=4,'yl'=2,'core'=2] {'zh','xh'}, dimensions={0} | all-to-all | bytes 1245184 | tf_op jit(solution)/shard_map/all_to_all | solution.py:20
  46.1 4.4 %collective-permute-start.8 = (f32[8,4096]{1,0:T(8,128)}, f32[8,4096]{1,0:T(8,128)S(1)}, u32[]{:S(2)}, u32[]{:S(2)}) collective-permute-start(f32[8,4096]{1,0:T(8,128)} %bitcast.32), channel_id=1, source_target_pairs={{0,32},{32,0},{1,33},{33,1},{2,34},{34,2},{3,35},{35,3},{4,36},{36... | collective-permute-start | bytes 393224 | tf_op jit(solution)/shard_map/ppermute | solution.py:178
  50.5 2.3 %collective-permute-start = (bf16[128,2432]{1,0:T(8,128)(2,1)}, bf16[128,2432]{1,0:T(8,128)(2,1)}, u32[]{:S(2)}, u32[]{:S(2)}) collective-permute-start(bf16[128,2432]{1,0:T(8,128)(2,1)} %bitcast.6.near_ref), channel_id=1, source_target_pairs={{0,16},{16,32},{32,48},{48,0},{1,49},{17,1},{33,17},{49,33},{2,18}... | collective-permute-start | bytes 1867784 | tf_op jit(solution)/shard_map/ppermute | solution.py:30
  52.7 5.3 %collective-permute-start.1 = (bf16[128,2432]{1,0:T(8,128)(2,1)}, bf16[128,2432]{1,0:T(8,128)(2,1)}, u32[]{:S(2)}, u32[]{:S(2)}) collective-permute-start(bf16[128,2432]{1,0:T(8,128)(2,1)} %bitcast.6.near_ref), channel_id=1, source_target_pairs={{0,64},{64,128},{128,192},{192,256},{256,320},{320,384},{384,448},... | collective-permute-start | bytes 1867784 | tf_op jit(solution)/shard_map/ppermute | solution.py:30
  58.1 1.9 %collective-permute-start.4 = (bf16[4608,256]{1,0:T(8,128)(2,1)}, bf16[4608,256]{1,0:T(8,128)(2,1)}, u32[]{:S(2)}, u32[]{:S(2)}) collective-permute-start(bf16[4608,256]{1,0:T(8,128)(2,1)} %w0.3), channel_id=1, source_target_pairs={{0,1},{1,0},{2,3},{3,2},{4,5},{5,4},{6,7},{7,6},{8,9},{9,8},{10,11... | collective-permute-start | bytes 7077896 | tf_op jit(solution)/shard_map/ppermute | solution.py:184
  60.0 0.9 copy.22
  60.9 0.0 collective-permute-done.8
  61.0 3.1 %collective-permute-start.5 = (f32[256,64]{1,0:T(8,128)S(1)}, f32[256,64]{1,0:T(8,128)S(1)}, u32[]{:S(2)}, u32[]{:S(2)}) collective-permute-start(f32[256,64]{1,0:T(8,128)S(1)} %copy.22), channel_id=1, source_target_pairs={{0,2},{2,4},{4,6},{6,8},{8,10},{10,12},{12,14},{14,0},{1,15},{3,1}... | collective-permute-start | bytes 196616 | tf_op jit(solution)/shard_map/ppermute | solution.py:30
  64.1 0.7 pad_maximum_fusion.1
  64.8 0.0 all-gather.3.cloned.1.call-update
  64.8 1.8 %collective-permute-done.5 = f32[256,64]{1,0:T(8,128)S(1)} collective-permute-done((f32[256,64]{1,0:T(8,128)S(1)}, f32[256,64]{1,0:T(8,128)S(1)}, u32[]{:S(2)}, u32[]{:S(2)}) %collective-permute-start.5) | collective-permute-done | bytes 65568 | tf_op jit(solution)/shard_map/ppermute | solution.py:30
  66.7 0.0 collective-permute-done.near_ref
  66.7 0.0 collective-permute-done.1.far_ref
  66.7 0.0 collective-permute-done.3.w1
  66.7 4.8 %collective-permute-start.6 = (bf16[4608,256]{1,0:T(8,128)(2,1)}, bf16[4608,256]{1,0:T(8,128)(2,1)}, u32[]{:S(2)}, u32[]{:S(2)}) collective-permute-start(bf16[4608,256]{1,0:T(8,128)(2,1)} %collective-permute-done.3.w1), channel_id=1, source_target_pairs={{0,1},{1,0},{2,3},{3,2},{4,5},{5,4},{6,7},{7,6},{8,9},{9,8},{10,11... | collective-permute-start | bytes 7077896 | tf_op jit(solution)/shard_map/ppermute | solution.py:184
  71.6 0.1 pad_add_fusion.1
  71.7 0.8 slice.28
  72.4 0.8 slice.29
  73.2 2.5 %collective-permute-start.2 = (bf16[128,2432]{1,0:T(8,128)(2,1)}, bf16[128,2432]{1,0:T(8,128)(2,1)S(1)}, u32[]{:S(2)}, u32[]{:S(2)}) collective-permute-start(bf16[128,2432]{1,0:T(8,128)(2,1)} %collective-permute-done.1.far_ref), channel_id=1, source_target_pairs={{0,16},{16,32},{32,48},{48,0},{1,49},{17,1},{33,17},{49,33},{2,18}... | collective-permute-start | bytes 1867784 | tf_op jit(solution)/shard_map/ppermute | solution.py:30
  75.7 1.9 %collective-permute-start.7 = (f32[512,64]{1,0:T(8,128)S(1)}, f32[512,64]{1,0:T(8,128)S(1)}, u32[]{:S(2)}, u32[]{:S(2)}) collective-permute-start(f32[512,64]{1,0:T(8,128)S(1)} %pad_maximum_fusion), channel_id=1, source_target_pairs={{0,1},{1,0},{2,3},{3,2},{4,5},{5,4},{6,7},{7,6},{8,9},{9,8},{10,11... | collective-permute-start | bytes 393224 | tf_op jit(solution)/shard_map/ppermute | solution.py:185
  77.7 0.2 fusion.5
  77.9 1.3 collective-permute-done.7
  79.2 0.7 fusion.label_ref
  79.8 0.0 collective-permute-done.4.w2
  79.8 0.0 collective-permute-done.6.w3
  79.9 4.8 %shard_map.82.begun_ref = f32[256,1024]{1,0:T(8,128)S(1)} custom-call(s32[2]{0:T(128)S(1)} %get-tuple-element.15.where_ref, bf16[128,2432]{1,0:T(8,128)(2,1)} %bitcast.6.near_ref, bf16[128,2432]{1,0:T(8,128)(2,1)} %collective-permute-done.1.far_ref, bf16[4608,256]{1,0:T(8,128)(2,1)S(1)} %copy-done.1, bf16[4608,256]{1,0:T(8,128)(2,1)} %collective-permute-done.3.w1, ...), custom_call_target="tpu_custom_call" | custom-call | flops 1207959552 | bytes 7000000 | tf_op jit(solution)/shard_map/pallas_call | solution.py:131
  84.7 0.1 collective-permute-done.2.far_ref
  84.8 5.8 %shard_map.83 = f32[4,2,32,256]{3,2,1,0:T(8,128)S(1)} custom-call(s32[2]{0:T(128)S(1)} %get-tuple-element.14.where_ref, bf16[128,2432]{1,0:T(8,128)(2,1)} %collective-permute-done.near_ref, bf16[128,2432]{1,0:T(8,128)(2,1)S(1)} %collective-permute-done.2.far_ref, bf16[4608,256]{1,0:T(8,128)(2,1)S(1)} %copy-done.1, ...), custom_call_target="tpu_custom_call" | custom-call | flops 1207959552 | bytes 7000000 | tf_op jit(solution)/shard_map/pallas_call | solution.py:146
  90.6 0.0 copy-start.3
  90.6 18.5 %all_to_all.16.parts_ref = f32[32,8,256]{2,1,0:T(8,128)} all-to-all(f32[32,8,256]{2,1,0:T(8,128)S(1)} %bitcast.28), channel_id=1, replica_groups=mesh['zh'=4,'zl'=2,'xh'=2,'xl'=2,'yh'=4,'yl'=2,'core'=2] {'zh','zl','xh'..., dimensions={0} | all-to-all | bytes 524288 | tf_op jit(solution)/shard_map/all_to_all | solution.py:20
  109.0 1.8 %shard_map.84 = f32[32,8,256]{2,1,0:T(8,128)} custom-call(f32[32,8,256]{2,1,0:T(8,128)} %all_to_all.16.parts_ref), custom_call_target="tpu_custom_call" | custom-call | flops 300000 | bytes 600000 | tf_op jit(solution)/shard_map/pallas_call | solution.py:209
  110.9 6.5 %all-to-all-start.2 = ((f32[32,8,256]{2,1,0:T(8,128)}), f32[32,8,256]{2,1,0:T(8,128)S(1)}, u32[]{:S(2)}, u32[]{:S(2)}) async-start(f32[32,8,256]{2,1,0:T(8,128)} %shard_map.84), calls=%async_computation.2 | async-start | bytes 524288 | tf_op jit(solution)/shard_map/all_to_all | solution.py:20
  117.4 0.8 slice.26.even_ref
  118.2 0.8 slice.27.odd_ref
  119.0 0.0 copy-done.4
  119.0 0.3 fusion.13
  119.3 0.1 copy.25.mapped_ref
  119.4 0.0 all-gather.3.cloned.1.call-done
  119.4 10.0 %all-to-all-done.2 = f32[32,8,256]{2,1,0:T(8,128)S(1)} async-done(((f32[32,8,256]{2,1,0:T(8,128)}), f32[32,8,256]{2,1,0:T(8,128)S(1)}, u32[]{:S(2)}, u32[]{:S(2)}) %all-to-all-start.2) | async-done | bytes 262176 | tf_op jit(solution)/shard_map/all_to_all | solution.py:20
  129.4 0.0 copy-done.3
  129.4 1.6 %copy-done.2 = f32[16,8,4096]{2,1,0:T(8,128)S(1)} copy-done((f32[16,8,4096]{2,1,0:T(8,128)S(1)}, f32[16,8,4096]{2,1,0:T(8,128)}, u32[]{:S(2)}) %copy-start.2) | copy-done | bytes 2097176
  131.0 1.6 %shard_map.85 = f32[8,16]{1,0:T(8,128)} custom-call(s32[1]{0:T(128)} %bitcast.half_ref, f32[2,4,4,8,256]{4,3,2,1,0:T(8,128)S(1)} %bitcast.29, f32[64,64]{1,0:T(8,128)S(1)} %copy.25.mapped_ref, f32[32,64]{1,0:T(8,128)S(1)} %slice.26.even_ref, f32[32,64]{1,0:T(8,128)S(1)} %slice.27.odd_ref, f32[64,64]{1,0:T(8,128)S(1)} %copy-done.3, f32[128,4096]{1,0:T(8,128)S(1)} %bitcast.27), custom_call_target="tpu_custom_call" | custom-call | flops 2000000 | bytes 2500000 | tf_op jit(solution)/shard_map/pallas_call | solution.py:216
  (19 shorter events, 0.2 us)
Async XLA Ops:
  6.5 112.4 %copy-start = (bf16[4608,64]{0,1:T(8,128)(2,1)S(1)}, bf16[4608,64]{0,1:T(8,128)(2,1)}, u32[]{:S(2)}) copy-start(bf16[4608,64]{0,1:T(8,128)(2,1)} %param.11) | copy-start | bytes 1769476
  6.5 57.6 %copy-start.5 = (f32[1,8,4096]{2,1,0:T(8,128)S(1)}, f32[1,8,4096]{2,1,0:T(8,128)}, u32[]{:S(2)}) copy-start(f32[1,8,4096]{2,1,0:T(8,128)} %param.15) | copy-start | bytes 393220
  6.5 112.8 %all-gather.3.cloned.1.call-start = ((), (), s32[]{:S(2)}) async-start(), calls=%async_computation.3 | async-start | bytes 2359296 | tf_op jit(solution)/shard_map/all_gather | solution.py:179
  6.5 60.2 %collective-permute-start.3 = (bf16[4608,256]{1,0:T(8,128)(2,1)}, bf16[4608,256]{1,0:T(8,128)(2,1)}, u32[]{:S(2)}, u32[]{:S(2)}) collective-permute-start(bf16[4608,256]{1,0:T(8,128)(2,1)} %w0.3), channel_id=1, source_target_pairs={{0,2},{2,4},{4,6},{6,8},{8,10},{10,12},{12,14},{14,0},{1,15},{3,1}... | collective-permute-start | bytes 7077896 | tf_op jit(solution)/shard_map/ppermute | solution.py:30
  46.1 33.8 %copy-start.1 = (bf16[4608,256]{1,0:T(8,128)(2,1)S(1)}, bf16[4608,256]{1,0:T(8,128)(2,1)}, u32[]{:S(2)}) copy-start(bf16[4608,256]{1,0:T(8,128)(2,1)} %w0.3) | copy-start | bytes 7077892
  46.1 14.9 %collective-permute-start.8 = (f32[8,4096]{1,0:T(8,128)}, f32[8,4096]{1,0:T(8,128)S(1)}, u32[]{:S(2)}, u32[]{:S(2)}) collective-permute-start(f32[8,4096]{1,0:T(8,128)} %bitcast.32), channel_id=1, source_target_pairs={{0,32},{32,0},{1,33},{33,1},{2,34},{34,2},{3,35},{35,3},{4,36},{36... | collective-permute-start | bytes 393224 | tf_op jit(solution)/shard_map/ppermute | solution.py:178
  50.5 16.2 %collective-permute-start = (bf16[128,2432]{1,0:T(8,128)(2,1)}, bf16[128,2432]{1,0:T(8,128)(2,1)}, u32[]{:S(2)}, u32[]{:S(2)}) collective-permute-start(bf16[128,2432]{1,0:T(8,128)(2,1)} %bitcast.6.near_ref), channel_id=1, source_target_pairs={{0,16},{16,32},{32,48},{48,0},{1,49},{17,1},{33,17},{49,33},{2,18}... | collective-permute-start | bytes 1867784 | tf_op jit(solution)/shard_map/ppermute | solution.py:30
  52.7 14.0 %collective-permute-start.1 = (bf16[128,2432]{1,0:T(8,128)(2,1)}, bf16[128,2432]{1,0:T(8,128)(2,1)}, u32[]{:S(2)}, u32[]{:S(2)}) collective-permute-start(bf16[128,2432]{1,0:T(8,128)(2,1)} %bitcast.6.near_ref), channel_id=1, source_target_pairs={{0,64},{64,128},{128,192},{192,256},{256,320},{320,384},{384,448},... | collective-permute-start | bytes 1867784 | tf_op jit(solution)/shard_map/ppermute | solution.py:30
  58.1 21.8 %collective-permute-start.4 = (bf16[4608,256]{1,0:T(8,128)(2,1)}, bf16[4608,256]{1,0:T(8,128)(2,1)}, u32[]{:S(2)}, u32[]{:S(2)}) collective-permute-start(bf16[4608,256]{1,0:T(8,128)(2,1)} %w0.3), channel_id=1, source_target_pairs={{0,1},{1,0},{2,3},{3,2},{4,5},{5,4},{6,7},{7,6},{8,9},{9,8},{10,11... | collective-permute-start | bytes 7077896 | tf_op jit(solution)/shard_map/ppermute | solution.py:184
  61.0 5.7 %collective-permute-start.5 = (f32[256,64]{1,0:T(8,128)S(1)}, f32[256,64]{1,0:T(8,128)S(1)}, u32[]{:S(2)}, u32[]{:S(2)}) collective-permute-start(f32[256,64]{1,0:T(8,128)S(1)} %copy.22), channel_id=1, source_target_pairs={{0,2},{2,4},{4,6},{6,8},{8,10},{10,12},{12,14},{14,0},{1,15},{3,1}... | collective-permute-start | bytes 196616 | tf_op jit(solution)/shard_map/ppermute | solution.py:30
  66.7 13.1 %collective-permute-start.6 = (bf16[4608,256]{1,0:T(8,128)(2,1)}, bf16[4608,256]{1,0:T(8,128)(2,1)}, u32[]{:S(2)}, u32[]{:S(2)}) collective-permute-start(bf16[4608,256]{1,0:T(8,128)(2,1)} %collective-permute-done.3.w1), channel_id=1, source_target_pairs={{0,1},{1,0},{2,3},{3,2},{4,5},{5,4},{6,7},{7,6},{8,9},{9,8},{10,11... | collective-permute-start | bytes 7077896 | tf_op jit(solution)/shard_map/ppermute | solution.py:184
  73.2 11.6 %collective-permute-start.2 = (bf16[128,2432]{1,0:T(8,128)(2,1)}, bf16[128,2432]{1,0:T(8,128)(2,1)S(1)}, u32[]{:S(2)}, u32[]{:S(2)}) collective-permute-start(bf16[128,2432]{1,0:T(8,128)(2,1)} %collective-permute-done.1.far_ref), channel_id=1, source_target_pairs={{0,16},{16,32},{32,48},{48,0},{1,49},{17,1},{33,17},{49,33},{2,18}... | collective-permute-start | bytes 1867784 | tf_op jit(solution)/shard_map/ppermute | solution.py:30
  75.7 3.4 %collective-permute-start.7 = (f32[512,64]{1,0:T(8,128)S(1)}, f32[512,64]{1,0:T(8,128)S(1)}, u32[]{:S(2)}, u32[]{:S(2)}) collective-permute-start(f32[512,64]{1,0:T(8,128)S(1)} %pad_maximum_fusion), channel_id=1, source_target_pairs={{0,1},{1,0},{2,3},{3,2},{4,5},{5,4},{6,7},{7,6},{8,9},{9,8},{10,11... | collective-permute-start | bytes 393224 | tf_op jit(solution)/shard_map/ppermute | solution.py:185
  84.8 34.2 %copy-start.4 = (bf16[64,4608]{1,0:T(8,128)(2,1)S(1)}, bf16[64,4608]{1,0:T(8,128)(2,1)}, u32[]{:S(2)}) copy-start(bf16[64,4608]{1,0:T(8,128)(2,1)} %param.8) | copy-start | bytes 1769476
  90.6 38.8 %copy-start.3 = (f32[64,64]{1,0:T(8,128)S(1)}, f32[64,64]{1,0:T(8,128)}, u32[]{:S(2)}) copy-start(f32[64,64]{1,0:T(8,128)} %right_ref.1) | copy-start | bytes 49156
  110.9 18.5 %all-to-all-start.2 = ((f32[32,8,256]{2,1,0:T(8,128)}), f32[32,8,256]{2,1,0:T(8,128)S(1)}, u32[]{:S(2)}, u32[]{:S(2)}) async-start(f32[32,8,256]{2,1,0:T(8,128)} %shard_map.84), calls=%async_computation.2 | async-start | bytes 524288 | tf_op jit(solution)/shard_map/all_to_all | solution.py:20
  129.4 1.6 %copy-start.2 = (f32[16,8,4096]{2,1,0:T(8,128)S(1)}, f32[16,8,4096]{2,1,0:T(8,128)}, u32[]{:S(2)}) copy-start(f32[16,8,4096]{2,1,0:T(8,128)} %all-gather.3.cloned.1.call-done) | copy-start | bytes 6291460
Sparse Core Ops, SparseCore 0:
  65.0 34.5 all-gather.2

commit v4 on v3

--- a/solution.py
+++ b/solution.py
@@ -170,19 +170,21 @@
     digits = jnp.pad(digits, ((0, 0), (0, 125))).astype(jnp.bfloat16)
     chosen = jnp.concatenate([chosen, digits], axis=1)
     near = spread_out(chosen, ("zh", "xh"), 8).reshape(ROWS, 2432)
+
+    swapped = lax.ppermute(unembed, "core", SWAP)
+    tables = jnp.concatenate([out_proj, both_ways(out_proj, ("yh", "yl"), 8)], axis=0)
+    table = jnp.concatenate([tables, lax.ppermute(tables, "core", SWAP)], axis=0)
+    query_pair = jnp.stack([queries[0], lax.ppermute(queries[0], "xh", SWAP)])
+    near, swapped, table, query_pair = lax.optimization_barrier((near, swapped, table, query_pair))
+
     far = both_ways(near, ("zh", "zl"), 8)
     near_x = both_ways(near, ("xh", "xl"), 4)
     far_x = both_ways(far, ("xh", "xl"), 4)
-
-    late_query, _ = lax.optimization_barrier((queries[0], near))
-    query_pair = jnp.stack([late_query, lax.ppermute(late_query, "xh", SWAP)])
     every_query = lax.all_gather(query_pair, ("zh", "zl"), axis=0)
 
-    weights = [unembed, both_ways(unembed, ("yh", "yl"), 8)]
-    tables = jnp.concatenate([out_proj, both_ways(out_proj, ("yh", "yl"), 8)], axis=0)
-    late_weight, tables, _, _ = lax.optimization_barrier((weights[1], tables, far, near_x))
-    weights += [lax.ppermute(block, "core", SWAP) for block in (unembed, late_weight)]
-    table = jnp.concatenate([tables, lax.ppermute(tables, "core", SWAP)], axis=0)
+    moved = both_ways(unembed, ("yh", "yl"), 8)
+    late, _, _ = lax.optimization_barrier((moved, far, near_x))
+    weights = [unembed, moved, swapped, lax.ppermute(late, "core", SWAP)]
 
     def block_start(at_y, at_core):
         return (((z * 2 + xh) * 2 + xl) * 16 + at_y * 2 + at_core) * 256
@@ -206,6 +208,7 @@
     packed = last_products(jnp.stack([1 - xl, zl]), near_x, far_x, weights, begun, table, label_rows)
 
     parts = exchange(packed.reshape(32, 8, 256), ("zh", "zl", "xh", "xl"))
+    parts, every_query = lax.optimization_barrier((parts, every_query))
     merged = pl.pallas_call(
         merge_kernel,
         out_shape=jax.ShapeDtypeStruct((32, 8, 256), jnp.float32),

time: 140 us -> 142 us (1.014)
  blocking collectives: 50.1 us -> 18.4 us
  starting transfers between devices: 38.8 us -> 58.6 us
  waiting for transfers between devices: 13.2 us -> 25.8 us
  local copies, waits for them, and re-layouts: 6.75 us -> 4.61 us
  other arithmetic: 1.85 us -> 3.91 us
    all_to_all x2 -> x1, blocking collectives: 50.1 us -> 18.4 us  [exchange(): return lax.all_to_all(blocks, axes, split_axis=0, concat_axis=0, tiled=True)]
    ppermute x5, waiting for transfers between devices: 1.9 us -> 15.3 us  [both_ways(): return lax.ppermute(value, axes + ('core',), pairs)]
    all_to_all x1 -> x2, starting transfers between devices: 6.55 us -> 19.1 us  [exchange(): return lax.all_to_all(blocks, axes, split_axis=0, concat_axis=0, tiled=True)]
    ppermute x3, starting transfers between devices: 11.1 us -> 15.6 us  [the longest x1 8.91 us: local(): swapped = lax.ppermute(unembed, 'core', SWAP)]
    ppermute x1, starting transfers between devices: 1.92 us -> 3.88 us  [local(): lax.ppermute(tables, 'core', SWAP)]
    unnamed x15 -> x16, local copies, waits for them, and re-layouts: 2.66 us -> 1.21 us
    all_to_all x1 -> x2, waiting for transfers between devices: 9.97 us -> 10.4 us  [exchange(): return lax.all_to_all(blocks, axes, split_axis=0, concat_axis=0, tiled=True)]
  transfers between devices with their start and end apart: 11 -> 12, of which waited for: 4 -> 5; matrix products, arithmetic and copies ran while one was open for 6% -> 7% of each run, Pallas kernels for 9% -> 8%
where the time goes in v4:
time: 142 us; the launch traced here: 141 us
  starting transfers between devices  58.6 us (41%)
  waiting for transfers between devices  25.8 us (18%)
  blocking collectives  18.4 us (13%)
  Pallas kernels  14.2 us (10%)
  between operations  13.7 us (10%)
  local copies, waits for them, and re-layouts  4.61 us (3%)
  other arithmetic  3.91 us (3%)
  matrix products  2.02 us (1%)
    ppermute x5, starting transfers between devices, both_ways(): return lax.ppermute(value, axes + ('core',), pairs)  19.9 us
    all_to_all x2, starting transfers between devices, exchange(): return lax.all_to_all(blocks, axes, split_axis=0, concat_axis=0, tiled=True)  19.1 us
    all_to_all x1, blocking collectives, exchange(): return lax.all_to_all(blocks, axes, split_axis=0, concat_axis=0, tiled=True)  18.4 us
    ppermute x5, waiting for transfers between devices, both_ways(): return lax.ppermute(value, axes + ('core',), pairs)  15.3 us
    all_to_all x2, waiting for transfers between devices, exchange(): return lax.all_to_all(blocks, axes, split_axis=0, concat_axis=0, tiled=True)  10.4 us
    ppermute x1, starting transfers between devices, local(): swapped = lax.ppermute(unembed, 'core', SWAP)  8.91 us
    pallas_call x1, Pallas kernels, last_products(): pl.pallas_call(last_kernel, out_shape=jax.ShapeDtypeStruct((4, 2, 32, 256...  5.82 us
    ppermute x1, starting transfers between devices, local(): query_pair = jnp.stack([queries[0], lax.ppermute(queries[0], 'xh', SWAP)])  4.82 us
  transfers between devices with their start and end apart: 12, of which 5 were waited for; matrix products, arithmetic and copies ran while one was open for 7% of the time, Pallas kernels for 8%

profile of v4, /device:TPU:1, one launch (start us, length us, event | category | flops | bytes accessed | tf_op | source)
XLA Modules:
  0.0 141.2 jit_solution(11263716542138792831)
XLA Ops:
  6.5 8.9 %collective-permute-start = (bf16[4608,256]{1,0:T(8,128)(2,1)}, bf16[4608,256]{1,0:T(8,128)(2,1)}, u32[]{:S(2)}, u32[]{:S(2)}) collective-permute-start(bf16[4608,256]{1,0:T(8,128)(2,1)} %w0.3), channel_id=1, source_target_pairs={{0,1},{1,0},{2,3},{3,2},{4,5},{5,4},{6,7},{7,6},{8,9},{9,8},{10,11... | collective-permute-start | bytes 7077896 | tf_op jit(solution)/shard_map/ppermute | solution.py:174
  15.5 1.9 %collective-permute-start.7 = (bf16[4608,256]{1,0:T(8,128)(2,1)}, bf16[4608,256]{1,0:T(8,128)(2,1)}, u32[]{:S(2)}, u32[]{:S(2)}) collective-permute-start(bf16[4608,256]{1,0:T(8,128)(2,1)} %w0.3), channel_id=1, source_target_pairs={{0,2},{2,4},{4,6},{6,8},{8,10},{10,12},{12,14},{14,0},{1,15},{3,1}... | collective-permute-start | bytes 7077896 | tf_op jit(solution)/shard_map/ppermute | solution.py:30
  17.4 0.7 fusion.9
  18.2 0.1 copy.30
  18.3 0.9 dynamic_slice.6
  19.2 0.9 broadcast_in_dim.4
  20.1 10.3 %all-to-all-start = ((bf16[8,16,2432]{2,1,0:T(8,128)(2,1)}), bf16[8,16,2432]{2,1,0:T(8,128)(2,1)}, u32[]{:S(2)}, u32[]{:S(2)}) async-start(bf16[8,16,2432]{2,1,0:T(8,128)(2,1)} %broadcast_in_dim.4), calls=%async_computation | async-start | bytes 1245184 | tf_op jit(solution)/shard_map/all_to_all | solution.py:20
  30.3 0.0 all-gather.3.cloned.1.call-start
  30.4 1.1 copy.25
  31.5 0.0 copy-start.4
  31.5 3.0 %collective-permute-start.1 = (f32[256,64]{1,0:T(8,128)S(1)}, f32[256,64]{1,0:T(8,128)S(1)}, u32[]{:S(2)}, u32[]{:S(2)}) collective-permute-start(f32[256,64]{1,0:T(8,128)S(1)} %copy.25), channel_id=1, source_target_pairs={{0,2},{2,4},{4,6},{6,8},{8,10},{10,12},{12,14},{14,0},{1,15},{3,1}... | collective-permute-start | bytes 196616 | tf_op jit(solution)/shard_map/ppermute | solution.py:30
  34.5 4.8 %collective-permute-start.3 = (f32[8,4096]{1,0:T(8,128)}, f32[8,4096]{1,0:T(8,128)S(1)}, u32[]{:S(2)}, u32[]{:S(2)}) collective-permute-start(f32[8,4096]{1,0:T(8,128)} %bitcast.7), channel_id=1, source_target_pairs={{0,32},{32,0},{1,33},{33,1},{2,34},{34,2},{3,35},{35,3},{4,36},{36... | collective-permute-start | bytes 393224 | tf_op jit(solution)/shard_map/ppermute | solution.py:177
  39.3 7.8 %collective-permute-done.1 = f32[256,64]{1,0:T(8,128)S(1)} collective-permute-done((f32[256,64]{1,0:T(8,128)S(1)}, f32[256,64]{1,0:T(8,128)S(1)}, u32[]{:S(2)}, u32[]{:S(2)}) %collective-permute-start.1) | collective-permute-done | bytes 65568 | tf_op jit(solution)/shard_map/ppermute | solution.py:30
  47.1 3.9 %collective-permute-start.2 = (f32[512,64]{1,0:T(8,128)S(1)}, f32[512,64]{1,0:T(8,128)}, u32[]{:S(2)}, u32[]{:S(2)}) collective-permute-start(f32[512,64]{1,0:T(8,128)S(1)} %pad_maximum_fusion.1), channel_id=1, source_target_pairs={{0,1},{1,0},{2,3},{3,2},{4,5},{5,4},{6,7},{7,6},{8,9},{9,8},{10,11... | collective-permute-start | bytes 393224 | tf_op jit(solution)/shard_map/ppermute | solution.py:176
  51.0 0.0 collective-permute-done.3
  51.0 1.6 %pad_maximum_fusion.2 = f32[2,8,4096]{2,1,0:T(8,128)} fusion(f32[1,8,4096]{2,1,0:T(8,128)S(1)} %bitcast.32, f32[1,8,4096]{2,1,0:T(8,128)} %param.15), kind=kLoop, calls=%fused_computation.6 | loop fusion | flops 65536 | bytes 524288 | tf_op jit(solution)/shard_map/stack | solution.py:177
  52.6 0.0 collective-permute-done.2
  52.6 1.1 pad_maximum_fusion.table_ref
  53.7 0.0 all-to-all-done
  53.7 0.0 collective-permute-done.w2
  53.7 5.5 %collective-permute-start.5 = (bf16[128,2432]{1,0:T(8,128)(2,1)}, bf16[128,2432]{1,0:T(8,128)(2,1)}, u32[]{:S(2)}, u32[]{:S(2)}) collective-permute-start(bf16[128,2432]{1,0:T(8,128)(2,1)} %bitcast.6.near_ref), channel_id=1, source_target_pairs={{0,64},{64,128},{128,192},{192,256},{256,320},{320,384},{384,448},... | collective-permute-start | bytes 1867784 | tf_op jit(solution)/shard_map/ppermute | solution.py:30
  59.3 4.4 %collective-permute-start.4 = (bf16[128,2432]{1,0:T(8,128)(2,1)}, bf16[128,2432]{1,0:T(8,128)(2,1)}, u32[]{:S(2)}, u32[]{:S(2)}) collective-permute-start(bf16[128,2432]{1,0:T(8,128)(2,1)} %bitcast.6.near_ref), channel_id=1, source_target_pairs={{0,16},{16,32},{32,48},{48,0},{1,49},{17,1},{33,17},{49,33},{2,18}... | collective-permute-start | bytes 1867784 | tf_op jit(solution)/shard_map/ppermute | solution.py:30
  63.7 0.0 all-gather.3.cloned.1.call-update
  63.7 0.0 collective-permute-done.7.w1
  63.7 3.0 %collective-permute-done.5.far_ref = bf16[128,2432]{1,0:T(8,128)(2,1)} collective-permute-done((bf16[128,2432]{1,0:T(8,128)(2,1)}, bf16[128,2432]{1,0:T(8,128)(2,1)}, u32[]{:S(2)}, u32[]{:S(2)}) %collective-permute-start.5) | collective-permute-done | bytes 622624 | tf_op jit(solution)/shard_map/ppermute | solution.py:30
  66.8 4.4 %collective-permute-done.4.near_ref = bf16[128,2432]{1,0:T(8,128)(2,1)} collective-permute-done((bf16[128,2432]{1,0:T(8,128)(2,1)}, bf16[128,2432]{1,0:T(8,128)(2,1)}, u32[]{:S(2)}, u32[]{:S(2)}) %collective-permute-start.4) | collective-permute-done | bytes 622624 | tf_op jit(solution)/shard_map/ppermute | solution.py:30
  71.2 1.9 %collective-permute-start.8 = (bf16[4608,256]{1,0:T(8,128)(2,1)}, bf16[4608,256]{1,0:T(8,128)(2,1)}, u32[]{:S(2)}, u32[]{:S(2)}) collective-permute-start(bf16[4608,256]{1,0:T(8,128)(2,1)} %collective-permute-done.7.w1), channel_id=1, source_target_pairs={{0,1},{1,0},{2,3},{3,2},{4,5},{5,4},{6,7},{7,6},{8,9},{9,8},{10,11... | collective-permute-start | bytes 7077896 | tf_op jit(solution)/shard_map/ppermute | solution.py:187
  73.1 0.1 pad_add_fusion.2.where_ref
  73.2 5.0 %collective-permute-start.6 = (bf16[128,2432]{1,0:T(8,128)(2,1)}, bf16[128,2432]{1,0:T(8,128)(2,1)S(1)}, u32[]{:S(2)}, u32[]{:S(2)}) collective-permute-start(bf16[128,2432]{1,0:T(8,128)(2,1)} %collective-permute-done.5.far_ref), channel_id=1, source_target_pairs={{0,16},{16,32},{32,48},{48,0},{1,49},{17,1},{33,17},{49,33},{2,18}... | collective-permute-start | bytes 1867784 | tf_op jit(solution)/shard_map/ppermute | solution.py:30
  78.2 0.1 pad_add_fusion.1.where_ref
  78.3 0.8 slice.21
  79.1 0.8 slice.28
  79.9 0.2 fusion.5
  80.1 0.7 fusion.label_ref
  80.8 0.0 collective-permute-done.8.w3
  80.8 4.8 %shard_map.82.begun_ref = f32[256,1024]{1,0:T(8,128)S(1)} custom-call(s32[2]{0:T(128)S(1)} %pad_add_fusion.2.where_ref, bf16[128,2432]{1,0:T(8,128)(2,1)} %bitcast.6.near_ref, bf16[128,2432]{1,0:T(8,128)(2,1)} %collective-permute-done.5.far_ref, bf16[4608,256]{1,0:T(8,128)(2,1)S(1)} %copy-done.1, bf16[4608,256]{1,0:T(8,128)(2,1)} %collective-permute-done.7.w1, ...), custom_call_target="tpu_custom_call" | custom-call | flops 1207959552 | bytes 7000000 | tf_op jit(solution)/shard_map/pallas_call | solution.py:131
  85.6 0.0 copy-start.6
  85.6 0.1 collective-permute-done.6.far_ref
  85.7 5.8 %shard_map.83 = f32[4,2,32,256]{3,2,1,0:T(8,128)S(1)} custom-call(s32[2]{0:T(128)S(1)} %pad_add_fusion.1.where_ref, bf16[128,2432]{1,0:T(8,128)(2,1)} %collective-permute-done.4.near_ref, bf16[128,2432]{1,0:T(8,128)(2,1)S(1)} %collective-permute-done.6.far_ref, bf16[4608,256]{1,0:T(8,128)(2,1)S(1)} %copy-done.1, ...), custom_call_target="tpu_custom_call" | custom-call | flops 1207959552 | bytes 7000000 | tf_op jit(solution)/shard_map/pallas_call | solution.py:146
  91.5 0.0 copy-start.3
  91.6 18.4 %all_to_all.15.parts_ref = f32[32,8,256]{2,1,0:T(8,128)} all-to-all(f32[32,8,256]{2,1,0:T(8,128)S(1)} %bitcast.28), channel_id=1, replica_groups=mesh['zh'=4,'zl'=2,'xh'=2,'xl'=2,'yh'=4,'yl'=2,'core'=2] {'zh','zl','xh'..., dimensions={0} | all-to-all | bytes 524288 | tf_op jit(solution)/shard_map/all_to_all | solution.py:20
  109.9 2.0 %shard_map.84 = f32[32,8,256]{2,1,0:T(8,128)} custom-call(f32[32,8,256]{2,1,0:T(8,128)} %all_to_all.15.parts_ref), custom_call_target="tpu_custom_call" | custom-call | flops 300000 | bytes 600000 | tf_op jit(solution)/shard_map/pallas_call | solution.py:212
  111.9 8.9 %all-to-all-start.2 = ((f32[32,8,256]{2,1,0:T(8,128)}), f32[32,8,256]{2,1,0:T(8,128)S(1)}, u32[]{:S(2)}, u32[]{:S(2)}) async-start(f32[32,8,256]{2,1,0:T(8,128)} %shard_map.84), calls=%async_computation.2 | async-start | bytes 524288 | tf_op jit(solution)/shard_map/all_to_all | solution.py:20
  120.8 0.0 copy-done.6
  120.9 1.4 fusion.13
  122.2 0.1 copy.28.mapped_ref
  122.3 10.4 %all-to-all-done.2 = f32[32,8,256]{2,1,0:T(8,128)S(1)} async-done(((f32[32,8,256]{2,1,0:T(8,128)}), f32[32,8,256]{2,1,0:T(8,128)S(1)}, u32[]{:S(2)}, u32[]{:S(2)}) %all-to-all-start.2) | async-done | bytes 262176 | tf_op jit(solution)/shard_map/all_to_all | solution.py:20
  132.7 1.6 %shard_map.85 = f32[8,16]{1,0:T(8,128)} custom-call(s32[1]{0:T(128)} %bitcast.half_ref, f32[2,4,4,8,256]{4,3,2,1,0:T(8,128)S(1)} %bitcast.29, f32[64,64]{1,0:T(8,128)S(1)} %copy.28.mapped_ref, f32[32,64]{1,0:T(8,128)S(1)} %slice.26.even_ref, f32[32,64]{1,0:T(8,128)S(1)} %slice.27.odd_ref, f32[64,64]{1,0:T(8,128)S(1)} %copy-done.3, f32[128,4096]{1,0:T(8,128)S(1)} %bitcast.27), custom_call_target="tpu_custom_call" | custom-call | flops 2000000 | bytes 2500000 | tf_op jit(solution)/shard_map/pallas_call | solution.py:219
  (22 shorter events, 0.1 us)
Async XLA Ops:
  6.5 114.3 %copy-start = (bf16[4608,64]{0,1:T(8,128)(2,1)S(1)}, bf16[4608,64]{0,1:T(8,128)(2,1)}, u32[]{:S(2)}) copy-start(bf16[4608,64]{0,1:T(8,128)(2,1)} %param.11) | copy-start | bytes 1769476
  6.5 47.2 %collective-permute-start = (bf16[4608,256]{1,0:T(8,128)(2,1)}, bf16[4608,256]{1,0:T(8,128)(2,1)}, u32[]{:S(2)}, u32[]{:S(2)}) collective-permute-start(bf16[4608,256]{1,0:T(8,128)(2,1)} %w0.3), channel_id=1, source_target_pairs={{0,1},{1,0},{2,3},{3,2},{4,5},{5,4},{6,7},{7,6},{8,9},{9,8},{10,11... | collective-permute-start | bytes 7077896 | tf_op jit(solution)/shard_map/ppermute | solution.py:174
  15.5 48.3 %collective-permute-start.7 = (bf16[4608,256]{1,0:T(8,128)(2,1)}, bf16[4608,256]{1,0:T(8,128)(2,1)}, u32[]{:S(2)}, u32[]{:S(2)}) collective-permute-start(bf16[4608,256]{1,0:T(8,128)(2,1)} %w0.3), channel_id=1, source_target_pairs={{0,2},{2,4},{4,6},{6,8},{8,10},{10,12},{12,14},{14,0},{1,15},{3,1}... | collective-permute-start | bytes 7077896 | tf_op jit(solution)/shard_map/ppermute | solution.py:30
  20.1 33.7 %all-to-all-start = ((bf16[8,16,2432]{2,1,0:T(8,128)(2,1)}), bf16[8,16,2432]{2,1,0:T(8,128)(2,1)}, u32[]{:S(2)}, u32[]{:S(2)}) async-start(bf16[8,16,2432]{2,1,0:T(8,128)(2,1)} %broadcast_in_dim.4), calls=%async_computation | async-start | bytes 1245184 | tf_op jit(solution)/shard_map/all_to_all | solution.py:20
  30.3 50.4 %copy-start.1 = (bf16[4608,256]{1,0:T(8,128)(2,1)S(1)}, bf16[4608,256]{1,0:T(8,128)(2,1)}, u32[]{:S(2)}) copy-start(bf16[4608,256]{1,0:T(8,128)(2,1)} %w0.3) | copy-start | bytes 7077892
  30.3 79.6 %all-gather.3.cloned.1.call-start = ((), (), s32[]{:S(2)}) async-start(), calls=%async_computation.3 | async-start | bytes 2359296 | tf_op jit(solution)/shard_map/all_gather | solution.py:183
  31.5 21.1 %copy-start.4 = (f32[256,64]{1,0:T(8,128)}, f32[256,64]{1,0:T(8,128)S(1)}, u32[]{:S(2)}) copy-start(f32[256,64]{1,0:T(8,128)S(1)} %copy.25) | copy-start | bytes 196612
  31.5 15.6 %collective-permute-start.1 = (f32[256,64]{1,0:T(8,128)S(1)}, f32[256,64]{1,0:T(8,128)S(1)}, u32[]{:S(2)}, u32[]{:S(2)}) collective-permute-start(f32[256,64]{1,0:T(8,128)S(1)} %copy.25), channel_id=1, source_target_pairs={{0,2},{2,4},{4,6},{6,8},{8,10},{10,12},{12,14},{14,0},{1,15},{3,1}... | collective-permute-start | bytes 196616 | tf_op jit(solution)/shard_map/ppermute | solution.py:30
  34.5 16.5 %collective-permute-start.3 = (f32[8,4096]{1,0:T(8,128)}, f32[8,4096]{1,0:T(8,128)S(1)}, u32[]{:S(2)}, u32[]{:S(2)}) collective-permute-start(f32[8,4096]{1,0:T(8,128)} %bitcast.7), channel_id=1, source_target_pairs={{0,32},{32,0},{1,33},{33,1},{2,34},{34,2},{3,35},{35,3},{4,36},{36... | collective-permute-start | bytes 393224 | tf_op jit(solution)/shard_map/ppermute | solution.py:177
  47.1 5.6 %copy-start.5 = (f32[256,64]{1,0:T(8,128)}, f32[256,64]{1,0:T(8,128)S(1)}, u32[]{:S(2)}) copy-start(f32[256,64]{1,0:T(8,128)S(1)} %collective-permute-done.1) | copy-start | bytes 196612
  47.1 5.5 %collective-permute-start.2 = (f32[512,64]{1,0:T(8,128)S(1)}, f32[512,64]{1,0:T(8,128)}, u32[]{:S(2)}, u32[]{:S(2)}) collective-permute-start(f32[512,64]{1,0:T(8,128)S(1)} %pad_maximum_fusion.1), channel_id=1, source_target_pairs={{0,1},{1,0},{2,3},{3,2},{4,5},{5,4},{6,7},{7,6},{8,9},{9,8},{10,11... | collective-permute-start | bytes 393224 | tf_op jit(solution)/shard_map/ppermute | solution.py:176
  53.7 13.0 %collective-permute-start.5 = (bf16[128,2432]{1,0:T(8,128)(2,1)}, bf16[128,2432]{1,0:T(8,128)(2,1)}, u32[]{:S(2)}, u32[]{:S(2)}) collective-permute-start(bf16[128,2432]{1,0:T(8,128)(2,1)} %bitcast.6.near_ref), channel_id=1, source_target_pairs={{0,64},{64,128},{128,192},{192,256},{256,320},{320,384},{384,448},... | collective-permute-start | bytes 1867784 | tf_op jit(solution)/shard_map/ppermute | solution.py:30
  59.3 11.9 %collective-permute-start.4 = (bf16[128,2432]{1,0:T(8,128)(2,1)}, bf16[128,2432]{1,0:T(8,128)(2,1)}, u32[]{:S(2)}, u32[]{:S(2)}) collective-permute-start(bf16[128,2432]{1,0:T(8,128)(2,1)} %bitcast.6.near_ref), channel_id=1, source_target_pairs={{0,16},{16,32},{32,48},{48,0},{1,49},{17,1},{33,17},{49,33},{2,18}... | collective-permute-start | bytes 1867784 | tf_op jit(solution)/shard_map/ppermute | solution.py:30
  71.2 9.6 %collective-permute-start.8 = (bf16[4608,256]{1,0:T(8,128)(2,1)}, bf16[4608,256]{1,0:T(8,128)(2,1)}, u32[]{:S(2)}, u32[]{:S(2)}) collective-permute-start(bf16[4608,256]{1,0:T(8,128)(2,1)} %collective-permute-done.7.w1), channel_id=1, source_target_pairs={{0,1},{1,0},{2,3},{3,2},{4,5},{5,4},{6,7},{7,6},{8,9},{9,8},{10,11... | collective-permute-start | bytes 7077896 | tf_op jit(solution)/shard_map/ppermute | solution.py:187
  73.2 12.5 %collective-permute-start.6 = (bf16[128,2432]{1,0:T(8,128)(2,1)}, bf16[128,2432]{1,0:T(8,128)(2,1)S(1)}, u32[]{:S(2)}, u32[]{:S(2)}) collective-permute-start(bf16[128,2432]{1,0:T(8,128)(2,1)} %collective-permute-done.5.far_ref), channel_id=1, source_target_pairs={{0,16},{16,32},{32,48},{48,0},{1,49},{17,1},{33,17},{49,33},{2,18}... | collective-permute-start | bytes 1867784 | tf_op jit(solution)/shard_map/ppermute | solution.py:30
  85.6 35.2 %copy-start.6 = (f32[64,64]{1,0:T(8,128)S(1)}, f32[64,64]{1,0:T(8,128)}, u32[]{:S(2)}) copy-start(f32[64,64]{1,0:T(8,128)} %param.13) | copy-start | bytes 49156
  91.5 41.2 %copy-start.3 = (f32[64,64]{1,0:T(8,128)S(1)}, f32[64,64]{1,0:T(8,128)}, u32[]{:S(2)}) copy-start(f32[64,64]{1,0:T(8,128)} %right_ref.1) | copy-start | bytes 49156
  109.9 22.8 %copy-start.2 = (f32[16,8,4096]{2,1,0:T(8,128)S(1)}, f32[16,8,4096]{2,1,0:T(8,128)}, u32[]{:S(2)}) copy-start(f32[16,8,4096]{2,1,0:T(8,128)} %all-gather.3.cloned.1.call-done) | copy-start | bytes 6291460
  111.9 20.8 %all-to-all-start.2 = ((f32[32,8,256]{2,1,0:T(8,128)}), f32[32,8,256]{2,1,0:T(8,128)S(1)}, u32[]{:S(2)}, u32[]{:S(2)}) async-start(f32[32,8,256]{2,1,0:T(8,128)} %shard_map.84), calls=%async_computation.2 | async-start | bytes 524288 | tf_op jit(solution)/shard_map/all_to_all | solution.py:20
Sparse Core Ops, SparseCore 0:
  63.8 35.7 all-gather.2

commit v5 on v4

--- a/solution.py
+++ b/solution.py
@@ -30,31 +30,65 @@
     return lax.ppermute(value, axes + ("core",), pairs)
 
 
-def add_products(near_ref, far_ref, weight_refs, acc_ref):
+def diagonal(value):
+    pairs = []
+    for z in range(8):
+        for x in range(4):
+            for core, by in ((0, 1), (1, -1)):
+                to = (z + by) % 8 * 4 + (x + by) % 4
+                pairs.append(((z * 4 + x) * 2 + core, to * 2 + core))
+    return lax.ppermute(value, ("zh", "zl", "xh", "xl", "core"), pairs)
+
+
+def add_products(near_ref, far_ref, weight_refs, acc_ref, first_column=0):
     for block, weight in enumerate(weight_refs):
-        columns = pl.ds(256 * block, 256)
+        columns = pl.ds(first_column + 256 * block, 256)
         for start, rows in ((0, near_ref), (ROWS, far_ref)):
             acc_ref[pl.ds(start, ROWS), columns] += jnp.dot(
                 rows[...], weight[...], preferred_element_type=jnp.float32
             )
 
 
-def first_kernel(where_ref, near_ref, far_ref, w0, w1, w2, w3, acc_ref):
+def times_block(values, block_ref):
+    parts = block_ref[...].astype(jnp.float32)
+    table = parts[0:64] + parts[64:128] + parts[128:192]
+    return lax.dot_general(
+        values, table, (((1,), (1,)), ((), ())), precision=PRECISE, preferred_element_type=jnp.float32
+    )
+
+
+def label_rows_of(near_digits, far_digits, starts, tables):
+    digits = jnp.concatenate([near_digits[...], far_digits[...]], axis=0).astype(jnp.float32)
+    labels = digits[:, 0:1] * 65536.0 + digits[:, 1:2] * 256.0 + digits[:, 2:3]
+    ids = lax.broadcasted_iota(jnp.int32, (2 * ROWS, 256), 1)
+    rows = jnp.zeros((2 * ROWS, 64), jnp.float32)
+    for start, table in zip(starts, tables):
+        columns = (ids + start).astype(jnp.float32)
+        rows += times_block(jnp.where(labels == columns, 1.0, 0.0), table)
+    return rows
+
+
+def first_kernel(where_ref, near_ref, far_ref, w0, w1, w2, near_digits, far_digits, t0, t1, t2, acc_ref, label_ref):
     @pl.when(pl.program_id(0) == 0)
     def _():
         acc_ref[...] = jnp.zeros_like(acc_ref)
-
-    add_products(near_ref, far_ref, (w0, w1, w2, w3), acc_ref)
-
-
-def last_kernel(where_ref, near_ref, far_ref, w0, w1, w2, w3, begun_ref, table_ref, label_ref, out_ref, acc_ref):
+        label_ref[...] = label_rows_of(near_digits, far_digits, [where_ref[3 + i] for i in range(3)], (t0, t1, t2))
+
+    add_products(near_ref, far_ref, (w0, w1, w2), acc_ref)
+
+
+def last_kernel(
+    where_ref, near_ref, far_ref, w0, w1, w2, w3, near3_ref, far3_ref, own3_ref, near_digits, far_digits, t0, t1, t2, t3, begun_ref, label_ref, out_ref, acc_ref
+):
     step = pl.program_id(0)
 
     @pl.when(step == 0)
     def _():
-        acc_ref[...] = begun_ref[...]
+        acc_ref[:, 0:768] = begun_ref[...]
+        acc_ref[:, 768:1024] = jnp.zeros((2 * ROWS, 256), jnp.float32)
 
     add_products(near_ref, far_ref, (w0, w1, w2, w3), acc_ref)
+    add_products(near3_ref, far3_ref, (own3_ref,), acc_ref, 768)
 
     @pl.when(step == STEPS - 1)
     def _():
@@ -62,8 +96,11 @@
         largest = jnp.max(logits, axis=1, keepdims=True)
         exponent = jnp.exp(logits - largest)
         totals = jnp.sum(exponent, axis=1, keepdims=True)
-        sums = jnp.dot(exponent, table_ref[...], precision=PRECISE, preferred_element_type=jnp.float32)
-        left = jnp.concatenate([sums, label_ref[...]], axis=1)
+        sums = jnp.zeros((2 * ROWS, 64), jnp.float32)
+        for block, table in enumerate((t0, t1, t2, t3)):
+            sums += times_block(exponent[:, 256 * block : 256 * block + 256], table)
+        label_rows = label_ref[...] + label_rows_of(near_digits, far_digits, [where_ref[6]], [t3])
+        left = jnp.concatenate([sums, label_rows], axis=1)
         lane = lax.broadcasted_iota(jnp.int32, (2 * ROWS, 128), 1)
         right = jnp.where(lane == 0, largest, jnp.where(lane == 1, totals, 0.0))
         parity = where_ref[1]
@@ -87,7 +124,7 @@
     out_ref[:, :, 128:256] = jnp.broadcast_to(right, (32, 8, 128))
 
 
-def end_kernel(half_ref, parts_ref, mapped_ref, even_ref, odd_ref, right_ref, queries_ref, out_ref):
+def end_kernel(parts_ref, mapped_ref, even_ref, odd_ref, right_ref, queries_ref, out_ref):
     def precise(first, second):
         return jnp.dot(first, second, precision=PRECISE, preferred_element_type=jnp.float32)
 
@@ -108,16 +145,21 @@
     lane = lax.broadcasted_iota(jnp.int32, (8, 16), 1)
     scores = jnp.zeros((8, 16), jnp.float32)
     for block in range(16):
-        group = block // 2 * 2 + jnp.where(half_ref[0] == 0, block % 2, 1 - block % 2)
         column = jnp.sum(products[8 * block : 8 * block + 8], axis=1, keepdims=True)
-        scores = jnp.where(lane == group, column, scores)
+        scores = jnp.where(lane == block, column, scores)
     out_ref[...] = scores
 
 
-def product_specs():
+def product_specs(blocks, half=0):
     rows = pl.BlockSpec((ROWS, DEPTH), lambda step, where: (0, step))
-    weight = pl.BlockSpec((DEPTH, 256), lambda step, where: (where[0] * STEPS + step, 0))
-    return [rows, rows] + [weight] * 4
+    weight = pl.BlockSpec((DEPTH, 256), lambda step, where: (where[half] * STEPS + step, 0))
+    return [rows, rows] + [weight] * blocks
+
+
+def side_specs(blocks):
+    digits = pl.BlockSpec((ROWS, 128), lambda step, where: (0, 18))
+    table = pl.BlockSpec((192, 256), lambda step, where: (24, 0))
+    return [digits, digits] + [table] * blocks
 
 
 def whole(shape):
@@ -130,32 +172,35 @@
 def first_products(where, near, far, weights):
     return pl.pallas_call(
         first_kernel,
-        out_shape=jax.ShapeDtypeStruct((256, 1024), jnp.float32),
+        out_shape=(jax.ShapeDtypeStruct((256, 768), jnp.float32), jax.ShapeDtypeStruct((256, 64), jnp.float32)),
         grid_spec=pltpu.PrefetchScalarGridSpec(
             num_scalar_prefetch=1,
             grid=(STEPS,),
-            in_specs=product_specs(),
-            out_specs=whole((256, 1024)),
+            in_specs=product_specs(3, 2) + side_specs(3),
+            out_specs=(whole((256, 768)), whole((256, 64))),
         ),
         compiler_params=pltpu.CompilerParams(vmem_limit_bytes=24 << 20),
         cost_estimate=pl.CostEstimate(transcendentals=0, **COST),
-    )(where, near, far, *weights)
-
-
-def last_products(where, near, far, weights, begun, table, label_rows):
+    )(where, near, far, *weights, near, far, *weights)
+
+
+def last_products(where, near_x, far_x, weights, near, far, begun, label_rows):
     return pl.pallas_call(
         last_kernel,
         out_shape=jax.ShapeDtypeStruct((4, 2, 32, 256), jnp.float32),
         grid_spec=pltpu.PrefetchScalarGridSpec(
             num_scalar_prefetch=1,
             grid=(STEPS,),
-            in_specs=product_specs() + [whole((256, 1024)), whole((1024, 64)), whole((256, 64))],
+            in_specs=product_specs(4)
+            + product_specs(1, 2)
+            + side_specs(4)
+            + [whole((256, 768)), whole((256, 64))],
             out_specs=whole((4, 2, 32, 256)),
             scratch_shapes=[pltpu.VMEM((256, 1024), jnp.float32)],
         ),
         compiler_params=pltpu.CompilerParams(vmem_limit_bytes=24 << 20),
         cost_estimate=pl.CostEstimate(transcendentals=256 * 1024, **COST),
-    )(where, near, far, *weights, begun, table, label_rows)
+    )(where, near_x, far_x, *weights, near, far, weights[3], near, far, *weights, begun, label_rows)
 
 
 def local(hidden, labels, unembed, in_proj, out_proj, left_inv, right_inv, queries):
@@ -171,44 +216,37 @@
     chosen = jnp.concatenate([chosen, digits], axis=1)
     near = spread_out(chosen, ("zh", "xh"), 8).reshape(ROWS, 2432)
 
-    swapped = lax.ppermute(unembed, "core", SWAP)
-    tables = jnp.concatenate([out_proj, both_ways(out_proj, ("yh", "yl"), 8)], axis=0)
-    table = jnp.concatenate([tables, lax.ppermute(tables, "core", SWAP)], axis=0)
-    query_pair = jnp.stack([queries[0], lax.ppermute(queries[0], "xh", SWAP)])
-    near, swapped, table, query_pair = lax.optimization_barrier((near, swapped, table, query_pair))
-
+    table = out_proj.T
+    high = lax.reduce_precision(table, 8, 7)
+    middle = lax.reduce_precision(table - high, 8, 7)
+    parts = [part.astype(jnp.bfloat16) for part in (high, middle, table - high - middle)]
+    block = jnp.concatenate([unembed] + parts, axis=0)
+
+    query_pair = lax.all_gather(queries[0], "xh", axis=0)
+    near, query_pair = lax.optimization_barrier((near, query_pair))
     far = both_ways(near, ("zh", "zl"), 8)
     near_x = both_ways(near, ("xh", "xl"), 4)
-    far_x = both_ways(far, ("xh", "xl"), 4)
+    far_x = diagonal(near)
+    moved = both_ways(block, ("yh", "yl"), 8)
     every_query = lax.all_gather(query_pair, ("zh", "zl"), axis=0)
-
-    moved = both_ways(unembed, ("yh", "yl"), 8)
+    swapped = lax.ppermute(block, "core", SWAP)
     late, _, _ = lax.optimization_barrier((moved, far, near_x))
-    weights = [unembed, moved, swapped, lax.ppermute(late, "core", SWAP)]
-
-    def block_start(at_y, at_core):
-        return (((z * 2 + xh) * 2 + xl) * 16 + at_y * 2 + at_core) * 256
-
-    below, above = (y + 7) % 8, (y + 1) % 8
-    starts = [
-        block_start(y, core),
-        block_start(jnp.where(core == 0, below, above), core),
-        block_start(y, 1 - core),
-        block_start(jnp.where(core == 0, above, below), 1 - core),
+    weights = [block, moved, swapped, lax.ppermute(late, "core", SWAP)]
+
+    below, above = ((y + 7) % 8) * 2, ((y + 1) % 8) * 2 + 1
+    places = [
+        2 * y + core,
+        jnp.where(core == 0, below, above),
+        2 * y + 1 - core,
+        jnp.where(core == 0, above, below),
     ]
-    ids = lax.iota(jnp.int32, 256)
-    column_ids = jnp.concatenate([start + ids for start in starts])
-    digits = jnp.concatenate([near[:, 2304:], far[:, 2304:]], axis=0).astype(jnp.int32)
-    every_label = digits[:, 0:1] * 65536 + digits[:, 1:2] * 256 + digits[:, 2:3]
-    mask = (every_label == column_ids[None, :]).astype(jnp.float32)
-    label_rows = jnp.dot(mask, table, precision=PRECISE)
+    starts = [(((z * 2 + xh) * 2 + xl) * 16 + place) * 256 for place in places]
+    where = jnp.stack([1 - xl, zl, xl] + starts)
     mapped = jnp.dot(hidden, in_proj, preferred_element_type=jnp.float32)
 
-    begun = first_products(jnp.stack([xl, zl]), near, far, weights)
-    packed = last_products(jnp.stack([1 - xl, zl]), near_x, far_x, weights, begun, table, label_rows)
-
+    begun, label_rows = first_products(where, near, far, weights[:3])
+    packed = last_products(where, near_x, far_x, weights, near, far, begun, label_rows)
     parts = exchange(packed.reshape(32, 8, 256), ("zh", "zl", "xh", "xl"))
-    parts, every_query = lax.optimization_barrier((parts, every_query))
     merged = pl.pallas_call(
         merge_kernel,
         out_shape=jax.ShapeDtypeStruct((32, 8, 256), jnp.float32),
@@ -219,10 +257,10 @@
     scores = pl.pallas_call(
         end_kernel,
         out_shape=jax.ShapeDtypeStruct((8, 16), jnp.float32),
-        in_specs=[pl.BlockSpec(memory_space=pltpu.SMEM)] + [pl.BlockSpec(memory_space=pltpu.VMEM)] * 6,
+        in_specs=[pl.BlockSpec(memory_space=pltpu.VMEM)] * 6,
         cost_estimate=pl.CostEstimate(flops=2_000_000, bytes_accessed=2_500_000, transcendentals=256),
         compiler_params=pltpu.CompilerParams(vmem_limit_bytes=24 << 20),
-    )(xh.reshape(1), parts, mapped, left_inv[0::2], left_inv[1::2], right_inv, every_query.reshape(128, 4096))
+    )(parts, mapped, left_inv[0::2], left_inv[1::2], right_inv, every_query.reshape(128, 4096))
     return scores.T[None]
 
 

time: 142 us -> 150 us (1.056)
  waiting for transfers between devices: 25.8 us -> 44 us
  starting transfers between devices: 58.6 us -> 41.3 us
  blocking collectives: 18.4 us -> 26.5 us
  Pallas kernels: 14.2 us -> 15.8 us
    ppermute x4 -> x3, waiting for transfers between devices: 0.01 us -> 14.9 us  [the longest x1 14.9 us: diagonal(): return lax.ppermute(value, ('zh', 'zl', 'xh', 'xl', 'core'), pairs)]
    all_to_all x2, waiting for transfers between devices: 10.4 us -> 21.7 us  [exchange(): return lax.all_to_all(blocks, axes, split_axis=0, concat_axis=0, tiled=True)]
    ppermute x4 -> x3, starting transfers between devices: 19.5 us -> 10 us  [the longest x1 4.1 us: diagonal(): return lax.ppermute(value, ('zh', 'zl', 'xh', 'xl', 'core'), pairs)]
    all_gather x0 -> x1, blocking collectives: none -> 8.92 us  [local(): query_pair = lax.all_gather(queries[0], 'xh', axis=0)]
    ppermute x5 -> x3, waiting for transfers between devices: 15.3 us -> 7.36 us  [both_ways(): return lax.ppermute(value, axes + ('core',), pairs)]
    ppermute x5 -> x3, starting transfers between devices: 19.9 us -> 12.1 us  [both_ways(): return lax.ppermute(value, axes + ('core',), pairs)]
    another operation x3 -> x0, other arithmetic: 1.78 us -> none  [the longest x1 1.63 us: local(): query_pair = jnp.stack([queries[0], lax.ppermute(queries[0], 'xh', SWAP)])]
    slice x2 -> x0, local copies, waits for them, and re-layouts: 1.52 us -> none  [the longest x1 0.76 us: local(): near[:, 2304:]]
  transfers between devices with their start and end apart: 12 -> 9, of which waited for: 5 -> 5; matrix products, arithmetic and copies ran while one was open for 7% -> 2% of each run, Pallas kernels for 8% -> 10%
where the time goes in v5:
time: 150 us; the launch traced here: 149 us
  waiting for transfers between devices  44 us (29%)
  starting transfers between devices  41.3 us (28%)
  blocking collectives  26.5 us (18%)
  Pallas kernels  15.8 us (11%)
  between operations  13.6 us (9%)
  local copies, waits for them, and re-layouts  3.68 us (2%)
  other arithmetic  2.94 us (2%)
    all_to_all x2, waiting for transfers between devices, exchange(): return lax.all_to_all(blocks, axes, split_axis=0, concat_axis=0, tiled=True)  21.7 us
    all_to_all x2, starting transfers between devices, exchange(): return lax.all_to_all(blocks, axes, split_axis=0, concat_axis=0, tiled=True)  19.1 us
    all_to_all x1, blocking collectives, exchange(): return lax.all_to_all(blocks, axes, split_axis=0, concat_axis=0, tiled=True)  17.6 us
    ppermute x1, waiting for transfers between devices, diagonal(): return lax.ppermute(value, ('zh', 'zl', 'xh', 'xl', 'core'), pairs)  14.9 us
    ppermute x3, starting transfers between devices, both_ways(): return lax.ppermute(value, axes + ('core',), pairs)  12.1 us
    all_gather x1, blocking collectives, local(): query_pair = lax.all_gather(queries[0], 'xh', axis=0)  8.92 us
    ppermute x3, waiting for transfers between devices, both_ways(): return lax.ppermute(value, axes + ('core',), pairs)  7.36 us
    pallas_call x1, Pallas kernels, last_products(): pl.pallas_call(last_kernel, out_shape=jax.ShapeDtypeStruct((4, 2, 32, 256...  7.04 us
  transfers between devices with their start and end apart: 9, of which 5 were waited for; matrix products, arithmetic and copies ran while one was open for 2% of the time, Pallas kernels for 10%

profile of v5, /device:TPU:1, one launch (start us, length us, event | category | flops | bytes accessed | tf_op | source)
XLA Modules:
  0.0 149.2 jit_solution(9767443435179330047)
XLA Ops:
  6.5 0.0 copy-start
  6.5 0.9 reduce-precision_convert_fusion.1
  7.5 0.0 copy-start.5
  7.5 0.0 copy-start.3
  7.5 1.9 %pad_maximum_fusion.w0.t0 = bf16[4800,256]{1,0:T(8,128)(2,1)S(1)} fusion(bf16[64,256]{1,0:T(8,128)(2,1)S(1)} %get-tuple-element.18, bf16[64,256]{1,0:T(8,128)(2,1)S(1)} %get-tuple-element.19, bf16[64,256]{1,0:T(8,128)(2,1)S(1)} %get-tuple-element.17, bf16[4608,256]{1,0:T(8,128)(2,1)} %param.10), kind=kLoop, calls=%fused_computation | loop fusion | flops 9830400 | bytes 4915200 | tf_op jit(solution)/shard_map/concatenate | solution.py:223
  9.4 5.9 %collective-permute-start.2 = (bf16[4800,256]{1,0:T(8,128)(2,1)S(1)}, bf16[4800,256]{1,0:T(8,128)(2,1)}, u32[]{:S(2)}, u32[]{:S(2)}) collective-permute-start(bf16[4800,256]{1,0:T(8,128)(2,1)S(1)} %pad_maximum_fusion.w0.t0), channel_id=1, source_target_pairs={{0,2},{2,4},{4,6},{6,8},{8,10},{10,12},{12,14},{14,0},{1,15},{3,1}... | collective-permute-start | bytes 7372808 | tf_op jit(solution)/shard_map/ppermute | solution.py:30
  15.3 0.0 copy-done.5
  15.3 0.1 fusion.4
  15.5 0.1 copy.17
  15.6 0.9 dynamic_slice.6
  16.5 0.9 broadcast_in_dim.4
  17.3 12.5 %all-to-all-start = ((bf16[8,16,2432]{2,1,0:T(8,128)(2,1)}), bf16[8,16,2432]{2,1,0:T(8,128)(2,1)}, u32[]{:S(2)}, u32[]{:S(2)}) async-start(bf16[8,16,2432]{2,1,0:T(8,128)(2,1)} %broadcast_in_dim.4), calls=%async_computation | async-start | bytes 1245184 | tf_op jit(solution)/shard_map/all_to_all | solution.py:20
  29.8 0.0 all-gather.3.cloned.1.call-start
  29.9 0.0 copy-done.3
  29.9 8.9 %all_gather.9 = f32[2,8,4096]{2,1,0:T(8,128)} all-gather(f32[1,8,4096]{2,1,0:T(8,128)S(1)} %copy-done.3), channel_id=1, replica_groups=mesh['zh'=4,'zl'=2,'xh'=2,'xl'=2,'yh'=4,'yl'=2,'core'=2] {'xh'}, dimensions={0}, use_global_device_ids=true | all-gather | bytes 393216 | tf_op jit(solution)/shard_map/all_gather | solution.py:225
  38.8 11.3 %all-to-all-done = bf16[8,16,2432]{2,1,0:T(8,128)(2,1)} async-done(((bf16[8,16,2432]{2,1,0:T(8,128)(2,1)}), bf16[8,16,2432]{2,1,0:T(8,128)(2,1)}, u32[]{:S(2)}, u32[]{:S(2)}) %all-to-all-start) | async-done | bytes 622624 | tf_op jit(solution)/shard_map/all_to_all | solution.py:20
  50.1 4.2 %collective-permute-start.4 = (bf16[128,2432]{1,0:T(8,128)(2,1)}, bf16[128,2432]{1,0:T(8,128)(2,1)}, u32[]{:S(2)}, u32[]{:S(2)}) collective-permute-start(bf16[128,2432]{1,0:T(8,128)(2,1)} %bitcast.10.near_ref.near_digits.near3_ref), channel_id=1, source_target_pairs={{0,64},{64,128},{128,192},{192,256},{256,320},{320,384},{384,448},... | collective-permute-start | bytes 1867784 | tf_op jit(solution)/shard_map/ppermute | solution.py:30
  54.3 2.0 %collective-permute-start = (bf16[128,2432]{1,0:T(8,128)(2,1)}, bf16[128,2432]{1,0:T(8,128)(2,1)}, u32[]{:S(2)}, u32[]{:S(2)}) collective-permute-start(bf16[128,2432]{1,0:T(8,128)(2,1)} %bitcast.10.near_ref.near_digits.near3_ref), channel_id=1, source_target_pairs={{0,16},{16,32},{32,48},{48,0},{1,49},{17,1},{33,17},{49,33},{2,18}... | collective-permute-start | bytes 1867784 | tf_op jit(solution)/shard_map/ppermute | solution.py:30
  56.3 2.2 %collective-permute-start.3 = (bf16[4800,256]{1,0:T(8,128)(2,1)S(1)}, bf16[4800,256]{1,0:T(8,128)(2,1)}, u32[]{:S(2)}, u32[]{:S(2)}) collective-permute-start(bf16[4800,256]{1,0:T(8,128)(2,1)S(1)} %pad_maximum_fusion.w0.t0), channel_id=1, source_target_pairs={{0,1},{1,0},{2,3},{3,2},{4,5},{5,4},{6,7},{7,6},{8,9},{9,8},{10,11... | collective-permute-start | bytes 7372808 | tf_op jit(solution)/shard_map/ppermute | solution.py:232
  58.5 0.0 all-gather.3.cloned.1.call-update
  58.5 3.2 %collective-permute-done.4.far_ref.far_digits.far3_ref = bf16[128,2432]{1,0:T(8,128)(2,1)} collective-permute-done((bf16[128,2432]{1,0:T(8,128)(2,1)}, bf16[128,2432]{1,0:T(8,128)(2,1)}, u32[]{:S(2)}, u32[]{:S(2)}) %collective-permute-start.4) | collective-permute-done | bytes 622624 | tf_op jit(solution)/shard_map/ppermute | solution.py:30
  61.7 4.1 %collective-permute-done.near_ref = bf16[128,2432]{1,0:T(8,128)(2,1)} collective-permute-done((bf16[128,2432]{1,0:T(8,128)(2,1)}, bf16[128,2432]{1,0:T(8,128)(2,1)}, u32[]{:S(2)}, u32[]{:S(2)}) %collective-permute-start) | collective-permute-done | bytes 622624 | tf_op jit(solution)/shard_map/ppermute | solution.py:30
  65.9 0.0 collective-permute-done.2.w1.t1
  65.9 3.7 %collective-permute-start.5 = (bf16[4800,256]{1,0:T(8,128)(2,1)}, bf16[4800,256]{1,0:T(8,128)(2,1)}, u32[]{:S(2)}, u32[]{:S(2)}) collective-permute-start(bf16[4800,256]{1,0:T(8,128)(2,1)} %collective-permute-done.2.w1.t1), channel_id=1, source_target_pairs={{0,1},{1,0},{2,3},{3,2},{4,5},{5,4},{6,7},{7,6},{8,9},{9,8},{10,11... | collective-permute-start | bytes 7372808 | tf_op jit(solution)/shard_map/ppermute | solution.py:234
  69.6 4.1 %collective-permute-start.1 = (bf16[128,2432]{1,0:T(8,128)(2,1)}, bf16[128,2432]{1,0:T(8,128)(2,1)}, u32[]{:S(2)}, u32[]{:S(2)}) collective-permute-start(bf16[128,2432]{1,0:T(8,128)(2,1)} %bitcast.10.near_ref.near_digits.near3_ref), channel_id=1, source_target_pairs={{0,80},{1,497},{16,96},{17,449},{32,112},{33,465},{48,64},{49,481}... | collective-permute-start | bytes 1867784 | tf_op jit(solution)/shard_map/ppermute | solution.py:40
  73.8 0.1 stack.47.where_ref
  73.9 0.0 collective-permute-done.3.w2.t2
  73.9 5.3 %shard_map.82 = (f32[256,768]{1,0:T(8,128)S(1)}, f32[256,64]{1,0:T(8,128)S(1)}) custom-call(s32[7]{0:T(128)S(1)} %stack.47.where_ref, bf16[128,2432]{1,0:T(8,128)(2,1)} %bitcast.10.near_ref.near_digits.near3_ref, bf16[128,2432]{1,0:T(8,128)(2,1)} %collective-permute-done.4.far_ref.far_digits.far3_ref, bf16[4800,256]{1,0:T(8,128)(2,1)S(1)} %pad_maximum_fusion.w0.t0, ...), custom_call_target="tpu_custom_call" | custom-call | flops 1207959552 | bytes 7000000 | tf_op jit(solution)/shard_map/pallas_call | solution.py:173
  79.2 14.9 %collective-permute-done.1.far_ref = bf16[128,2432]{1,0:T(8,128)(2,1)} collective-permute-done((bf16[128,2432]{1,0:T(8,128)(2,1)}, bf16[128,2432]{1,0:T(8,128)(2,1)}, u32[]{:S(2)}, u32[]{:S(2)}) %collective-permute-start.1) | collective-permute-done | bytes 622624 | tf_op jit(solution)/shard_map/ppermute | solution.py:40
  94.1 0.0 collective-permute-done.5.w3.own3_ref.t3
  94.1 0.0 copy-start.4
  94.1 7.0 %shard_map.83 = f32[4,2,32,256]{3,2,1,0:T(8,128)S(1)} custom-call(s32[7]{0:T(128)S(1)} %stack.47.where_ref, bf16[128,2432]{1,0:T(8,128)(2,1)} %collective-permute-done.near_ref, bf16[128,2432]{1,0:T(8,128)(2,1)} %collective-permute-done.1.far_ref, bf16[4800,256]{1,0:T(8,128)(2,1)S(1)} %pad_maximum_fusion.w0.t0, ...), custom_call_target="tpu_custom_call" | custom-call | flops 1207959552 | bytes 7000000 | tf_op jit(solution)/shard_map/pallas_call | solution.py:188
  101.1 0.0 copy-start.2
  101.1 17.6 %all_to_all.15.parts_ref = f32[32,8,256]{2,1,0:T(8,128)} all-to-all(f32[32,8,256]{2,1,0:T(8,128)S(1)} %bitcast.34), channel_id=1, replica_groups=mesh['zh'=4,'zl'=2,'xh'=2,'xl'=2,'yh'=4,'yl'=2,'core'=2] {'zh','zl','xh'..., dimensions={0} | all-to-all | bytes 524288 | tf_op jit(solution)/shard_map/all_to_all | solution.py:20
  118.7 1.9 %shard_map.84 = f32[32,8,256]{2,1,0:T(8,128)} custom-call(f32[32,8,256]{2,1,0:T(8,128)} %all_to_all.15.parts_ref), custom_call_target="tpu_custom_call" | custom-call | flops 300000 | bytes 600000 | tf_op jit(solution)/shard_map/pallas_call | solution.py:250
  120.6 6.6 %all-to-all-start.2 = ((f32[32,8,256]{2,1,0:T(8,128)}), f32[32,8,256]{2,1,0:T(8,128)S(1)}, u32[]{:S(2)}, u32[]{:S(2)}) async-start(f32[32,8,256]{2,1,0:T(8,128)} %shard_map.84), calls=%async_computation.2 | async-start | bytes 524288 | tf_op jit(solution)/shard_map/all_to_all | solution.py:20
  127.2 0.0 copy-done.4
  127.2 0.0 copy-done
  127.2 1.4 fusion.8
  128.6 0.1 copy.16.mapped_ref
  128.7 0.0 all-gather.3.cloned.1.call-done
  128.7 10.4 %all-to-all-done.2 = f32[32,8,256]{2,1,0:T(8,128)S(1)} async-done(((f32[32,8,256]{2,1,0:T(8,128)}), f32[32,8,256]{2,1,0:T(8,128)S(1)}, u32[]{:S(2)}, u32[]{:S(2)}) %all-to-all-start.2) | async-done | bytes 262176 | tf_op jit(solution)/shard_map/all_to_all | solution.py:20
  139.1 0.0 copy-done.2
  139.1 0.0 copy-start.1
  139.1 1.6 %copy-done.1 = f32[16,8,4096]{2,1,0:T(8,128)S(1)} copy-done((f32[16,8,4096]{2,1,0:T(8,128)S(1)}, f32[16,8,4096]{2,1,0:T(8,128)}, u32[]{:S(2)}) %copy-start.1) | copy-done | bytes 2097176
  140.7 1.6 %shard_map.85 = f32[8,16]{1,0:T(8,128)} custom-call(f32[2,4,4,8,256]{4,3,2,1,0:T(8,128)S(1)} %bitcast.35, f32[64,64]{1,0:T(8,128)S(1)} %copy.16.mapped_ref, f32[32,64]{1,0:T(8,128)S(1)} %slice.6.even_ref, f32[32,64]{1,0:T(8,128)S(1)} %slice.7.odd_ref, f32[64,64]{1,0:T(8,128)S(1)} %copy-done.2, f32[128,4096]{1,0:T(8,128)S(1)} %bitcast.33), custom_call_target="tpu_custom_call" | custom-call | flops 2000000 | bytes 2500000 | tf_op jit(solution)/shard_map/pallas_call | solution.py:257
  (6 shorter events, 0.1 us)
Async XLA Ops:
  6.5 120.7 %copy-start = (bf16[4608,64]{0,1:T(8,128)(2,1)S(1)}, bf16[4608,64]{0,1:T(8,128)(2,1)}, u32[]{:S(2)}) copy-start(bf16[4608,64]{0,1:T(8,128)(2,1)} %param.11) | copy-start | bytes 1769476
  7.5 7.9 %copy-start.5 = (s32[64]{0:T(128)S(1)}, s32[64]{0:T(128)}, u32[]{:S(2)}) copy-start(s32[64]{0:T(128)} %param.9) | copy-start | bytes 772
  7.5 22.4 %copy-start.3 = (f32[1,8,4096]{2,1,0:T(8,128)S(1)}, f32[1,8,4096]{2,1,0:T(8,128)}, u32[]{:S(2)}) copy-start(f32[1,8,4096]{2,1,0:T(8,128)} %param.15) | copy-start | bytes 393220
  9.4 56.5 %collective-permute-start.2 = (bf16[4800,256]{1,0:T(8,128)(2,1)S(1)}, bf16[4800,256]{1,0:T(8,128)(2,1)}, u32[]{:S(2)}, u32[]{:S(2)}) collective-permute-start(bf16[4800,256]{1,0:T(8,128)(2,1)S(1)} %pad_maximum_fusion.w0.t0), channel_id=1, source_target_pairs={{0,2},{2,4},{4,6},{6,8},{8,10},{10,12},{12,14},{14,0},{1,15},{3,1}... | collective-permute-start | bytes 7372808 | tf_op jit(solution)/shard_map/ppermute | solution.py:30
  17.3 32.7 %all-to-all-start = ((bf16[8,16,2432]{2,1,0:T(8,128)(2,1)}), bf16[8,16,2432]{2,1,0:T(8,128)(2,1)}, u32[]{:S(2)}, u32[]{:S(2)}) async-start(bf16[8,16,2432]{2,1,0:T(8,128)(2,1)} %broadcast_in_dim.4), calls=%async_computation | async-start | bytes 1245184 | tf_op jit(solution)/shard_map/all_to_all | solution.py:20
  29.8 98.9 %all-gather.3.cloned.1.call-start = ((), (), s32[]{:S(2)}) async-start(), calls=%async_computation.3 | async-start | bytes 2359296 | tf_op jit(solution)/shard_map/all_gather | solution.py:231
  50.1 11.6 %collective-permute-start.4 = (bf16[128,2432]{1,0:T(8,128)(2,1)}, bf16[128,2432]{1,0:T(8,128)(2,1)}, u32[]{:S(2)}, u32[]{:S(2)}) collective-permute-start(bf16[128,2432]{1,0:T(8,128)(2,1)} %bitcast.10.near_ref.near_digits.near3_ref), channel_id=1, source_target_pairs={{0,64},{64,128},{128,192},{192,256},{256,320},{320,384},{384,448},... | collective-permute-start | bytes 1867784 | tf_op jit(solution)/shard_map/ppermute | solution.py:30
  54.3 11.6 %collective-permute-start = (bf16[128,2432]{1,0:T(8,128)(2,1)}, bf16[128,2432]{1,0:T(8,128)(2,1)}, u32[]{:S(2)}, u32[]{:S(2)}) collective-permute-start(bf16[128,2432]{1,0:T(8,128)(2,1)} %bitcast.10.near_ref.near_digits.near3_ref), channel_id=1, source_target_pairs={{0,16},{16,32},{32,48},{48,0},{1,49},{17,1},{33,17},{49,33},{2,18}... | collective-permute-start | bytes 1867784 | tf_op jit(solution)/shard_map/ppermute | solution.py:30
  56.3 17.6 %collective-permute-start.3 = (bf16[4800,256]{1,0:T(8,128)(2,1)S(1)}, bf16[4800,256]{1,0:T(8,128)(2,1)}, u32[]{:S(2)}, u32[]{:S(2)}) collective-permute-start(bf16[4800,256]{1,0:T(8,128)(2,1)S(1)} %pad_maximum_fusion.w0.t0), channel_id=1, source_target_pairs={{0,1},{1,0},{2,3},{3,2},{4,5},{5,4},{6,7},{7,6},{8,9},{9,8},{10,11... | collective-permute-start | bytes 7372808 | tf_op jit(solution)/shard_map/ppermute | solution.py:232
  65.9 28.2 %collective-permute-start.5 = (bf16[4800,256]{1,0:T(8,128)(2,1)}, bf16[4800,256]{1,0:T(8,128)(2,1)}, u32[]{:S(2)}, u32[]{:S(2)}) collective-permute-start(bf16[4800,256]{1,0:T(8,128)(2,1)} %collective-permute-done.2.w1.t1), channel_id=1, source_target_pairs={{0,1},{1,0},{2,3},{3,2},{4,5},{5,4},{6,7},{7,6},{8,9},{9,8},{10,11... | collective-permute-start | bytes 7372808 | tf_op jit(solution)/shard_map/ppermute | solution.py:234
  69.6 24.5 %collective-permute-start.1 = (bf16[128,2432]{1,0:T(8,128)(2,1)}, bf16[128,2432]{1,0:T(8,128)(2,1)}, u32[]{:S(2)}, u32[]{:S(2)}) collective-permute-start(bf16[128,2432]{1,0:T(8,128)(2,1)} %bitcast.10.near_ref.near_digits.near3_ref), channel_id=1, source_target_pairs={{0,80},{1,497},{16,96},{17,449},{32,112},{33,465},{48,64},{49,481}... | collective-permute-start | bytes 1867784 | tf_op jit(solution)/shard_map/ppermute | solution.py:40
  94.1 33.1 %copy-start.4 = (f32[64,64]{1,0:T(8,128)S(1)}, f32[64,64]{1,0:T(8,128)}, u32[]{:S(2)}) copy-start(f32[64,64]{1,0:T(8,128)} %param.13) | copy-start | bytes 49156
  101.1 38.0 %copy-start.2 = (f32[64,64]{1,0:T(8,128)S(1)}, f32[64,64]{1,0:T(8,128)}, u32[]{:S(2)}) copy-start(f32[64,64]{1,0:T(8,128)} %right_ref.1) | copy-start | bytes 49156
  120.6 18.5 %all-to-all-start.2 = ((f32[32,8,256]{2,1,0:T(8,128)}), f32[32,8,256]{2,1,0:T(8,128)S(1)}, u32[]{:S(2)}, u32[]{:S(2)}) async-start(f32[32,8,256]{2,1,0:T(8,128)} %shard_map.84), calls=%async_computation.2 | async-start | bytes 524288 | tf_op jit(solution)/shard_map/all_to_all | solution.py:20
  139.1 1.6 %copy-start.1 = (f32[16,8,4096]{2,1,0:T(8,128)S(1)}, f32[16,8,4096]{2,1,0:T(8,128)}, u32[]{:S(2)}) copy-start(f32[16,8,4096]{2,1,0:T(8,128)} %all-gather.3.cloned.1.call-done) | copy-start | bytes 6291460
Sparse Core Ops, SparseCore 0:
  58.6 40.0 all-gather.2

commit v6 on v5

--- a/solution.py
+++ b/solution.py
@@ -28,16 +28,6 @@
     pairs = [(2 * i, 2 * ((i + 1) % count)) for i in range(count)]
     pairs += [(2 * i + 1, 2 * ((i - 1) % count) + 1) for i in range(count)]
     return lax.ppermute(value, axes + ("core",), pairs)
-
-
-def diagonal(value):
-    pairs = []
-    for z in range(8):
-        for x in range(4):
-            for core, by in ((0, 1), (1, -1)):
-                to = (z + by) % 8 * 4 + (x + by) % 4
-                pairs.append(((z * 4 + x) * 2 + core, to * 2 + core))
-    return lax.ppermute(value, ("zh", "zl", "xh", "xl", "core"), pairs)
 
 
 def add_products(near_ref, far_ref, weight_refs, acc_ref, first_column=0):
@@ -226,11 +216,11 @@
     near, query_pair = lax.optimization_barrier((near, query_pair))
     far = both_ways(near, ("zh", "zl"), 8)
     near_x = both_ways(near, ("xh", "xl"), 4)
-    far_x = diagonal(near)
+    far_x = both_ways(far, ("xh", "xl"), 4)
     moved = both_ways(block, ("yh", "yl"), 8)
     every_query = lax.all_gather(query_pair, ("zh", "zl"), axis=0)
     swapped = lax.ppermute(block, "core", SWAP)
-    late, _, _ = lax.optimization_barrier((moved, far, near_x))
+    late, _ = lax.optimization_barrier((moved, far))
     weights = [block, moved, swapped, lax.ppermute(late, "core", SWAP)]
 
     below, above = ((y + 7) % 8) * 2, ((y + 1) % 8) * 2 + 1
@@ -252,6 +242,7 @@
         out_shape=jax.ShapeDtypeStruct((32, 8, 256), jnp.float32),
         cost_estimate=pl.CostEstimate(flops=300_000, bytes_accessed=600_000, transcendentals=256),
     )(parts)
+    merged, every_query = lax.optimization_barrier((merged, every_query))
     parts = exchange(merged, VOC).reshape(2, 4, 4, 8, 256)
     mapped = jnp.transpose(mapped.reshape(4, 2, 8, 64), (3, 1, 0, 2)).reshape(64, 64)
     scores = pl.pallas_call(

time: 150 us -> 139 us (0.927)
  waiting for transfers between devices: 44 us -> 34 us
    ppermute x1 -> x0, waiting for transfers between devices: 14.9 us -> none  [diagonal(): return lax.ppermute(value, ('zh', 'zl', 'xh', 'xl', 'core'), pairs)]
    ppermute x3 -> x4, waiting for transfers between devices: 7.36 us -> 12.2 us  [both_ways(): return lax.ppermute(value, axes + ('core',), pairs)]
    ppermute x3 -> x4, starting transfers between devices: 12.1 us -> 16.8 us  [both_ways(): return lax.ppermute(value, axes + ('core',), pairs)]
    ppermute x1 -> x0, starting transfers between devices: 4.1 us -> none  [diagonal(): return lax.ppermute(value, ('zh', 'zl', 'xh', 'xl', 'core'), pairs)]
  transfers between devices with their start and end apart: 9 -> 9, of which waited for: 5 -> 4; matrix products, arithmetic and copies ran while one was open for 2% -> 3% of each run, Pallas kernels for 10% -> 10%
where the time goes in v6:
time: 139 us; the launch traced here: 138 us
  starting transfers between devices  41.5 us (30%)
  waiting for transfers between devices  34 us (24%)
  blocking collectives  25.2 us (18%)
  Pallas kernels  15.8 us (11%)
  between operations  13.6 us (10%)
  local copies, waits for them, and re-layouts  3.68 us (3%)
  other arithmetic  2.94 us (2%)
    all_to_all x2, waiting for transfers between devices, exchange(): return lax.all_to_all(blocks, axes, split_axis=0, concat_axis=0, tiled=True)  21.7 us
    all_to_all x2, starting transfers between devices, exchange(): return lax.all_to_all(blocks, axes, split_axis=0, concat_axis=0, tiled=True)  18.9 us
    ppermute x4, starting transfers between devices, both_ways(): return lax.ppermute(value, axes + ('core',), pairs)  16.8 us
    all_to_all x1, blocking collectives, exchange(): return lax.all_to_all(blocks, axes, split_axis=0, concat_axis=0, tiled=True)  16.2 us
    ppermute x4, waiting for transfers between devices, both_ways(): return lax.ppermute(value, axes + ('core',), pairs)  12.2 us
    all_gather x1, blocking collectives, local(): query_pair = lax.all_gather(queries[0], 'xh', axis=0)  8.92 us
    pallas_call x1, Pallas kernels, last_products(): pl.pallas_call(last_kernel, out_shape=jax.ShapeDtypeStruct((4, 2, 32, 256...  7 us
    pallas_call x1, Pallas kernels, first_products(): pl.pallas_call(first_kernel, out_shape=(jax.ShapeDtypeStruct((256, 768),...  5.33 us
  transfers between devices with their start and end apart: 9, of which 4 were waited for; matrix products, arithmetic and copies ran while one was open for 3% of the time, Pallas kernels for 10%

profile of v6, /device:TPU:1, one launch (start us, length us, event | category | flops | bytes accessed | tf_op | source)
XLA Modules:
  0.0 138.0 jit_solution(9953724520731377346)
XLA Ops:
  6.5 0.0 copy-start
  6.5 0.9 reduce-precision_convert_fusion.1
  7.5 0.0 copy-start.5
  7.5 0.0 copy-start.3
  7.5 1.9 %pad_maximum_fusion.w0.t0 = bf16[4800,256]{1,0:T(8,128)(2,1)S(1)} fusion(bf16[64,256]{1,0:T(8,128)(2,1)S(1)} %get-tuple-element.22, bf16[64,256]{1,0:T(8,128)(2,1)S(1)} %get-tuple-element.23, bf16[64,256]{1,0:T(8,128)(2,1)S(1)} %get-tuple-element.21, bf16[4608,256]{1,0:T(8,128)(2,1)} %param.10), kind=kLoop, calls=%fused_computation | loop fusion | flops 9830400 | bytes 4915200 | tf_op jit(solution)/shard_map/concatenate | solution.py:213
  9.4 5.9 %collective-permute-start.3 = (bf16[4800,256]{1,0:T(8,128)(2,1)S(1)}, bf16[4800,256]{1,0:T(8,128)(2,1)}, u32[]{:S(2)}, u32[]{:S(2)}) collective-permute-start(bf16[4800,256]{1,0:T(8,128)(2,1)S(1)} %pad_maximum_fusion.w0.t0), channel_id=1, source_target_pairs={{0,2},{2,4},{4,6},{6,8},{8,10},{10,12},{12,14},{14,0},{1,15},{3,1}... | collective-permute-start | bytes 7372808 | tf_op jit(solution)/shard_map/ppermute | solution.py:30
  15.3 0.0 copy-done.5
  15.3 0.1 fusion.4
  15.5 0.1 copy.17
  15.6 0.9 dynamic_slice.6
  16.5 0.9 broadcast_in_dim.4
  17.3 12.5 %all-to-all-start = ((bf16[8,16,2432]{2,1,0:T(8,128)(2,1)}), bf16[8,16,2432]{2,1,0:T(8,128)(2,1)}, u32[]{:S(2)}, u32[]{:S(2)}) async-start(bf16[8,16,2432]{2,1,0:T(8,128)(2,1)} %broadcast_in_dim.4), calls=%async_computation | async-start | bytes 1245184 | tf_op jit(solution)/shard_map/all_to_all | solution.py:20
  29.8 0.0 all-gather.3.cloned.1.call-start
  29.9 0.0 copy-done.3
  29.9 8.9 %all_gather.9 = f32[2,8,4096]{2,1,0:T(8,128)} all-gather(f32[1,8,4096]{2,1,0:T(8,128)S(1)} %copy-done.3), channel_id=1, replica_groups=mesh['zh'=4,'zl'=2,'xh'=2,'xl'=2,'yh'=4,'yl'=2,'core'=2] {'xh'}, dimensions={0}, use_global_device_ids=true | all-gather | bytes 393216 | tf_op jit(solution)/shard_map/all_gather | solution.py:215
  38.8 11.3 %all-to-all-done = bf16[8,16,2432]{2,1,0:T(8,128)(2,1)} async-done(((bf16[8,16,2432]{2,1,0:T(8,128)(2,1)}), bf16[8,16,2432]{2,1,0:T(8,128)(2,1)}, u32[]{:S(2)}, u32[]{:S(2)}) %all-to-all-start) | async-done | bytes 622624 | tf_op jit(solution)/shard_map/all_to_all | solution.py:20
  50.1 4.2 %collective-permute-start.1 = (bf16[128,2432]{1,0:T(8,128)(2,1)}, bf16[128,2432]{1,0:T(8,128)(2,1)}, u32[]{:S(2)}, u32[]{:S(2)}) collective-permute-start(bf16[128,2432]{1,0:T(8,128)(2,1)} %bitcast.10.near_ref.near_digits.near3_ref), channel_id=1, source_target_pairs={{0,64},{64,128},{128,192},{192,256},{256,320},{320,384},{384,448},... | collective-permute-start | bytes 1867784 | tf_op jit(solution)/shard_map/ppermute | solution.py:30
  54.3 0.0 all-gather.3.cloned.1.call-update
  54.3 1.9 %collective-permute-start.4 = (bf16[4800,256]{1,0:T(8,128)(2,1)S(1)}, bf16[4800,256]{1,0:T(8,128)(2,1)}, u32[]{:S(2)}, u32[]{:S(2)}) collective-permute-start(bf16[4800,256]{1,0:T(8,128)(2,1)S(1)} %pad_maximum_fusion.w0.t0), channel_id=1, source_target_pairs={{0,1},{1,0},{2,3},{3,2},{4,5},{5,4},{6,7},{7,6},{8,9},{9,8},{10,11... | collective-permute-start | bytes 7372808 | tf_op jit(solution)/shard_map/ppermute | solution.py:222
  56.2 6.0 %collective-permute-done.1.far_ref.far_digits.far3_ref = bf16[128,2432]{1,0:T(8,128)(2,1)} collective-permute-done((bf16[128,2432]{1,0:T(8,128)(2,1)}, bf16[128,2432]{1,0:T(8,128)(2,1)}, u32[]{:S(2)}, u32[]{:S(2)}) %collective-permute-start.1) | collective-permute-done | bytes 622624 | tf_op jit(solution)/shard_map/ppermute | solution.py:30
  62.3 0.0 collective-permute-done.3.w1.t1
  62.3 3.8 %collective-permute-start.5 = (bf16[4800,256]{1,0:T(8,128)(2,1)}, bf16[4800,256]{1,0:T(8,128)(2,1)}, u32[]{:S(2)}, u32[]{:S(2)}) collective-permute-start(bf16[4800,256]{1,0:T(8,128)(2,1)} %collective-permute-done.3.w1.t1), channel_id=1, source_target_pairs={{0,1},{1,0},{2,3},{3,2},{4,5},{5,4},{6,7},{7,6},{8,9},{9,8},{10,11... | collective-permute-start | bytes 7372808 | tf_op jit(solution)/shard_map/ppermute | solution.py:224
  66.0 4.3 %collective-permute-start = (bf16[128,2432]{1,0:T(8,128)(2,1)}, bf16[128,2432]{1,0:T(8,128)(2,1)}, u32[]{:S(2)}, u32[]{:S(2)}) collective-permute-start(bf16[128,2432]{1,0:T(8,128)(2,1)} %bitcast.10.near_ref.near_digits.near3_ref), channel_id=1, source_target_pairs={{0,16},{16,32},{32,48},{48,0},{1,49},{17,1},{33,17},{49,33},{2,18}... | collective-permute-start | bytes 1867784 | tf_op jit(solution)/shard_map/ppermute | solution.py:30
  70.3 2.5 %collective-permute-start.2 = (bf16[128,2432]{1,0:T(8,128)(2,1)}, bf16[128,2432]{1,0:T(8,128)(2,1)}, u32[]{:S(2)}, u32[]{:S(2)}) collective-permute-start(bf16[128,2432]{1,0:T(8,128)(2,1)} %collective-permute-done.1.far_ref.far_digits.far3_ref), channel_id=1, source_target_pairs={{0,16},{16,32},{32,48},{48,0},{1,49},{17,1},{33,17},{49,33},{2,18}... | collective-permute-start | bytes 1867784 | tf_op jit(solution)/shard_map/ppermute | solution.py:30
  72.9 0.1 stack.47.where_ref
  72.9 0.0 collective-permute-done.4.w2.t2
  72.9 5.3 %shard_map.82 = (f32[256,768]{1,0:T(8,128)S(1)}, f32[256,64]{1,0:T(8,128)S(1)}) custom-call(s32[7]{0:T(128)S(1)} %stack.47.where_ref, bf16[128,2432]{1,0:T(8,128)(2,1)} %bitcast.10.near_ref.near_digits.near3_ref, bf16[128,2432]{1,0:T(8,128)(2,1)} %collective-permute-done.1.far_ref.far_digits.far3_ref, bf16[4800,256]{1,0:T(8,128)(2,1)S(1)} %pad_maximum_fusion.w0.t0, ...), custom_call_target="tpu_custom_call" | custom-call | flops 1207959552 | bytes 7000000 | tf_op jit(solution)/shard_map/pallas_call | solution.py:163
  78.3 0.0 collective-permute-done.near_ref
  78.3 6.2 %collective-permute-done.2.far_ref = bf16[128,2432]{1,0:T(8,128)(2,1)} collective-permute-done((bf16[128,2432]{1,0:T(8,128)(2,1)}, bf16[128,2432]{1,0:T(8,128)(2,1)}, u32[]{:S(2)}, u32[]{:S(2)}) %collective-permute-start.2) | collective-permute-done | bytes 622624 | tf_op jit(solution)/shard_map/ppermute | solution.py:30
  84.5 0.0 collective-permute-done.5.w3.own3_ref.t3
  84.5 0.0 copy-start.4
  84.5 7.0 %shard_map.83 = f32[4,2,32,256]{3,2,1,0:T(8,128)S(1)} custom-call(s32[7]{0:T(128)S(1)} %stack.47.where_ref, bf16[128,2432]{1,0:T(8,128)(2,1)} %collective-permute-done.near_ref, bf16[128,2432]{1,0:T(8,128)(2,1)} %collective-permute-done.2.far_ref, bf16[4800,256]{1,0:T(8,128)(2,1)S(1)} %pad_maximum_fusion.w0.t0, ...), custom_call_target="tpu_custom_call" | custom-call | flops 1207959552 | bytes 7000000 | tf_op jit(solution)/shard_map/pallas_call | solution.py:178
  91.5 0.0 copy-start.2
  91.5 16.2 %all_to_all.15.parts_ref = f32[32,8,256]{2,1,0:T(8,128)} all-to-all(f32[32,8,256]{2,1,0:T(8,128)S(1)} %bitcast.35), channel_id=1, replica_groups=mesh['zh'=4,'zl'=2,'xh'=2,'xl'=2,'yh'=4,'yl'=2,'core'=2] {'zh','zl','xh'..., dimensions={0} | all-to-all | bytes 524288 | tf_op jit(solution)/shard_map/all_to_all | solution.py:20
  107.7 1.9 %shard_map.84 = f32[32,8,256]{2,1,0:T(8,128)} custom-call(f32[32,8,256]{2,1,0:T(8,128)} %all_to_all.15.parts_ref), custom_call_target="tpu_custom_call" | custom-call | flops 300000 | bytes 600000 | tf_op jit(solution)/shard_map/pallas_call | solution.py:240
  109.6 0.0 all-gather.3.cloned.1.call-done
  109.6 6.4 %all-to-all-start.2 = ((f32[32,8,256]{2,1,0:T(8,128)}), f32[32,8,256]{2,1,0:T(8,128)S(1)}, u32[]{:S(2)}, u32[]{:S(2)}) async-start(f32[32,8,256]{2,1,0:T(8,128)} %shard_map.84), calls=%async_computation.2 | async-start | bytes 524288 | tf_op jit(solution)/shard_map/all_to_all | solution.py:20
  116.0 0.0 copy-done.4
  116.1 0.0 copy-done
  116.1 1.4 fusion.8
  117.4 0.1 copy.16.mapped_ref
  117.5 10.4 %all-to-all-done.2 = f32[32,8,256]{2,1,0:T(8,128)S(1)} async-done(((f32[32,8,256]{2,1,0:T(8,128)}), f32[32,8,256]{2,1,0:T(8,128)S(1)}, u32[]{:S(2)}, u32[]{:S(2)}) %all-to-all-start.2) | async-done | bytes 262176 | tf_op jit(solution)/shard_map/all_to_all | solution.py:20
  127.9 0.0 copy-done.2
  127.9 0.0 copy-start.1
  127.9 1.6 %copy-done.1 = f32[16,8,4096]{2,1,0:T(8,128)S(1)} copy-done((f32[16,8,4096]{2,1,0:T(8,128)S(1)}, f32[16,8,4096]{2,1,0:T(8,128)}, u32[]{:S(2)}) %copy-start.1) | copy-done | bytes 2097176
  129.5 1.6 %shard_map.85 = f32[8,16]{1,0:T(8,128)} custom-call(f32[2,4,4,8,256]{4,3,2,1,0:T(8,128)S(1)} %bitcast.36, f32[64,64]{1,0:T(8,128)S(1)} %copy.16.mapped_ref, f32[32,64]{1,0:T(8,128)S(1)} %slice.6.even_ref, f32[32,64]{1,0:T(8,128)S(1)} %slice.7.odd_ref, f32[64,64]{1,0:T(8,128)S(1)} %copy-done.2, f32[128,4096]{1,0:T(8,128)S(1)} %bitcast.34), custom_call_target="tpu_custom_call" | custom-call | flops 2000000 | bytes 2500000 | tf_op jit(solution)/shard_map/pallas_call | solution.py:248
  (6 shorter events, 0.1 us)
Async XLA Ops:
  6.5 109.5 %copy-start = (bf16[4608,64]{0,1:T(8,128)(2,1)S(1)}, bf16[4608,64]{0,1:T(8,128)(2,1)}, u32[]{:S(2)}) copy-start(bf16[4608,64]{0,1:T(8,128)(2,1)} %param.11) | copy-start | bytes 1769476
  7.5 7.9 %copy-start.5 = (s32[64]{0:T(128)S(1)}, s32[64]{0:T(128)}, u32[]{:S(2)}) copy-start(s32[64]{0:T(128)} %param.9) | copy-start | bytes 772
  7.5 22.4 %copy-start.3 = (f32[1,8,4096]{2,1,0:T(8,128)S(1)}, f32[1,8,4096]{2,1,0:T(8,128)}, u32[]{:S(2)}) copy-start(f32[1,8,4096]{2,1,0:T(8,128)} %param.15) | copy-start | bytes 393220
  9.4 52.9 %collective-permute-start.3 = (bf16[4800,256]{1,0:T(8,128)(2,1)S(1)}, bf16[4800,256]{1,0:T(8,128)(2,1)}, u32[]{:S(2)}, u32[]{:S(2)}) collective-permute-start(bf16[4800,256]{1,0:T(8,128)(2,1)S(1)} %pad_maximum_fusion.w0.t0), channel_id=1, source_target_pairs={{0,2},{2,4},{4,6},{6,8},{8,10},{10,12},{12,14},{14,0},{1,15},{3,1}... | collective-permute-start | bytes 7372808 | tf_op jit(solution)/shard_map/ppermute | solution.py:30
  17.3 32.7 %all-to-all-start = ((bf16[8,16,2432]{2,1,0:T(8,128)(2,1)}), bf16[8,16,2432]{2,1,0:T(8,128)(2,1)}, u32[]{:S(2)}, u32[]{:S(2)}) async-start(bf16[8,16,2432]{2,1,0:T(8,128)(2,1)} %broadcast_in_dim.4), calls=%async_computation | async-start | bytes 1245184 | tf_op jit(solution)/shard_map/all_to_all | solution.py:20
  29.8 79.8 %all-gather.3.cloned.1.call-start = ((), (), s32[]{:S(2)}) async-start(), calls=%async_computation.3 | async-start | bytes 2359296 | tf_op jit(solution)/shard_map/all_gather | solution.py:221
  50.1 12.2 %collective-permute-start.1 = (bf16[128,2432]{1,0:T(8,128)(2,1)}, bf16[128,2432]{1,0:T(8,128)(2,1)}, u32[]{:S(2)}, u32[]{:S(2)}) collective-permute-start(bf16[128,2432]{1,0:T(8,128)(2,1)} %bitcast.10.near_ref.near_digits.near3_ref), channel_id=1, source_target_pairs={{0,64},{64,128},{128,192},{192,256},{256,320},{320,384},{384,448},... | collective-permute-start | bytes 1867784 | tf_op jit(solution)/shard_map/ppermute | solution.py:30
  54.3 18.7 %collective-permute-start.4 = (bf16[4800,256]{1,0:T(8,128)(2,1)S(1)}, bf16[4800,256]{1,0:T(8,128)(2,1)}, u32[]{:S(2)}, u32[]{:S(2)}) collective-permute-start(bf16[4800,256]{1,0:T(8,128)(2,1)S(1)} %pad_maximum_fusion.w0.t0), channel_id=1, source_target_pairs={{0,1},{1,0},{2,3},{3,2},{4,5},{5,4},{6,7},{7,6},{8,9},{9,8},{10,11... | collective-permute-start | bytes 7372808 | tf_op jit(solution)/shard_map/ppermute | solution.py:222
  62.3 22.2 %collective-permute-start.5 = (bf16[4800,256]{1,0:T(8,128)(2,1)}, bf16[4800,256]{1,0:T(8,128)(2,1)}, u32[]{:S(2)}, u32[]{:S(2)}) collective-permute-start(bf16[4800,256]{1,0:T(8,128)(2,1)} %collective-permute-done.3.w1.t1), channel_id=1, source_target_pairs={{0,1},{1,0},{2,3},{3,2},{4,5},{5,4},{6,7},{7,6},{8,9},{9,8},{10,11... | collective-permute-start | bytes 7372808 | tf_op jit(solution)/shard_map/ppermute | solution.py:224
  66.0 12.3 %collective-permute-start = (bf16[128,2432]{1,0:T(8,128)(2,1)}, bf16[128,2432]{1,0:T(8,128)(2,1)}, u32[]{:S(2)}, u32[]{:S(2)}) collective-permute-start(bf16[128,2432]{1,0:T(8,128)(2,1)} %bitcast.10.near_ref.near_digits.near3_ref), channel_id=1, source_target_pairs={{0,16},{16,32},{32,48},{48,0},{1,49},{17,1},{33,17},{49,33},{2,18}... | collective-permute-start | bytes 1867784 | tf_op jit(solution)/shard_map/ppermute | solution.py:30
  70.3 14.1 %collective-permute-start.2 = (bf16[128,2432]{1,0:T(8,128)(2,1)}, bf16[128,2432]{1,0:T(8,128)(2,1)}, u32[]{:S(2)}, u32[]{:S(2)}) collective-permute-start(bf16[128,2432]{1,0:T(8,128)(2,1)} %collective-permute-done.1.far_ref.far_digits.far3_ref), channel_id=1, source_target_pairs={{0,16},{16,32},{32,48},{48,0},{1,49},{17,1},{33,17},{49,33},{2,18}... | collective-permute-start | bytes 1867784 | tf_op jit(solution)/shard_map/ppermute | solution.py:30
  84.5 31.5 %copy-start.4 = (f32[64,64]{1,0:T(8,128)S(1)}, f32[64,64]{1,0:T(8,128)}, u32[]{:S(2)}) copy-start(f32[64,64]{1,0:T(8,128)} %param.13) | copy-start | bytes 49156
  91.5 36.4 %copy-start.2 = (f32[64,64]{1,0:T(8,128)S(1)}, f32[64,64]{1,0:T(8,128)}, u32[]{:S(2)}) copy-start(f32[64,64]{1,0:T(8,128)} %right_ref.1) | copy-start | bytes 49156
  109.6 18.3 %all-to-all-start.2 = ((f32[32,8,256]{2,1,0:T(8,128)}), f32[32,8,256]{2,1,0:T(8,128)S(1)}, u32[]{:S(2)}, u32[]{:S(2)}) async-start(f32[32,8,256]{2,1,0:T(8,128)} %shard_map.84), calls=%async_computation.2 | async-start | bytes 524288 | tf_op jit(solution)/shard_map/all_to_all | solution.py:20
  127.9 1.6 %copy-start.1 = (f32[16,8,4096]{2,1,0:T(8,128)S(1)}, f32[16,8,4096]{2,1,0:T(8,128)}, u32[]{:S(2)}) copy-start(f32[16,8,4096]{2,1,0:T(8,128)} %all-gather.3.cloned.1.call-done) | copy-start | bytes 6291460
Sparse Core Ops, SparseCore 0:
  54.4 33.2 all-gather.2

commit v7 on v6

--- a/solution.py
+++ b/solution.py
@@ -234,15 +234,16 @@
     where = jnp.stack([1 - xl, zl, xl] + starts)
     mapped = jnp.dot(hidden, in_proj, preferred_element_type=jnp.float32)
 
+    near, near_x = lax.optimization_barrier((near, near_x))
     begun, label_rows = first_products(where, near, far, weights[:3])
     packed = last_products(where, near_x, far_x, weights, near, far, begun, label_rows)
     parts = exchange(packed.reshape(32, 8, 256), ("zh", "zl", "xh", "xl"))
+    parts, every_query = lax.optimization_barrier((parts, every_query))
     merged = pl.pallas_call(
         merge_kernel,
         out_shape=jax.ShapeDtypeStruct((32, 8, 256), jnp.float32),
         cost_estimate=pl.CostEstimate(flops=300_000, bytes_accessed=600_000, transcendentals=256),
     )(parts)
-    merged, every_query = lax.optimization_barrier((merged, every_query))
     parts = exchange(merged, VOC).reshape(2, 4, 4, 8, 256)
     mapped = jnp.transpose(mapped.reshape(4, 2, 8, 64), (3, 1, 0, 2)).reshape(64, 64)
     scores = pl.pallas_call(

time: 139 us -> 139 us (level)
  blocking collectives: 25.2 us -> 8.92 us
  waiting for transfers between devices: 34 us -> 45.2 us
  starting transfers between devices: 41.5 us -> 46.5 us
    all_to_all x1 -> x0, blocking collectives: 16.2 us -> none  [exchange(): return lax.all_to_all(blocks, axes, split_axis=0, concat_axis=0, tiled=True)]
    all_to_all x2 -> x3, waiting for transfers between devices: 21.7 us -> 32.9 us  [exchange(): return lax.all_to_all(blocks, axes, split_axis=0, concat_axis=0, tiled=True)]
    all_to_all x2 -> x3, starting transfers between devices: 18.9 us -> 23.9 us  [exchange(): return lax.all_to_all(blocks, axes, split_axis=0, concat_axis=0, tiled=True)]
  transfers between devices with their start and end apart: 9 -> 10, of which waited for: 4 -> 6; matrix products, arithmetic and copies ran while one was open for 3% -> 3% of each run, Pallas kernels for 10% -> 9%
where the time goes in v7:
time: 139 us; the launch traced here: 138 us
  starting transfers between devices  46.5 us (33%)
  waiting for transfers between devices  45.2 us (33%)
  Pallas kernels  16.5 us (12%)
  between operations  13.7 us (10%)
  blocking collectives  8.92 us (6%)
  other arithmetic  2.94 us (2%)
  local copies, waits for them, and re-layouts  2.8 us (2%)
    all_to_all x3, waiting for transfers between devices, exchange(): return lax.all_to_all(blocks, axes, split_axis=0, concat_axis=0, tiled=True)  32.9 us
    all_to_all x3, starting transfers between devices, exchange(): return lax.all_to_all(blocks, axes, split_axis=0, concat_axis=0, tiled=True)  23.9 us
    ppermute x4, starting transfers between devices, both_ways(): return lax.ppermute(value, axes + ('core',), pairs)  16.8 us
    ppermute x4, waiting for transfers between devices, both_ways(): return lax.ppermute(value, axes + ('core',), pairs)  12.2 us
    all_gather x1, blocking collectives, local(): query_pair = lax.all_gather(queries[0], 'xh', axis=0)  8.92 us
    pallas_call x1, Pallas kernels, last_products(): pl.pallas_call(last_kernel, out_shape=jax.ShapeDtypeStruct((4, 2, 32, 256...  7.67 us
    pallas_call x1, Pallas kernels, first_products(): pl.pallas_call(first_kernel, out_shape=(jax.ShapeDtypeStruct((256, 768),...  5.33 us
    ppermute x1, starting transfers between devices, local(): weights = [block, moved, swapped, lax.ppermute(late, 'core', SWAP)]  3.76 us
  transfers between devices with their start and end apart: 10, of which 6 were waited for; matrix products, arithmetic and copies ran while one was open for 3% of the time, Pallas kernels for 9%

profile of v7, /device:TPU:1, one launch (start us, length us, event | category | flops | bytes accessed | tf_op | source)
XLA Modules:
  0.0 137.8 jit_solution(13826379449148739229)
XLA Ops:
  6.5 0.0 copy-start
  6.5 0.9 reduce-precision_convert_fusion.1
  7.5 0.0 copy-start.6
  7.5 0.0 copy-start.4
  7.5 1.9 %pad_maximum_fusion.w0.t0 = bf16[4800,256]{1,0:T(8,128)(2,1)S(1)} fusion(bf16[64,256]{1,0:T(8,128)(2,1)S(1)} %get-tuple-element.26, bf16[64,256]{1,0:T(8,128)(2,1)S(1)} %get-tuple-element.27, bf16[64,256]{1,0:T(8,128)(2,1)S(1)} %get-tuple-element.25, bf16[4608,256]{1,0:T(8,128)(2,1)} %param.10), kind=kLoop, calls=%fused_computation | loop fusion | flops 9830400 | bytes 4915200 | tf_op jit(solution)/shard_map/concatenate | solution.py:213
  9.4 5.9 %collective-permute-start.3 = (bf16[4800,256]{1,0:T(8,128)(2,1)S(1)}, bf16[4800,256]{1,0:T(8,128)(2,1)}, u32[]{:S(2)}, u32[]{:S(2)}) collective-permute-start(bf16[4800,256]{1,0:T(8,128)(2,1)S(1)} %pad_maximum_fusion.w0.t0), channel_id=1, source_target_pairs={{0,2},{2,4},{4,6},{6,8},{8,10},{10,12},{12,14},{14,0},{1,15},{3,1}... | collective-permute-start | bytes 7372808 | tf_op jit(solution)/shard_map/ppermute | solution.py:30
  15.3 0.0 copy-done.6
  15.3 0.1 fusion.4
  15.5 0.1 copy.17
  15.6 0.9 dynamic_slice.6
  16.5 0.9 broadcast_in_dim.4
  17.3 12.5 %all-to-all-start = ((bf16[8,16,2432]{2,1,0:T(8,128)(2,1)}), bf16[8,16,2432]{2,1,0:T(8,128)(2,1)}, u32[]{:S(2)}, u32[]{:S(2)}) async-start(bf16[8,16,2432]{2,1,0:T(8,128)(2,1)} %broadcast_in_dim.4), calls=%async_computation | async-start | bytes 1245184 | tf_op jit(solution)/shard_map/all_to_all | solution.py:20
  29.8 0.0 all-gather.3.cloned.1.call-start
  29.9 0.0 copy-done.4
  29.9 8.9 %all_gather.9 = f32[2,8,4096]{2,1,0:T(8,128)} all-gather(f32[1,8,4096]{2,1,0:T(8,128)S(1)} %copy-done.4), channel_id=1, replica_groups=mesh['zh'=4,'zl'=2,'xh'=2,'xl'=2,'yh'=4,'yl'=2,'core'=2] {'xh'}, dimensions={0}, use_global_device_ids=true | all-gather | bytes 393216 | tf_op jit(solution)/shard_map/all_gather | solution.py:215
  38.8 11.3 %all-to-all-done = bf16[8,16,2432]{2,1,0:T(8,128)(2,1)} async-done(((bf16[8,16,2432]{2,1,0:T(8,128)(2,1)}), bf16[8,16,2432]{2,1,0:T(8,128)(2,1)}, u32[]{:S(2)}, u32[]{:S(2)}) %all-to-all-start) | async-done | bytes 622624 | tf_op jit(solution)/shard_map/all_to_all | solution.py:20
  50.1 4.2 %collective-permute-start.1 = (bf16[128,2432]{1,0:T(8,128)(2,1)}, bf16[128,2432]{1,0:T(8,128)(2,1)}, u32[]{:S(2)}, u32[]{:S(2)}) collective-permute-start(bf16[128,2432]{1,0:T(8,128)(2,1)} %bitcast.10.near_ref.near_digits.near3_ref), channel_id=1, source_target_pairs={{0,64},{64,128},{128,192},{192,256},{256,320},{320,384},{384,448},... | collective-permute-start | bytes 1867784 | tf_op jit(solution)/shard_map/ppermute | solution.py:30
  54.3 0.0 all-gather.3.cloned.1.call-update
  54.3 1.9 %collective-permute-start.4 = (bf16[4800,256]{1,0:T(8,128)(2,1)S(1)}, bf16[4800,256]{1,0:T(8,128)(2,1)}, u32[]{:S(2)}, u32[]{:S(2)}) collective-permute-start(bf16[4800,256]{1,0:T(8,128)(2,1)S(1)} %pad_maximum_fusion.w0.t0), channel_id=1, source_target_pairs={{0,1},{1,0},{2,3},{3,2},{4,5},{5,4},{6,7},{7,6},{8,9},{9,8},{10,11... | collective-permute-start | bytes 7372808 | tf_op jit(solution)/shard_map/ppermute | solution.py:222
  56.2 6.0 %collective-permute-done.1.far_ref.far_digits.far3_ref = bf16[128,2432]{1,0:T(8,128)(2,1)} collective-permute-done((bf16[128,2432]{1,0:T(8,128)(2,1)}, bf16[128,2432]{1,0:T(8,128)(2,1)}, u32[]{:S(2)}, u32[]{:S(2)}) %collective-permute-start.1) | collective-permute-done | bytes 622624 | tf_op jit(solution)/shard_map/ppermute | solution.py:30
  62.3 0.0 collective-permute-done.3.w1.t1
  62.3 3.8 %collective-permute-start.5 = (bf16[4800,256]{1,0:T(8,128)(2,1)}, bf16[4800,256]{1,0:T(8,128)(2,1)}, u32[]{:S(2)}, u32[]{:S(2)}) collective-permute-start(bf16[4800,256]{1,0:T(8,128)(2,1)} %collective-permute-done.3.w1.t1), channel_id=1, source_target_pairs={{0,1},{1,0},{2,3},{3,2},{4,5},{5,4},{6,7},{7,6},{8,9},{9,8},{10,11... | collective-permute-start | bytes 7372808 | tf_op jit(solution)/shard_map/ppermute | solution.py:224
  66.0 4.3 %collective-permute-start = (bf16[128,2432]{1,0:T(8,128)(2,1)}, bf16[128,2432]{1,0:T(8,128)(2,1)}, u32[]{:S(2)}, u32[]{:S(2)}) collective-permute-start(bf16[128,2432]{1,0:T(8,128)(2,1)} %bitcast.10.near_ref.near_digits.near3_ref), channel_id=1, source_target_pairs={{0,16},{16,32},{32,48},{48,0},{1,49},{17,1},{33,17},{49,33},{2,18}... | collective-permute-start | bytes 1867784 | tf_op jit(solution)/shard_map/ppermute | solution.py:30
  70.3 2.5 %collective-permute-start.2 = (bf16[128,2432]{1,0:T(8,128)(2,1)}, bf16[128,2432]{1,0:T(8,128)(2,1)}, u32[]{:S(2)}, u32[]{:S(2)}) collective-permute-start(bf16[128,2432]{1,0:T(8,128)(2,1)} %collective-permute-done.1.far_ref.far_digits.far3_ref), channel_id=1, source_target_pairs={{0,16},{16,32},{32,48},{48,0},{1,49},{17,1},{33,17},{49,33},{2,18}... | collective-permute-start | bytes 1867784 | tf_op jit(solution)/shard_map/ppermute | solution.py:30
  72.8 0.1 stack.47.where_ref
  72.9 4.9 %collective-permute-done.near_ref = bf16[128,2432]{1,0:T(8,128)(2,1)} collective-permute-done((bf16[128,2432]{1,0:T(8,128)(2,1)}, bf16[128,2432]{1,0:T(8,128)(2,1)}, u32[]{:S(2)}, u32[]{:S(2)}) %collective-permute-start) | collective-permute-done | bytes 622624 | tf_op jit(solution)/shard_map/ppermute | solution.py:30
  77.8 0.0 collective-permute-done.4.w2.t2
  77.8 5.3 %shard_map.82 = (f32[256,768]{1,0:T(8,128)S(1)}, f32[256,64]{1,0:T(8,128)S(1)}) custom-call(s32[7]{0:T(128)S(1)} %stack.47.where_ref, bf16[128,2432]{1,0:T(8,128)(2,1)} %bitcast.10.near_ref.near_digits.near3_ref, bf16[128,2432]{1,0:T(8,128)(2,1)} %collective-permute-done.1.far_ref.far_digits.far3_ref, bf16[4800,256]{1,0:T(8,128)(2,1)S(1)} %pad_maximum_fusion.w0.t0, ...), custom_call_target="tpu_custom_call" | custom-call | flops 1207959552 | bytes 7000000 | tf_op jit(solution)/shard_map/pallas_call | solution.py:163
  83.2 1.3 collective-permute-done.2.far_ref
  84.5 0.0 collective-permute-done.5.w3.own3_ref.t3
  84.5 7.7 %shard_map.83 = f32[4,2,32,256]{3,2,1,0:T(8,128)} custom-call(s32[7]{0:T(128)S(1)} %stack.47.where_ref, bf16[128,2432]{1,0:T(8,128)(2,1)} %collective-permute-done.near_ref, bf16[128,2432]{1,0:T(8,128)(2,1)} %collective-permute-done.2.far_ref, bf16[4800,256]{1,0:T(8,128)(2,1)S(1)} %pad_maximum_fusion.w0.t0, bf16[4800,256]{1,0:T(8,128)(2,1)} %collective-permute-done.3.w1.t1, ...), custom_call_target="tpu_custom_call" | custom-call | flops 1207959552 | bytes 7000000 | tf_op jit(solution)/shard_map/pallas_call | solution.py:178
  92.2 0.0 copy-start.2
  92.2 4.8 %all-to-all-start.1 = ((f32[32,8,256]{2,1,0:T(8,128)}), f32[32,8,256]{2,1,0:T(8,128)S(1)}, u32[]{:S(2)}, u32[]{:S(2)}) async-start(f32[32,8,256]{2,1,0:T(8,128)} %bitcast.12), calls=%async_computation.1 | async-start | bytes 524288 | tf_op jit(solution)/shard_map/all_to_all | solution.py:20
  97.0 0.0 all-gather.3.cloned.1.call-done
  97.0 0.0 copy-start.1
  97.0 11.2 %all-to-all-done.1.parts_ref = f32[32,8,256]{2,1,0:T(8,128)S(1)} async-done(((f32[32,8,256]{2,1,0:T(8,128)}), f32[32,8,256]{2,1,0:T(8,128)S(1)}, u32[]{:S(2)}, u32[]{:S(2)}) %all-to-all-start.1) | async-done | bytes 262176 | tf_op jit(solution)/shard_map/all_to_all | solution.py:20
  108.2 0.0 copy-start.3
  108.2 0.7 copy-done.3
  108.9 1.9 %shard_map.84 = f32[32,8,256]{2,1,0:T(8,128)} custom-call(f32[32,8,256]{2,1,0:T(8,128)} %copy-done.3), custom_call_target="tpu_custom_call" | custom-call | flops 300000 | bytes 600000 | tf_op jit(solution)/shard_map/pallas_call | solution.py:242
  110.7 6.6 %all-to-all-start.2 = ((f32[32,8,256]{2,1,0:T(8,128)}), f32[32,8,256]{2,1,0:T(8,128)S(1)}, u32[]{:S(2)}, u32[]{:S(2)}) async-start(f32[32,8,256]{2,1,0:T(8,128)} %shard_map.84), calls=%async_computation.2 | async-start | bytes 524288 | tf_op jit(solution)/shard_map/all_to_all | solution.py:20
  117.4 0.0 copy-done.5
  117.4 0.0 copy-done
  117.4 1.4 fusion.8
  118.8 0.1 copy.16.mapped_ref
  118.9 10.4 %all-to-all-done.2 = f32[32,8,256]{2,1,0:T(8,128)S(1)} async-done(((f32[32,8,256]{2,1,0:T(8,128)}), f32[32,8,256]{2,1,0:T(8,128)S(1)}, u32[]{:S(2)}, u32[]{:S(2)}) %all-to-all-start.2) | async-done | bytes 262176 | tf_op jit(solution)/shard_map/all_to_all | solution.py:20
  129.3 0.0 copy-done.2
  129.3 0.0 copy-done.1
  129.3 1.6 %shard_map.85 = f32[8,16]{1,0:T(8,128)} custom-call(f32[2,4,4,8,256]{4,3,2,1,0:T(8,128)S(1)} %bitcast.35, f32[64,64]{1,0:T(8,128)S(1)} %copy.16.mapped_ref, f32[32,64]{1,0:T(8,128)S(1)} %slice.6.even_ref, f32[32,64]{1,0:T(8,128)S(1)} %slice.7.odd_ref, f32[64,64]{1,0:T(8,128)S(1)} %copy-done.2, f32[128,4096]{1,0:T(8,128)S(1)} %bitcast.34), custom_call_target="tpu_custom_call" | custom-call | flops 2000000 | bytes 2500000 | tf_op jit(solution)/shard_map/pallas_call | solution.py:249
  (7 shorter events, 0.1 us)
Async XLA Ops:
  6.5 110.9 %copy-start = (bf16[4608,64]{0,1:T(8,128)(2,1)S(1)}, bf16[4608,64]{0,1:T(8,128)(2,1)}, u32[]{:S(2)}) copy-start(bf16[4608,64]{0,1:T(8,128)(2,1)} %param.11) | copy-start | bytes 1769476
  7.5 7.9 %copy-start.6 = (s32[64]{0:T(128)S(1)}, s32[64]{0:T(128)}, u32[]{:S(2)}) copy-start(s32[64]{0:T(128)} %param.9) | copy-start | bytes 772
  7.5 22.4 %copy-start.4 = (f32[1,8,4096]{2,1,0:T(8,128)S(1)}, f32[1,8,4096]{2,1,0:T(8,128)}, u32[]{:S(2)}) copy-start(f32[1,8,4096]{2,1,0:T(8,128)} %param.15) | copy-start | bytes 393220
  9.4 52.9 %collective-permute-start.3 = (bf16[4800,256]{1,0:T(8,128)(2,1)S(1)}, bf16[4800,256]{1,0:T(8,128)(2,1)}, u32[]{:S(2)}, u32[]{:S(2)}) collective-permute-start(bf16[4800,256]{1,0:T(8,128)(2,1)S(1)} %pad_maximum_fusion.w0.t0), channel_id=1, source_target_pairs={{0,2},{2,4},{4,6},{6,8},{8,10},{10,12},{12,14},{14,0},{1,15},{3,1}... | collective-permute-start | bytes 7372808 | tf_op jit(solution)/shard_map/ppermute | solution.py:30
  17.3 32.7 %all-to-all-start = ((bf16[8,16,2432]{2,1,0:T(8,128)(2,1)}), bf16[8,16,2432]{2,1,0:T(8,128)(2,1)}, u32[]{:S(2)}, u32[]{:S(2)}) async-start(bf16[8,16,2432]{2,1,0:T(8,128)(2,1)} %broadcast_in_dim.4), calls=%async_computation | async-start | bytes 1245184 | tf_op jit(solution)/shard_map/all_to_all | solution.py:20
  29.8 67.2 %all-gather.3.cloned.1.call-start = ((), (), s32[]{:S(2)}) async-start(), calls=%async_computation.3 | async-start | bytes 2359296 | tf_op jit(solution)/shard_map/all_gather | solution.py:221
  50.1 12.2 %collective-permute-start.1 = (bf16[128,2432]{1,0:T(8,128)(2,1)}, bf16[128,2432]{1,0:T(8,128)(2,1)}, u32[]{:S(2)}, u32[]{:S(2)}) collective-permute-start(bf16[128,2432]{1,0:T(8,128)(2,1)} %bitcast.10.near_ref.near_digits.near3_ref), channel_id=1, source_target_pairs={{0,64},{64,128},{128,192},{192,256},{256,320},{320,384},{384,448},... | collective-permute-start | bytes 1867784 | tf_op jit(solution)/shard_map/ppermute | solution.py:30
  54.3 23.5 %collective-permute-start.4 = (bf16[4800,256]{1,0:T(8,128)(2,1)S(1)}, bf16[4800,256]{1,0:T(8,128)(2,1)}, u32[]{:S(2)}, u32[]{:S(2)}) collective-permute-start(bf16[4800,256]{1,0:T(8,128)(2,1)S(1)} %pad_maximum_fusion.w0.t0), channel_id=1, source_target_pairs={{0,1},{1,0},{2,3},{3,2},{4,5},{5,4},{6,7},{7,6},{8,9},{9,8},{10,11... | collective-permute-start | bytes 7372808 | tf_op jit(solution)/shard_map/ppermute | solution.py:222
  62.3 22.2 %collective-permute-start.5 = (bf16[4800,256]{1,0:T(8,128)(2,1)}, bf16[4800,256]{1,0:T(8,128)(2,1)}, u32[]{:S(2)}, u32[]{:S(2)}) collective-permute-start(bf16[4800,256]{1,0:T(8,128)(2,1)} %collective-permute-done.3.w1.t1), channel_id=1, source_target_pairs={{0,1},{1,0},{2,3},{3,2},{4,5},{5,4},{6,7},{7,6},{8,9},{9,8},{10,11... | collective-permute-start | bytes 7372808 | tf_op jit(solution)/shard_map/ppermute | solution.py:224
  66.0 11.8 %collective-permute-start = (bf16[128,2432]{1,0:T(8,128)(2,1)}, bf16[128,2432]{1,0:T(8,128)(2,1)}, u32[]{:S(2)}, u32[]{:S(2)}) collective-permute-start(bf16[128,2432]{1,0:T(8,128)(2,1)} %bitcast.10.near_ref.near_digits.near3_ref), channel_id=1, source_target_pairs={{0,16},{16,32},{32,48},{48,0},{1,49},{17,1},{33,17},{49,33},{2,18}... | collective-permute-start | bytes 1867784 | tf_op jit(solution)/shard_map/ppermute | solution.py:30
  70.3 14.1 %collective-permute-start.2 = (bf16[128,2432]{1,0:T(8,128)(2,1)}, bf16[128,2432]{1,0:T(8,128)(2,1)}, u32[]{:S(2)}, u32[]{:S(2)}) collective-permute-start(bf16[128,2432]{1,0:T(8,128)(2,1)} %collective-permute-done.1.far_ref.far_digits.far3_ref), channel_id=1, source_target_pairs={{0,16},{16,32},{32,48},{48,0},{1,49},{17,1},{33,17},{49,33},{2,18}... | collective-permute-start | bytes 1867784 | tf_op jit(solution)/shard_map/ppermute | solution.py:30
  84.5 32.9 %copy-start.5 = (f32[64,64]{1,0:T(8,128)S(1)}, f32[64,64]{1,0:T(8,128)}, u32[]{:S(2)}) copy-start(f32[64,64]{1,0:T(8,128)} %param.13) | copy-start | bytes 49156
  92.2 37.1 %copy-start.2 = (f32[64,64]{1,0:T(8,128)S(1)}, f32[64,64]{1,0:T(8,128)}, u32[]{:S(2)}) copy-start(f32[64,64]{1,0:T(8,128)} %right_ref.1) | copy-start | bytes 49156
  92.2 16.0 %all-to-all-start.1 = ((f32[32,8,256]{2,1,0:T(8,128)}), f32[32,8,256]{2,1,0:T(8,128)S(1)}, u32[]{:S(2)}, u32[]{:S(2)}) async-start(f32[32,8,256]{2,1,0:T(8,128)} %bitcast.12), calls=%async_computation.1 | async-start | bytes 524288 | tf_op jit(solution)/shard_map/all_to_all | solution.py:20
  97.0 32.3 %copy-start.1 = (f32[16,8,4096]{2,1,0:T(8,128)S(1)}, f32[16,8,4096]{2,1,0:T(8,128)}, u32[]{:S(2)}) copy-start(f32[16,8,4096]{2,1,0:T(8,128)} %all-gather.3.cloned.1.call-done) | copy-start | bytes 6291460
  108.2 0.7 copy-start.3
  110.7 18.5 %all-to-all-start.2 = ((f32[32,8,256]{2,1,0:T(8,128)}), f32[32,8,256]{2,1,0:T(8,128)S(1)}, u32[]{:S(2)}, u32[]{:S(2)}) async-start(f32[32,8,256]{2,1,0:T(8,128)} %shard_map.84), calls=%async_computation.2 | async-start | bytes 524288 | tf_op jit(solution)/shard_map/all_to_all | solution.py:20
Sparse Core Ops, SparseCore 0:
  54.4 33.2 all-gather.2

commit v8 on v7

--- a/solution.py
+++ b/solution.py
@@ -216,7 +216,8 @@
     near, query_pair = lax.optimization_barrier((near, query_pair))
     far = both_ways(near, ("zh", "zl"), 8)
     near_x = both_ways(near, ("xh", "xl"), 4)
-    far_x = both_ways(far, ("xh", "xl"), 4)
+    late, near_x = lax.optimization_barrier((far, near_x))
+    far_x = both_ways(late, ("xh", "xl"), 4)
     moved = both_ways(block, ("yh", "yl"), 8)
     every_query = lax.all_gather(query_pair, ("zh", "zl"), axis=0)
     swapped = lax.ppermute(block, "core", SWAP)
@@ -234,7 +235,6 @@
     where = jnp.stack([1 - xl, zl, xl] + starts)
     mapped = jnp.dot(hidden, in_proj, preferred_element_type=jnp.float32)
 
-    near, near_x = lax.optimization_barrier((near, near_x))
     begun, label_rows = first_products(where, near, far, weights[:3])
     packed = last_products(where, near_x, far_x, weights, near, far, begun, label_rows)
     parts = exchange(packed.reshape(32, 8, 256), ("zh", "zl", "xh", "xl"))

time: 139 us -> 146 us (1.050)
  starting transfers between devices: 46.5 us -> 50.5 us
  waiting for transfers between devices: 45.2 us -> 47.7 us
    ppermute x4, waiting for transfers between devices: 12.2 us -> 15.5 us  [both_ways(): return lax.ppermute(value, axes + ('core',), pairs)]
    ppermute x4, starting transfers between devices: 16.8 us -> 19.7 us  [both_ways(): return lax.ppermute(value, axes + ('core',), pairs)]
  transfers between devices with their start and end apart: 10 -> 10, of which waited for: 6 -> 6; matrix products, arithmetic and copies ran while one was open for 3% -> 2% of each run, Pallas kernels for 9% -> 9%
where the time goes in v8:
time: 146 us; the launch traced here: 145 us
  starting transfers between devices  50.5 us (35%)
  waiting for transfers between devices  47.7 us (33%)
  Pallas kernels  16.3 us (11%)
  between operations  13.7 us (9%)
  blocking collectives  8.92 us (6%)
  local copies, waits for them, and re-layouts  3.62 us (2%)
  other arithmetic  2.94 us (2%)
    all_to_all x3, waiting for transfers between devices, exchange(): return lax.all_to_all(blocks, axes, split_axis=0, concat_axis=0, tiled=True)  32.1 us
    all_to_all x3, starting transfers between devices, exchange(): return lax.all_to_all(blocks, axes, split_axis=0, concat_axis=0, tiled=True)  25.1 us
    ppermute x4, starting transfers between devices, both_ways(): return lax.ppermute(value, axes + ('core',), pairs)  19.7 us
    ppermute x4, waiting for transfers between devices, both_ways(): return lax.ppermute(value, axes + ('core',), pairs)  15.5 us
    all_gather x1, blocking collectives, local(): query_pair = lax.all_gather(queries[0], 'xh', axis=0)  8.92 us
    pallas_call x1, Pallas kernels, last_products(): pl.pallas_call(last_kernel, out_shape=jax.ShapeDtypeStruct((4, 2, 32, 256...  7.55 us
    pallas_call x1, Pallas kernels, first_products(): pl.pallas_call(first_kernel, out_shape=(jax.ShapeDtypeStruct((256, 768),...  5.31 us
    ppermute x1, starting transfers between devices, local(): weights = [block, moved, swapped, lax.ppermute(late, 'core', SWAP)]  3.76 us
  transfers between devices with their start and end apart: 10, of which 6 were waited for; matrix products, arithmetic and copies ran while one was open for 2% of the time, Pallas kernels for 9%

profile of v8, /device:TPU:1, one launch (start us, length us, event | category | flops | bytes accessed | tf_op | source)
XLA Modules:
  0.0 144.9 jit_solution(14053188784270880726)
XLA Ops:
  6.5 0.0 copy-start
  6.5 0.9 reduce-precision_convert_fusion.1
  7.5 0.0 copy-start.8
  7.5 0.0 copy-start.6
  7.5 1.9 %pad_maximum_fusion.w0.t0 = bf16[4800,256]{1,0:T(8,128)(2,1)S(1)} fusion(bf16[64,256]{1,0:T(8,128)(2,1)S(1)} %get-tuple-element.26, bf16[64,256]{1,0:T(8,128)(2,1)S(1)} %get-tuple-element.27, bf16[64,256]{1,0:T(8,128)(2,1)S(1)} %get-tuple-element.25, bf16[4608,256]{1,0:T(8,128)(2,1)} %param.10), kind=kLoop, calls=%fused_computation | loop fusion | flops 9830400 | bytes 4915200 | tf_op jit(solution)/shard_map/concatenate | solution.py:213
  9.4 5.9 %collective-permute-start.3 = (bf16[4800,256]{1,0:T(8,128)(2,1)S(1)}, bf16[4800,256]{1,0:T(8,128)(2,1)}, u32[]{:S(2)}, u32[]{:S(2)}) collective-permute-start(bf16[4800,256]{1,0:T(8,128)(2,1)S(1)} %pad_maximum_fusion.w0.t0), channel_id=1, source_target_pairs={{0,2},{2,4},{4,6},{6,8},{8,10},{10,12},{12,14},{14,0},{1,15},{3,1}... | collective-permute-start | bytes 7372808 | tf_op jit(solution)/shard_map/ppermute | solution.py:30
  15.3 0.0 copy-done.8
  15.3 0.1 fusion.4
  15.5 0.1 copy.17
  15.6 0.9 dynamic_slice.6
  16.5 0.9 broadcast_in_dim.4
  17.3 12.5 %all-to-all-start = ((bf16[8,16,2432]{2,1,0:T(8,128)(2,1)}), bf16[8,16,2432]{2,1,0:T(8,128)(2,1)}, u32[]{:S(2)}, u32[]{:S(2)}) async-start(bf16[8,16,2432]{2,1,0:T(8,128)(2,1)} %broadcast_in_dim.4), calls=%async_computation | async-start | bytes 1245184 | tf_op jit(solution)/shard_map/all_to_all | solution.py:20
  29.8 0.0 all-gather.3.cloned.1.call-start
  29.9 0.0 copy-done.6
  29.9 8.9 %all_gather.9 = f32[2,8,4096]{2,1,0:T(8,128)} all-gather(f32[1,8,4096]{2,1,0:T(8,128)S(1)} %copy-done.6), channel_id=1, replica_groups=mesh['zh'=4,'zl'=2,'xh'=2,'xl'=2,'yh'=4,'yl'=2,'core'=2] {'xh'}, dimensions={0}, use_global_device_ids=true | all-gather | bytes 393216 | tf_op jit(solution)/shard_map/all_gather | solution.py:215
  38.8 11.3 %all-to-all-done = bf16[8,16,2432]{2,1,0:T(8,128)(2,1)} async-done(((bf16[8,16,2432]{2,1,0:T(8,128)(2,1)}), bf16[8,16,2432]{2,1,0:T(8,128)(2,1)}, u32[]{:S(2)}, u32[]{:S(2)}) %all-to-all-start) | async-done | bytes 622624 | tf_op jit(solution)/shard_map/all_to_all | solution.py:20
  50.1 4.2 %collective-permute-start = (bf16[128,2432]{1,0:T(8,128)(2,1)}, bf16[128,2432]{1,0:T(8,128)(2,1)}, u32[]{:S(2)}, u32[]{:S(2)}) collective-permute-start(bf16[128,2432]{1,0:T(8,128)(2,1)} %bitcast.10.near_ref.near_digits.near3_ref), channel_id=1, source_target_pairs={{0,64},{64,128},{128,192},{192,256},{256,320},{320,384},{384,448},... | collective-permute-start | bytes 1867784 | tf_op jit(solution)/shard_map/ppermute | solution.py:30
  54.3 0.0 all-gather.3.cloned.1.call-update
  54.3 1.9 %collective-permute-start.4 = (bf16[4800,256]{1,0:T(8,128)(2,1)S(1)}, bf16[4800,256]{1,0:T(8,128)(2,1)}, u32[]{:S(2)}, u32[]{:S(2)}) collective-permute-start(bf16[4800,256]{1,0:T(8,128)(2,1)S(1)} %pad_maximum_fusion.w0.t0), channel_id=1, source_target_pairs={{0,1},{1,0},{2,3},{3,2},{4,5},{5,4},{6,7},{7,6},{8,9},{9,8},{10,11... | collective-permute-start | bytes 7372808 | tf_op jit(solution)/shard_map/ppermute | solution.py:223
  56.2 6.0 %collective-permute-done.far_ref.far_digits.far3_ref = bf16[128,2432]{1,0:T(8,128)(2,1)} collective-permute-done((bf16[128,2432]{1,0:T(8,128)(2,1)}, bf16[128,2432]{1,0:T(8,128)(2,1)}, u32[]{:S(2)}, u32[]{:S(2)}) %collective-permute-start) | collective-permute-done | bytes 622624 | tf_op jit(solution)/shard_map/ppermute | solution.py:30
  62.3 0.0 collective-permute-done.3.w1.t1
  62.3 3.8 %collective-permute-start.5 = (bf16[4800,256]{1,0:T(8,128)(2,1)}, bf16[4800,256]{1,0:T(8,128)(2,1)}, u32[]{:S(2)}, u32[]{:S(2)}) collective-permute-start(bf16[4800,256]{1,0:T(8,128)(2,1)} %collective-permute-done.3.w1.t1), channel_id=1, source_target_pairs={{0,1},{1,0},{2,3},{3,2},{4,5},{5,4},{6,7},{7,6},{8,9},{9,8},{10,11... | collective-permute-start | bytes 7372808 | tf_op jit(solution)/shard_map/ppermute | solution.py:225
  66.0 4.3 %collective-permute-start.1 = (bf16[128,2432]{1,0:T(8,128)(2,1)}, bf16[128,2432]{1,0:T(8,128)(2,1)S(1)}, u32[]{:S(2)}, u32[]{:S(2)}) collective-permute-start(bf16[128,2432]{1,0:T(8,128)(2,1)} %bitcast.10.near_ref.near_digits.near3_ref), channel_id=1, source_target_pairs={{0,16},{16,32},{32,48},{48,0},{1,49},{17,1},{33,17},{49,33},{2,18}... | collective-permute-start | bytes 1867784 | tf_op jit(solution)/shard_map/ppermute | solution.py:30
  70.3 7.5 %collective-permute-done.1.near_ref = bf16[128,2432]{1,0:T(8,128)(2,1)S(1)} collective-permute-done((bf16[128,2432]{1,0:T(8,128)(2,1)}, bf16[128,2432]{1,0:T(8,128)(2,1)S(1)}, u32[]{:S(2)}, u32[]{:S(2)}) %collective-permute-start.1) | collective-permute-done | bytes 622624 | tf_op jit(solution)/shard_map/ppermute | solution.py:30
  77.8 0.8 copy-done.2
  78.6 5.3 %collective-permute-start.2 = (bf16[128,2432]{1,0:T(8,128)(2,1)}, bf16[128,2432]{1,0:T(8,128)(2,1)}, u32[]{:S(2)}, u32[]{:S(2)}) collective-permute-start(bf16[128,2432]{1,0:T(8,128)(2,1)} %collective-permute-done.far_ref.far_digits.far3_ref), channel_id=1, source_target_pairs={{0,16},{16,32},{32,48},{48,0},{1,49},{17,1},{33,17},{49,33},{2,18}... | collective-permute-start | bytes 1867784 | tf_op jit(solution)/shard_map/ppermute | solution.py:30
  84.0 0.1 stack.47.where_ref
  84.1 0.0 collective-permute-done.4.w2.t2
  84.1 5.3 %shard_map.82 = (f32[256,768]{1,0:T(8,128)S(1)}, f32[256,64]{1,0:T(8,128)S(1)}) custom-call(s32[7]{0:T(128)S(1)} %stack.47.where_ref, bf16[128,2432]{1,0:T(8,128)(2,1)} %bitcast.10.near_ref.near_digits.near3_ref, bf16[128,2432]{1,0:T(8,128)(2,1)} %collective-permute-done.far_ref.far_digits.far3_ref, bf16[4800,256]{1,0:T(8,128)(2,1)S(1)} %pad_maximum_fusion.w0.t0, ...), custom_call_target="tpu_custom_call" | custom-call | flops 1207959552 | bytes 7000000 | tf_op jit(solution)/shard_map/pallas_call | solution.py:163
  89.4 2.0 %collective-permute-done.2.far_ref = bf16[128,2432]{1,0:T(8,128)(2,1)} collective-permute-done((bf16[128,2432]{1,0:T(8,128)(2,1)}, bf16[128,2432]{1,0:T(8,128)(2,1)}, u32[]{:S(2)}, u32[]{:S(2)}) %collective-permute-start.2) | collective-permute-done | bytes 622624 | tf_op jit(solution)/shard_map/ppermute | solution.py:30
  91.4 0.0 collective-permute-done.5.w3.own3_ref.t3
  91.4 0.0 copy-done.3
  91.4 7.6 %shard_map.83 = f32[4,2,32,256]{3,2,1,0:T(8,128)} custom-call(s32[7]{0:T(128)S(1)} %stack.47.where_ref, bf16[128,2432]{1,0:T(8,128)(2,1)S(1)} %copy-done.3, bf16[128,2432]{1,0:T(8,128)(2,1)} %collective-permute-done.2.far_ref, bf16[4800,256]{1,0:T(8,128)(2,1)S(1)} %pad_maximum_fusion.w0.t0, bf16[4800,256]{1,0:T(8,128)(2,1)} %collective-permute-done.3.w1.t1, ...), custom_call_target="tpu_custom_call" | custom-call | flops 1207959552 | bytes 7000000 | tf_op jit(solution)/shard_map/pallas_call | solution.py:178
  99.0 4.9 %all-to-all-start.1 = ((f32[32,8,256]{2,1,0:T(8,128)}), f32[32,8,256]{2,1,0:T(8,128)S(1)}, u32[]{:S(2)}, u32[]{:S(2)}) async-start(f32[32,8,256]{2,1,0:T(8,128)} %bitcast.12), calls=%async_computation.1 | async-start | bytes 524288 | tf_op jit(solution)/shard_map/all_to_all | solution.py:20
  103.9 0.0 all-gather.3.cloned.1.call-done
  103.9 0.0 copy-start.1
  103.9 10.4 %all-to-all-done.1.parts_ref = f32[32,8,256]{2,1,0:T(8,128)S(1)} async-done(((f32[32,8,256]{2,1,0:T(8,128)}), f32[32,8,256]{2,1,0:T(8,128)S(1)}, u32[]{:S(2)}, u32[]{:S(2)}) %all-to-all-start.1) | async-done | bytes 262176 | tf_op jit(solution)/shard_map/all_to_all | solution.py:20
  114.3 0.7 copy-done.5
  115.0 1.8 %shard_map.84 = f32[32,8,256]{2,1,0:T(8,128)} custom-call(f32[32,8,256]{2,1,0:T(8,128)} %copy-done.5), custom_call_target="tpu_custom_call" | custom-call | flops 300000 | bytes 600000 | tf_op jit(solution)/shard_map/pallas_call | solution.py:242
  116.9 7.7 %all-to-all-start.2 = ((f32[32,8,256]{2,1,0:T(8,128)}), f32[32,8,256]{2,1,0:T(8,128)S(1)}, u32[]{:S(2)}, u32[]{:S(2)}) async-start(f32[32,8,256]{2,1,0:T(8,128)} %shard_map.84), calls=%async_computation.2 | async-start | bytes 524288 | tf_op jit(solution)/shard_map/all_to_all | solution.py:20
  124.5 0.0 copy-done.7
  124.6 0.0 copy-done
  124.6 1.4 fusion.8
  126.0 0.1 copy.16.mapped_ref
  126.0 10.4 %all-to-all-done.2 = f32[32,8,256]{2,1,0:T(8,128)S(1)} async-done(((f32[32,8,256]{2,1,0:T(8,128)}), f32[32,8,256]{2,1,0:T(8,128)S(1)}, u32[]{:S(2)}, u32[]{:S(2)}) %all-to-all-start.2) | async-done | bytes 262176 | tf_op jit(solution)/shard_map/all_to_all | solution.py:20
  136.5 0.0 copy-done.4
  136.5 0.0 copy-done.1
  136.5 1.6 %shard_map.85 = f32[8,16]{1,0:T(8,128)} custom-call(f32[2,4,4,8,256]{4,3,2,1,0:T(8,128)S(1)} %bitcast.35, f32[64,64]{1,0:T(8,128)S(1)} %copy.16.mapped_ref, f32[32,64]{1,0:T(8,128)S(1)} %slice.6.even_ref, f32[32,64]{1,0:T(8,128)S(1)} %slice.7.odd_ref, f32[64,64]{1,0:T(8,128)S(1)} %copy-done.4, f32[128,4096]{1,0:T(8,128)S(1)} %bitcast.34), custom_call_target="tpu_custom_call" | custom-call | flops 2000000 | bytes 2500000 | tf_op jit(solution)/shard_map/pallas_call | solution.py:249
  (11 shorter events, 0.1 us)
Async XLA Ops:
  6.5 118.1 %copy-start = (bf16[4608,64]{0,1:T(8,128)(2,1)S(1)}, bf16[4608,64]{0,1:T(8,128)(2,1)}, u32[]{:S(2)}) copy-start(bf16[4608,64]{0,1:T(8,128)(2,1)} %param.11) | copy-start | bytes 1769476
  7.5 7.9 %copy-start.8 = (s32[64]{0:T(128)S(1)}, s32[64]{0:T(128)}, u32[]{:S(2)}) copy-start(s32[64]{0:T(128)} %param.9) | copy-start | bytes 772
  7.5 22.4 %copy-start.6 = (f32[1,8,4096]{2,1,0:T(8,128)S(1)}, f32[1,8,4096]{2,1,0:T(8,128)}, u32[]{:S(2)}) copy-start(f32[1,8,4096]{2,1,0:T(8,128)} %param.15) | copy-start | bytes 393220
  9.4 52.9 %collective-permute-start.3 = (bf16[4800,256]{1,0:T(8,128)(2,1)S(1)}, bf16[4800,256]{1,0:T(8,128)(2,1)}, u32[]{:S(2)}, u32[]{:S(2)}) collective-permute-start(bf16[4800,256]{1,0:T(8,128)(2,1)S(1)} %pad_maximum_fusion.w0.t0), channel_id=1, source_target_pairs={{0,2},{2,4},{4,6},{6,8},{8,10},{10,12},{12,14},{14,0},{1,15},{3,1}... | collective-permute-start | bytes 7372808 | tf_op jit(solution)/shard_map/ppermute | solution.py:30
  17.3 32.7 %all-to-all-start = ((bf16[8,16,2432]{2,1,0:T(8,128)(2,1)}), bf16[8,16,2432]{2,1,0:T(8,128)(2,1)}, u32[]{:S(2)}, u32[]{:S(2)}) async-start(bf16[8,16,2432]{2,1,0:T(8,128)(2,1)} %broadcast_in_dim.4), calls=%async_computation | async-start | bytes 1245184 | tf_op jit(solution)/shard_map/all_to_all | solution.py:20
  29.8 74.1 %all-gather.3.cloned.1.call-start = ((), (), s32[]{:S(2)}) async-start(), calls=%async_computation.3 | async-start | bytes 2359296 | tf_op jit(solution)/shard_map/all_gather | solution.py:222
  50.1 12.2 %collective-permute-start = (bf16[128,2432]{1,0:T(8,128)(2,1)}, bf16[128,2432]{1,0:T(8,128)(2,1)}, u32[]{:S(2)}, u32[]{:S(2)}) collective-permute-start(bf16[128,2432]{1,0:T(8,128)(2,1)} %bitcast.10.near_ref.near_digits.near3_ref), channel_id=1, source_target_pairs={{0,64},{64,128},{128,192},{192,256},{256,320},{320,384},{384,448},... | collective-permute-start | bytes 1867784 | tf_op jit(solution)/shard_map/ppermute | solution.py:30
  54.3 29.8 %collective-permute-start.4 = (bf16[4800,256]{1,0:T(8,128)(2,1)S(1)}, bf16[4800,256]{1,0:T(8,128)(2,1)}, u32[]{:S(2)}, u32[]{:S(2)}) collective-permute-start(bf16[4800,256]{1,0:T(8,128)(2,1)S(1)} %pad_maximum_fusion.w0.t0), channel_id=1, source_target_pairs={{0,1},{1,0},{2,3},{3,2},{4,5},{5,4},{6,7},{7,6},{8,9},{9,8},{10,11... | collective-permute-start | bytes 7372808 | tf_op jit(solution)/shard_map/ppermute | solution.py:223
  62.3 29.2 %collective-permute-start.5 = (bf16[4800,256]{1,0:T(8,128)(2,1)}, bf16[4800,256]{1,0:T(8,128)(2,1)}, u32[]{:S(2)}, u32[]{:S(2)}) collective-permute-start(bf16[4800,256]{1,0:T(8,128)(2,1)} %collective-permute-done.3.w1.t1), channel_id=1, source_target_pairs={{0,1},{1,0},{2,3},{3,2},{4,5},{5,4},{6,7},{7,6},{8,9},{9,8},{10,11... | collective-permute-start | bytes 7372808 | tf_op jit(solution)/shard_map/ppermute | solution.py:225
  66.0 11.8 %collective-permute-start.1 = (bf16[128,2432]{1,0:T(8,128)(2,1)}, bf16[128,2432]{1,0:T(8,128)(2,1)S(1)}, u32[]{:S(2)}, u32[]{:S(2)}) collective-permute-start(bf16[128,2432]{1,0:T(8,128)(2,1)} %bitcast.10.near_ref.near_digits.near3_ref), channel_id=1, source_target_pairs={{0,16},{16,32},{32,48},{48,0},{1,49},{17,1},{33,17},{49,33},{2,18}... | collective-permute-start | bytes 1867784 | tf_op jit(solution)/shard_map/ppermute | solution.py:30
  77.8 0.8 copy-start.2
  78.6 12.8 %collective-permute-start.2 = (bf16[128,2432]{1,0:T(8,128)(2,1)}, bf16[128,2432]{1,0:T(8,128)(2,1)}, u32[]{:S(2)}, u32[]{:S(2)}) collective-permute-start(bf16[128,2432]{1,0:T(8,128)(2,1)} %collective-permute-done.far_ref.far_digits.far3_ref), channel_id=1, source_target_pairs={{0,16},{16,32},{32,48},{48,0},{1,49},{17,1},{33,17},{49,33},{2,18}... | collective-permute-start | bytes 1867784 | tf_op jit(solution)/shard_map/ppermute | solution.py:30
  84.1 7.3 %copy-start.3 = (bf16[128,2432]{1,0:T(8,128)(2,1)S(1)}, bf16[128,2432]{1,0:T(8,128)(2,1)}, u32[]{:S(2)}) copy-start(bf16[128,2432]{1,0:T(8,128)(2,1)} %copy-done.2) | copy-start | bytes 1867780
  91.4 33.1 %copy-start.7 = (f32[64,64]{1,0:T(8,128)S(1)}, f32[64,64]{1,0:T(8,128)}, u32[]{:S(2)}) copy-start(f32[64,64]{1,0:T(8,128)} %param.13) | copy-start | bytes 49156
  99.0 37.5 %copy-start.4 = (f32[64,64]{1,0:T(8,128)S(1)}, f32[64,64]{1,0:T(8,128)}, u32[]{:S(2)}) copy-start(f32[64,64]{1,0:T(8,128)} %right_ref.1) | copy-start | bytes 49156
  99.0 15.3 %all-to-all-start.1 = ((f32[32,8,256]{2,1,0:T(8,128)}), f32[32,8,256]{2,1,0:T(8,128)S(1)}, u32[]{:S(2)}, u32[]{:S(2)}) async-start(f32[32,8,256]{2,1,0:T(8,128)} %bitcast.12), calls=%async_computation.1 | async-start | bytes 524288 | tf_op jit(solution)/shard_map/all_to_all | solution.py:20
  103.9 32.5 %copy-start.1 = (f32[16,8,4096]{2,1,0:T(8,128)S(1)}, f32[16,8,4096]{2,1,0:T(8,128)}, u32[]{:S(2)}) copy-start(f32[16,8,4096]{2,1,0:T(8,128)} %all-gather.3.cloned.1.call-done) | copy-start | bytes 6291460
  114.3 0.7 copy-start.5
  116.9 19.6 %all-to-all-start.2 = ((f32[32,8,256]{2,1,0:T(8,128)}), f32[32,8,256]{2,1,0:T(8,128)S(1)}, u32[]{:S(2)}, u32[]{:S(2)}) async-start(f32[32,8,256]{2,1,0:T(8,128)} %shard_map.84), calls=%async_computation.2 | async-start | bytes 524288 | tf_op jit(solution)/shard_map/all_to_all | solution.py:20
Sparse Core Ops, SparseCore 0:
  54.4 33.2 all-gather.2

commit v9 on v7

--- a/solution.py
+++ b/solution.py
@@ -220,7 +220,7 @@
     moved = both_ways(block, ("yh", "yl"), 8)
     every_query = lax.all_gather(query_pair, ("zh", "zl"), axis=0)
     swapped = lax.ppermute(block, "core", SWAP)
-    late, _ = lax.optimization_barrier((moved, far))
+    late, _, _ = lax.optimization_barrier((moved, far, near_x))
     weights = [block, moved, swapped, lax.ppermute(late, "core", SWAP)]
 
     below, above = ((y + 7) % 8) * 2, ((y + 1) % 8) * 2 + 1
@@ -234,7 +234,6 @@
     where = jnp.stack([1 - xl, zl, xl] + starts)
     mapped = jnp.dot(hidden, in_proj, preferred_element_type=jnp.float32)
 
-    near, near_x = lax.optimization_barrier((near, near_x))
     begun, label_rows = first_products(where, near, far, weights[:3])
     packed = last_products(where, near_x, far_x, weights, near, far, begun, label_rows)
     parts = exchange(packed.reshape(32, 8, 256), ("zh", "zl", "xh", "xl"))

time: 139 us -> 136 us (0.978)
  waiting for transfers between devices: 45.2 us -> 43.7 us
    ppermute x4, starting transfers between devices: 16.8 us -> 14.1 us  [both_ways(): return lax.ppermute(value, axes + ('core',), pairs)]
  transfers between devices with their start and end apart: 10 -> 10, of which waited for: 6 -> 6; matrix products, arithmetic and copies ran while one was open for 3% -> 3% of each run, Pallas kernels for 9% -> 10%
where the time goes in v9:
time: 136 us; the launch traced here: 135 us
  starting transfers between devices  45.2 us (33%)
  waiting for transfers between devices  43.7 us (32%)
  Pallas kernels  16.5 us (12%)
  between operations  13.7 us (10%)
  blocking collectives  8.92 us (7%)
  other arithmetic  2.94 us (2%)
  local copies, waits for them, and re-layouts  2.8 us (2%)
  matrix products  1.36 us (1%)
    all_to_all x3, waiting for transfers between devices, exchange(): return lax.all_to_all(blocks, axes, split_axis=0, concat_axis=0, tiled=True)  32.1 us
    all_to_all x3, starting transfers between devices, exchange(): return lax.all_to_all(blocks, axes, split_axis=0, concat_axis=0, tiled=True)  25.3 us
    ppermute x4, starting transfers between devices, both_ways(): return lax.ppermute(value, axes + ('core',), pairs)  14.1 us
    ppermute x4, waiting for transfers between devices, both_ways(): return lax.ppermute(value, axes + ('core',), pairs)  11.5 us
    all_gather x1, blocking collectives, local(): query_pair = lax.all_gather(queries[0], 'xh', axis=0)  8.92 us
    pallas_call x1, Pallas kernels, last_products(): pl.pallas_call(last_kernel, out_shape=jax.ShapeDtypeStruct((4, 2, 32, 256...  7.73 us
    pallas_call x1, Pallas kernels, first_products(): pl.pallas_call(first_kernel, out_shape=(jax.ShapeDtypeStruct((256, 768),...  5.33 us
    ppermute x1, starting transfers between devices, local(): weights = [block, moved, swapped, lax.ppermute(late, 'core', SWAP)]  3.74 us
  transfers between devices with their start and end apart: 10, of which 6 were waited for; matrix products, arithmetic and copies ran while one was open for 3% of the time, Pallas kernels for 10%

profile of v9, /device:TPU:1, one launch (start us, length us, event | category | flops | bytes accessed | tf_op | source)
XLA Modules:
  0.0 135.1 jit_solution(2177323069451311541)
XLA Ops:
  6.5 0.0 copy-start
  6.5 0.9 reduce-precision_convert_fusion.1
  7.5 0.0 copy-start.6
  7.5 0.0 copy-start.4
  7.5 1.9 %pad_maximum_fusion.w0.t0 = bf16[4800,256]{1,0:T(8,128)(2,1)S(1)} fusion(bf16[64,256]{1,0:T(8,128)(2,1)S(1)} %get-tuple-element.22, bf16[64,256]{1,0:T(8,128)(2,1)S(1)} %get-tuple-element.23, bf16[64,256]{1,0:T(8,128)(2,1)S(1)} %get-tuple-element.21, bf16[4608,256]{1,0:T(8,128)(2,1)} %param.10), kind=kLoop, calls=%fused_computation | loop fusion | flops 9830400 | bytes 4915200 | tf_op jit(solution)/shard_map/concatenate | solution.py:213
  9.4 5.9 %collective-permute-start.3 = (bf16[4800,256]{1,0:T(8,128)(2,1)S(1)}, bf16[4800,256]{1,0:T(8,128)(2,1)}, u32[]{:S(2)}, u32[]{:S(2)}) collective-permute-start(bf16[4800,256]{1,0:T(8,128)(2,1)S(1)} %pad_maximum_fusion.w0.t0), channel_id=1, source_target_pairs={{0,2},{2,4},{4,6},{6,8},{8,10},{10,12},{12,14},{14,0},{1,15},{3,1}... | collective-permute-start | bytes 7372808 | tf_op jit(solution)/shard_map/ppermute | solution.py:30
  15.3 0.0 copy-done.6
  15.3 0.1 fusion.4
  15.5 0.1 copy.17
  15.6 0.9 dynamic_slice.6
  16.5 0.9 broadcast_in_dim.4
  17.3 12.5 %all-to-all-start = ((bf16[8,16,2432]{2,1,0:T(8,128)(2,1)}), bf16[8,16,2432]{2,1,0:T(8,128)(2,1)}, u32[]{:S(2)}, u32[]{:S(2)}) async-start(bf16[8,16,2432]{2,1,0:T(8,128)(2,1)} %broadcast_in_dim.4), calls=%async_computation | async-start | bytes 1245184 | tf_op jit(solution)/shard_map/all_to_all | solution.py:20
  29.8 0.0 all-gather.3.cloned.1.call-start
  29.9 0.0 copy-done.4
  29.9 8.9 %all_gather.9 = f32[2,8,4096]{2,1,0:T(8,128)} all-gather(f32[1,8,4096]{2,1,0:T(8,128)S(1)} %copy-done.4), channel_id=1, replica_groups=mesh['zh'=4,'zl'=2,'xh'=2,'xl'=2,'yh'=4,'yl'=2,'core'=2] {'xh'}, dimensions={0}, use_global_device_ids=true | all-gather | bytes 393216 | tf_op jit(solution)/shard_map/all_gather | solution.py:215
  38.8 11.3 %all-to-all-done = bf16[8,16,2432]{2,1,0:T(8,128)(2,1)} async-done(((bf16[8,16,2432]{2,1,0:T(8,128)(2,1)}), bf16[8,16,2432]{2,1,0:T(8,128)(2,1)}, u32[]{:S(2)}, u32[]{:S(2)}) %all-to-all-start) | async-done | bytes 622624 | tf_op jit(solution)/shard_map/all_to_all | solution.py:20
  50.1 4.2 %collective-permute-start.1 = (bf16[128,2432]{1,0:T(8,128)(2,1)}, bf16[128,2432]{1,0:T(8,128)(2,1)}, u32[]{:S(2)}, u32[]{:S(2)}) collective-permute-start(bf16[128,2432]{1,0:T(8,128)(2,1)} %bitcast.10.near_ref.near_digits.near3_ref), channel_id=1, source_target_pairs={{0,64},{64,128},{128,192},{192,256},{256,320},{320,384},{384,448},... | collective-permute-start | bytes 1867784 | tf_op jit(solution)/shard_map/ppermute | solution.py:30
  54.3 2.0 %collective-permute-start = (bf16[128,2432]{1,0:T(8,128)(2,1)}, bf16[128,2432]{1,0:T(8,128)(2,1)}, u32[]{:S(2)}, u32[]{:S(2)}) collective-permute-start(bf16[128,2432]{1,0:T(8,128)(2,1)} %bitcast.10.near_ref.near_digits.near3_ref), channel_id=1, source_target_pairs={{0,16},{16,32},{32,48},{48,0},{1,49},{17,1},{33,17},{49,33},{2,18}... | collective-permute-start | bytes 1867784 | tf_op jit(solution)/shard_map/ppermute | solution.py:30
  56.3 0.0 all-gather.3.cloned.1.call-update
  56.3 2.2 %collective-permute-start.4 = (bf16[4800,256]{1,0:T(8,128)(2,1)S(1)}, bf16[4800,256]{1,0:T(8,128)(2,1)}, u32[]{:S(2)}, u32[]{:S(2)}) collective-permute-start(bf16[4800,256]{1,0:T(8,128)(2,1)S(1)} %pad_maximum_fusion.w0.t0), channel_id=1, source_target_pairs={{0,1},{1,0},{2,3},{3,2},{4,5},{5,4},{6,7},{7,6},{8,9},{9,8},{10,11... | collective-permute-start | bytes 7372808 | tf_op jit(solution)/shard_map/ppermute | solution.py:222
  58.5 3.2 %collective-permute-done.1.far_ref.far_digits.far3_ref = bf16[128,2432]{1,0:T(8,128)(2,1)} collective-permute-done((bf16[128,2432]{1,0:T(8,128)(2,1)}, bf16[128,2432]{1,0:T(8,128)(2,1)}, u32[]{:S(2)}, u32[]{:S(2)}) %collective-permute-start.1) | collective-permute-done | bytes 622624 | tf_op jit(solution)/shard_map/ppermute | solution.py:30
  61.7 4.1 %collective-permute-done.near_ref = bf16[128,2432]{1,0:T(8,128)(2,1)} collective-permute-done((bf16[128,2432]{1,0:T(8,128)(2,1)}, bf16[128,2432]{1,0:T(8,128)(2,1)}, u32[]{:S(2)}, u32[]{:S(2)}) %collective-permute-start) | collective-permute-done | bytes 622624 | tf_op jit(solution)/shard_map/ppermute | solution.py:30
  65.8 0.0 collective-permute-done.3.w1.t1
  65.9 3.7 %collective-permute-start.5 = (bf16[4800,256]{1,0:T(8,128)(2,1)}, bf16[4800,256]{1,0:T(8,128)(2,1)}, u32[]{:S(2)}, u32[]{:S(2)}) collective-permute-start(bf16[4800,256]{1,0:T(8,128)(2,1)} %collective-permute-done.3.w1.t1), channel_id=1, source_target_pairs={{0,1},{1,0},{2,3},{3,2},{4,5},{5,4},{6,7},{7,6},{8,9},{9,8},{10,11... | collective-permute-start | bytes 7372808 | tf_op jit(solution)/shard_map/ppermute | solution.py:224
  69.6 1.9 %collective-permute-start.2 = (bf16[128,2432]{1,0:T(8,128)(2,1)}, bf16[128,2432]{1,0:T(8,128)(2,1)}, u32[]{:S(2)}, u32[]{:S(2)}) collective-permute-start(bf16[128,2432]{1,0:T(8,128)(2,1)} %collective-permute-done.1.far_ref.far_digits.far3_ref), channel_id=1, source_target_pairs={{0,16},{16,32},{32,48},{48,0},{1,49},{17,1},{33,17},{49,33},{2,18}... | collective-permute-start | bytes 1867784 | tf_op jit(solution)/shard_map/ppermute | solution.py:30
  71.6 0.1 stack.47.where_ref
  71.7 0.0 collective-permute-done.4.w2.t2
  71.7 5.3 %shard_map.82 = (f32[256,768]{1,0:T(8,128)S(1)}, f32[256,64]{1,0:T(8,128)S(1)}) custom-call(s32[7]{0:T(128)S(1)} %stack.47.where_ref, bf16[128,2432]{1,0:T(8,128)(2,1)} %bitcast.10.near_ref.near_digits.near3_ref, bf16[128,2432]{1,0:T(8,128)(2,1)} %collective-permute-done.1.far_ref.far_digits.far3_ref, bf16[4800,256]{1,0:T(8,128)(2,1)S(1)} %pad_maximum_fusion.w0.t0, ...), custom_call_target="tpu_custom_call" | custom-call | flops 1207959552 | bytes 7000000 | tf_op jit(solution)/shard_map/pallas_call | solution.py:163
  77.0 4.2 %collective-permute-done.2.far_ref = bf16[128,2432]{1,0:T(8,128)(2,1)} collective-permute-done((bf16[128,2432]{1,0:T(8,128)(2,1)}, bf16[128,2432]{1,0:T(8,128)(2,1)}, u32[]{:S(2)}, u32[]{:S(2)}) %collective-permute-start.2) | collective-permute-done | bytes 622624 | tf_op jit(solution)/shard_map/ppermute | solution.py:30
  81.2 0.0 collective-permute-done.5.w3.own3_ref.t3
  81.2 0.0 copy-start.5
  81.2 7.7 %shard_map.83 = f32[4,2,32,256]{3,2,1,0:T(8,128)} custom-call(s32[7]{0:T(128)S(1)} %stack.47.where_ref, bf16[128,2432]{1,0:T(8,128)(2,1)} %collective-permute-done.near_ref, bf16[128,2432]{1,0:T(8,128)(2,1)} %collective-permute-done.2.far_ref, bf16[4800,256]{1,0:T(8,128)(2,1)S(1)} %pad_maximum_fusion.w0.t0, bf16[4800,256]{1,0:T(8,128)(2,1)} %collective-permute-done.3.w1.t1, ...), custom_call_target="tpu_custom_call" | custom-call | flops 1207959552 | bytes 7000000 | tf_op jit(solution)/shard_map/pallas_call | solution.py:178
  88.9 0.0 copy-start.2
  88.9 5.0 %all-to-all-start.1 = ((f32[32,8,256]{2,1,0:T(8,128)}), f32[32,8,256]{2,1,0:T(8,128)S(1)}, u32[]{:S(2)}, u32[]{:S(2)}) async-start(f32[32,8,256]{2,1,0:T(8,128)} %bitcast.12), calls=%async_computation.1 | async-start | bytes 524288 | tf_op jit(solution)/shard_map/all_to_all | solution.py:20
  93.9 0.0 all-gather.3.cloned.1.call-done
  94.0 0.0 copy-start.1
  94.0 10.4 %all-to-all-done.1.parts_ref = f32[32,8,256]{2,1,0:T(8,128)S(1)} async-done(((f32[32,8,256]{2,1,0:T(8,128)}), f32[32,8,256]{2,1,0:T(8,128)S(1)}, u32[]{:S(2)}, u32[]{:S(2)}) %all-to-all-start.1) | async-done | bytes 262176 | tf_op jit(solution)/shard_map/all_to_all | solution.py:20
  104.4 0.7 copy-done.3
  105.1 1.9 %shard_map.84 = f32[32,8,256]{2,1,0:T(8,128)} custom-call(f32[32,8,256]{2,1,0:T(8,128)} %copy-done.3), custom_call_target="tpu_custom_call" | custom-call | flops 300000 | bytes 600000 | tf_op jit(solution)/shard_map/pallas_call | solution.py:241
  107.0 7.8 %all-to-all-start.2 = ((f32[32,8,256]{2,1,0:T(8,128)}), f32[32,8,256]{2,1,0:T(8,128)S(1)}, u32[]{:S(2)}, u32[]{:S(2)}) async-start(f32[32,8,256]{2,1,0:T(8,128)} %shard_map.84), calls=%async_computation.2 | async-start | bytes 524288 | tf_op jit(solution)/shard_map/all_to_all | solution.py:20
  114.8 0.0 copy-done.5
  114.8 0.0 copy-done
  114.8 1.4 %fusion.8 = f32[64,64]{1,0:T(8,128)S(1)} fusion(bf16[64,4608]{1,0:T(8,128)(2,1)} %param.8, bf16[4608,64]{0,1:T(8,128)(2,1)S(1)} %copy-done), kind=kOutput, calls=%fused_computation.28 | convolution fusion | flops 37748736 | bytes 1196032 | tf_op jit(solution)/shard_map/dot_general | solution.py:235
  116.2 0.1 copy.16.mapped_ref
  116.3 10.4 %all-to-all-done.2 = f32[32,8,256]{2,1,0:T(8,128)S(1)} async-done(((f32[32,8,256]{2,1,0:T(8,128)}), f32[32,8,256]{2,1,0:T(8,128)S(1)}, u32[]{:S(2)}, u32[]{:S(2)}) %all-to-all-start.2) | async-done | bytes 262176 | tf_op jit(solution)/shard_map/all_to_all | solution.py:20
  126.7 0.0 copy-done.2
  126.7 0.0 copy-done.1
  126.7 1.6 %shard_map.85 = f32[8,16]{1,0:T(8,128)} custom-call(f32[2,4,4,8,256]{4,3,2,1,0:T(8,128)S(1)} %bitcast.35, f32[64,64]{1,0:T(8,128)S(1)} %copy.16.mapped_ref, f32[32,64]{1,0:T(8,128)S(1)} %slice.6.even_ref, f32[32,64]{1,0:T(8,128)S(1)} %slice.7.odd_ref, f32[64,64]{1,0:T(8,128)S(1)} %copy-done.2, f32[128,4096]{1,0:T(8,128)S(1)} %bitcast.34), custom_call_target="tpu_custom_call" | custom-call | flops 2000000 | bytes 2500000 | tf_op jit(solution)/shard_map/pallas_call | solution.py:248
  (7 shorter events, 0.1 us)
Async XLA Ops:
  6.5 108.3 %copy-start = (bf16[4608,64]{0,1:T(8,128)(2,1)S(1)}, bf16[4608,64]{0,1:T(8,128)(2,1)}, u32[]{:S(2)}) copy-start(bf16[4608,64]{0,1:T(8,128)(2,1)} %param.11) | copy-start | bytes 1769476
  7.5 7.9 %copy-start.6 = (s32[64]{0:T(128)S(1)}, s32[64]{0:T(128)}, u32[]{:S(2)}) copy-start(s32[64]{0:T(128)} %param.9) | copy-start | bytes 772
  7.5 22.4 %copy-start.4 = (f32[1,8,4096]{2,1,0:T(8,128)S(1)}, f32[1,8,4096]{2,1,0:T(8,128)}, u32[]{:S(2)}) copy-start(f32[1,8,4096]{2,1,0:T(8,128)} %param.15) | copy-start | bytes 393220
  9.4 56.5 %collective-permute-start.3 = (bf16[4800,256]{1,0:T(8,128)(2,1)S(1)}, bf16[4800,256]{1,0:T(8,128)(2,1)}, u32[]{:S(2)}, u32[]{:S(2)}) collective-permute-start(bf16[4800,256]{1,0:T(8,128)(2,1)S(1)} %pad_maximum_fusion.w0.t0), channel_id=1, source_target_pairs={{0,2},{2,4},{4,6},{6,8},{8,10},{10,12},{12,14},{14,0},{1,15},{3,1}... | collective-permute-start | bytes 7372808 | tf_op jit(solution)/shard_map/ppermute | solution.py:30
  17.3 32.7 %all-to-all-start = ((bf16[8,16,2432]{2,1,0:T(8,128)(2,1)}), bf16[8,16,2432]{2,1,0:T(8,128)(2,1)}, u32[]{:S(2)}, u32[]{:S(2)}) async-start(bf16[8,16,2432]{2,1,0:T(8,128)(2,1)} %broadcast_in_dim.4), calls=%async_computation | async-start | bytes 1245184 | tf_op jit(solution)/shard_map/all_to_all | solution.py:20
  29.8 64.1 %all-gather.3.cloned.1.call-start = ((), (), s32[]{:S(2)}) async-start(), calls=%async_computation.3 | async-start | bytes 2359296 | tf_op jit(solution)/shard_map/all_gather | solution.py:221
  50.1 11.6 %collective-permute-start.1 = (bf16[128,2432]{1,0:T(8,128)(2,1)}, bf16[128,2432]{1,0:T(8,128)(2,1)}, u32[]{:S(2)}, u32[]{:S(2)}) collective-permute-start(bf16[128,2432]{1,0:T(8,128)(2,1)} %bitcast.10.near_ref.near_digits.near3_ref), channel_id=1, source_target_pairs={{0,64},{64,128},{128,192},{192,256},{256,320},{320,384},{384,448},... | collective-permute-start | bytes 1867784 | tf_op jit(solution)/shard_map/ppermute | solution.py:30
  54.3 11.6 %collective-permute-start = (bf16[128,2432]{1,0:T(8,128)(2,1)}, bf16[128,2432]{1,0:T(8,128)(2,1)}, u32[]{:S(2)}, u32[]{:S(2)}) collective-permute-start(bf16[128,2432]{1,0:T(8,128)(2,1)} %bitcast.10.near_ref.near_digits.near3_ref), channel_id=1, source_target_pairs={{0,16},{16,32},{32,48},{48,0},{1,49},{17,1},{33,17},{49,33},{2,18}... | collective-permute-start | bytes 1867784 | tf_op jit(solution)/shard_map/ppermute | solution.py:30
  56.3 15.3 %collective-permute-start.4 = (bf16[4800,256]{1,0:T(8,128)(2,1)S(1)}, bf16[4800,256]{1,0:T(8,128)(2,1)}, u32[]{:S(2)}, u32[]{:S(2)}) collective-permute-start(bf16[4800,256]{1,0:T(8,128)(2,1)S(1)} %pad_maximum_fusion.w0.t0), channel_id=1, source_target_pairs={{0,1},{1,0},{2,3},{3,2},{4,5},{5,4},{6,7},{7,6},{8,9},{9,8},{10,11... | collective-permute-start | bytes 7372808 | tf_op jit(solution)/shard_map/ppermute | solution.py:222
  65.9 15.3 %collective-permute-start.5 = (bf16[4800,256]{1,0:T(8,128)(2,1)}, bf16[4800,256]{1,0:T(8,128)(2,1)}, u32[]{:S(2)}, u32[]{:S(2)}) collective-permute-start(bf16[4800,256]{1,0:T(8,128)(2,1)} %collective-permute-done.3.w1.t1), channel_id=1, source_target_pairs={{0,1},{1,0},{2,3},{3,2},{4,5},{5,4},{6,7},{7,6},{8,9},{9,8},{10,11... | collective-permute-start | bytes 7372808 | tf_op jit(solution)/shard_map/ppermute | solution.py:224
  69.6 11.6 %collective-permute-start.2 = (bf16[128,2432]{1,0:T(8,128)(2,1)}, bf16[128,2432]{1,0:T(8,128)(2,1)}, u32[]{:S(2)}, u32[]{:S(2)}) collective-permute-start(bf16[128,2432]{1,0:T(8,128)(2,1)} %collective-permute-done.1.far_ref.far_digits.far3_ref), channel_id=1, source_target_pairs={{0,16},{16,32},{32,48},{48,0},{1,49},{17,1},{33,17},{49,33},{2,18}... | collective-permute-start | bytes 1867784 | tf_op jit(solution)/shard_map/ppermute | solution.py:30
  81.2 33.6 %copy-start.5 = (f32[64,64]{1,0:T(8,128)S(1)}, f32[64,64]{1,0:T(8,128)}, u32[]{:S(2)}) copy-start(f32[64,64]{1,0:T(8,128)} %param.13) | copy-start | bytes 49156
  88.9 37.8 %copy-start.2 = (f32[64,64]{1,0:T(8,128)S(1)}, f32[64,64]{1,0:T(8,128)}, u32[]{:S(2)}) copy-start(f32[64,64]{1,0:T(8,128)} %right_ref.1) | copy-start | bytes 49156
  88.9 15.5 %all-to-all-start.1 = ((f32[32,8,256]{2,1,0:T(8,128)}), f32[32,8,256]{2,1,0:T(8,128)S(1)}, u32[]{:S(2)}, u32[]{:S(2)}) async-start(f32[32,8,256]{2,1,0:T(8,128)} %bitcast.12), calls=%async_computation.1 | async-start | bytes 524288 | tf_op jit(solution)/shard_map/all_to_all | solution.py:20
  94.0 32.7 %copy-start.1 = (f32[16,8,4096]{2,1,0:T(8,128)S(1)}, f32[16,8,4096]{2,1,0:T(8,128)}, u32[]{:S(2)}) copy-start(f32[16,8,4096]{2,1,0:T(8,128)} %all-gather.3.cloned.1.call-done) | copy-start | bytes 6291460
  104.4 0.7 copy-start.3
  107.0 19.7 %all-to-all-start.2 = ((f32[32,8,256]{2,1,0:T(8,128)}), f32[32,8,256]{2,1,0:T(8,128)S(1)}, u32[]{:S(2)}, u32[]{:S(2)}) async-start(f32[32,8,256]{2,1,0:T(8,128)} %shard_map.84), calls=%async_computation.2 | async-start | bytes 524288 | tf_op jit(solution)/shard_map/all_to_all | solution.py:20
Sparse Core Ops, SparseCore 0:
  56.4 35.2 all-gather.2

commit v10 on v9

--- a/solution.py
+++ b/solution.py
@@ -11,7 +11,7 @@
 DP = ("zh", "zl", "xh")
 VOC = ("xl", "yh", "yl", "core")
 SWAP = [(0, 1), (1, 0)]
-STEPS = 3
+STEPS = 2
 DEPTH = 2304 // STEPS
 ROWS = 128
 

time: 136 us -> 135 us (level)
  Pallas kernels: 16.5 us -> 15 us
  transfers between devices with their start and end apart: 10 -> 10, of which waited for: 6 -> 6; matrix products, arithmetic and copies ran while one was open for 3% -> 3% of each run, Pallas kernels for 10% -> 9%
where the time goes in v10:
time: 135 us; the launch traced here: 134 us
  starting transfers between devices  45.2 us (33%)
  waiting for transfers between devices  44.5 us (33%)
  Pallas kernels  15 us (11%)
  between operations  13.7 us (10%)
  blocking collectives  8.92 us (7%)
  other arithmetic  2.94 us (2%)
  local copies, waits for them, and re-layouts  2.8 us (2%)
  matrix products  1.36 us (1%)
    all_to_all x3, waiting for transfers between devices, exchange(): return lax.all_to_all(blocks, axes, split_axis=0, concat_axis=0, tiled=True)  32.1 us
    all_to_all x3, starting transfers between devices, exchange(): return lax.all_to_all(blocks, axes, split_axis=0, concat_axis=0, tiled=True)  25.3 us
    ppermute x4, starting transfers between devices, both_ways(): return lax.ppermute(value, axes + ('core',), pairs)  14.1 us
    ppermute x4, waiting for transfers between devices, both_ways(): return lax.ppermute(value, axes + ('core',), pairs)  12.4 us
    all_gather x1, blocking collectives, local(): query_pair = lax.all_gather(queries[0], 'xh', axis=0)  8.92 us
    pallas_call x1, Pallas kernels, last_products(): pl.pallas_call(last_kernel, out_shape=jax.ShapeDtypeStruct((4, 2, 32, 256...  7.02 us
    pallas_call x1, Pallas kernels, first_products(): pl.pallas_call(first_kernel, out_shape=(jax.ShapeDtypeStruct((256, 768),...  4.52 us
    ppermute x1, starting transfers between devices, local(): weights = [block, moved, swapped, lax.ppermute(late, 'core', SWAP)]  3.74 us
  transfers between devices with their start and end apart: 10, of which 6 were waited for; matrix products, arithmetic and copies ran while one was open for 3% of the time, Pallas kernels for 9%

profile of v10, /device:TPU:1, one launch (start us, length us, event | category | flops | bytes accessed | tf_op | source)
XLA Modules:
  0.0 134.4 jit_solution(11763526073568720165)
XLA Ops:
  6.5 0.0 copy-start
  6.5 0.9 reduce-precision_convert_fusion.1
  7.5 0.0 copy-start.6
  7.5 0.0 copy-start.4
  7.5 1.9 %pad_maximum_fusion.w0.t0 = bf16[4800,256]{1,0:T(8,128)(2,1)S(1)} fusion(bf16[64,256]{1,0:T(8,128)(2,1)S(1)} %get-tuple-element.22, bf16[64,256]{1,0:T(8,128)(2,1)S(1)} %get-tuple-element.23, bf16[64,256]{1,0:T(8,128)(2,1)S(1)} %get-tuple-element.21, bf16[4608,256]{1,0:T(8,128)(2,1)} %param.10), kind=kLoop, calls=%fused_computation | loop fusion | flops 9830400 | bytes 4915200 | tf_op jit(solution)/shard_map/concatenate | solution.py:213
  9.4 5.9 %collective-permute-start.3 = (bf16[4800,256]{1,0:T(8,128)(2,1)S(1)}, bf16[4800,256]{1,0:T(8,128)(2,1)}, u32[]{:S(2)}, u32[]{:S(2)}) collective-permute-start(bf16[4800,256]{1,0:T(8,128)(2,1)S(1)} %pad_maximum_fusion.w0.t0), channel_id=1, source_target_pairs={{0,2},{2,4},{4,6},{6,8},{8,10},{10,12},{12,14},{14,0},{1,15},{3,1}... | collective-permute-start | bytes 7372808 | tf_op jit(solution)/shard_map/ppermute | solution.py:30
  15.3 0.0 copy-done.6
  15.3 0.1 fusion.4
  15.5 0.1 copy.17
  15.6 0.9 dynamic_slice.6
  16.5 0.9 broadcast_in_dim.4
  17.3 12.5 %all-to-all-start = ((bf16[8,16,2432]{2,1,0:T(8,128)(2,1)}), bf16[8,16,2432]{2,1,0:T(8,128)(2,1)}, u32[]{:S(2)}, u32[]{:S(2)}) async-start(bf16[8,16,2432]{2,1,0:T(8,128)(2,1)} %broadcast_in_dim.4), calls=%async_computation | async-start | bytes 1245184 | tf_op jit(solution)/shard_map/all_to_all | solution.py:20
  29.8 0.0 all-gather.3.cloned.1.call-start
  29.9 0.0 copy-done.4
  29.9 8.9 %all_gather.9 = f32[2,8,4096]{2,1,0:T(8,128)} all-gather(f32[1,8,4096]{2,1,0:T(8,128)S(1)} %copy-done.4), channel_id=1, replica_groups=mesh['zh'=4,'zl'=2,'xh'=2,'xl'=2,'yh'=4,'yl'=2,'core'=2] {'xh'}, dimensions={0}, use_global_device_ids=true | all-gather | bytes 393216 | tf_op jit(solution)/shard_map/all_gather | solution.py:215
  38.8 11.3 %all-to-all-done = bf16[8,16,2432]{2,1,0:T(8,128)(2,1)} async-done(((bf16[8,16,2432]{2,1,0:T(8,128)(2,1)}), bf16[8,16,2432]{2,1,0:T(8,128)(2,1)}, u32[]{:S(2)}, u32[]{:S(2)}) %all-to-all-start) | async-done | bytes 622624 | tf_op jit(solution)/shard_map/all_to_all | solution.py:20
  50.1 4.2 %collective-permute-start.1 = (bf16[128,2432]{1,0:T(8,128)(2,1)}, bf16[128,2432]{1,0:T(8,128)(2,1)}, u32[]{:S(2)}, u32[]{:S(2)}) collective-permute-start(bf16[128,2432]{1,0:T(8,128)(2,1)} %bitcast.10.near_ref.near_digits.near3_ref), channel_id=1, source_target_pairs={{0,64},{64,128},{128,192},{192,256},{256,320},{320,384},{384,448},... | collective-permute-start | bytes 1867784 | tf_op jit(solution)/shard_map/ppermute | solution.py:30
  54.3 2.0 %collective-permute-start = (bf16[128,2432]{1,0:T(8,128)(2,1)}, bf16[128,2432]{1,0:T(8,128)(2,1)}, u32[]{:S(2)}, u32[]{:S(2)}) collective-permute-start(bf16[128,2432]{1,0:T(8,128)(2,1)} %bitcast.10.near_ref.near_digits.near3_ref), channel_id=1, source_target_pairs={{0,16},{16,32},{32,48},{48,0},{1,49},{17,1},{33,17},{49,33},{2,18}... | collective-permute-start | bytes 1867784 | tf_op jit(solution)/shard_map/ppermute | solution.py:30
  56.3 0.0 all-gather.3.cloned.1.call-update
  56.3 2.2 %collective-permute-start.4 = (bf16[4800,256]{1,0:T(8,128)(2,1)S(1)}, bf16[4800,256]{1,0:T(8,128)(2,1)}, u32[]{:S(2)}, u32[]{:S(2)}) collective-permute-start(bf16[4800,256]{1,0:T(8,128)(2,1)S(1)} %pad_maximum_fusion.w0.t0), channel_id=1, source_target_pairs={{0,1},{1,0},{2,3},{3,2},{4,5},{5,4},{6,7},{7,6},{8,9},{9,8},{10,11... | collective-permute-start | bytes 7372808 | tf_op jit(solution)/shard_map/ppermute | solution.py:222
  58.5 3.2 %collective-permute-done.1.far_ref.far_digits.far3_ref = bf16[128,2432]{1,0:T(8,128)(2,1)} collective-permute-done((bf16[128,2432]{1,0:T(8,128)(2,1)}, bf16[128,2432]{1,0:T(8,128)(2,1)}, u32[]{:S(2)}, u32[]{:S(2)}) %collective-permute-start.1) | collective-permute-done | bytes 622624 | tf_op jit(solution)/shard_map/ppermute | solution.py:30
  61.7 4.1 %collective-permute-done.near_ref = bf16[128,2432]{1,0:T(8,128)(2,1)} collective-permute-done((bf16[128,2432]{1,0:T(8,128)(2,1)}, bf16[128,2432]{1,0:T(8,128)(2,1)}, u32[]{:S(2)}, u32[]{:S(2)}) %collective-permute-start) | collective-permute-done | bytes 622624 | tf_op jit(solution)/shard_map/ppermute | solution.py:30
  65.8 0.0 collective-permute-done.3.w1.t1
  65.9 3.7 %collective-permute-start.5 = (bf16[4800,256]{1,0:T(8,128)(2,1)}, bf16[4800,256]{1,0:T(8,128)(2,1)}, u32[]{:S(2)}, u32[]{:S(2)}) collective-permute-start(bf16[4800,256]{1,0:T(8,128)(2,1)} %collective-permute-done.3.w1.t1), channel_id=1, source_target_pairs={{0,1},{1,0},{2,3},{3,2},{4,5},{5,4},{6,7},{7,6},{8,9},{9,8},{10,11... | collective-permute-start | bytes 7372808 | tf_op jit(solution)/shard_map/ppermute | solution.py:224
  69.6 1.9 %collective-permute-start.2 = (bf16[128,2432]{1,0:T(8,128)(2,1)}, bf16[128,2432]{1,0:T(8,128)(2,1)}, u32[]{:S(2)}, u32[]{:S(2)}) collective-permute-start(bf16[128,2432]{1,0:T(8,128)(2,1)} %collective-permute-done.1.far_ref.far_digits.far3_ref), channel_id=1, source_target_pairs={{0,16},{16,32},{32,48},{48,0},{1,49},{17,1},{33,17},{49,33},{2,18}... | collective-permute-start | bytes 1867784 | tf_op jit(solution)/shard_map/ppermute | solution.py:30
  71.6 0.1 stack.47.where_ref
  71.7 0.0 collective-permute-done.4.w2.t2
  71.7 4.5 %shard_map.82 = (f32[256,768]{1,0:T(8,128)S(1)}, f32[256,64]{1,0:T(8,128)S(1)}) custom-call(s32[7]{0:T(128)S(1)} %stack.47.where_ref, bf16[128,2432]{1,0:T(8,128)(2,1)} %bitcast.10.near_ref.near_digits.near3_ref, bf16[128,2432]{1,0:T(8,128)(2,1)} %collective-permute-done.1.far_ref.far_digits.far3_ref, bf16[4800,256]{1,0:T(8,128)(2,1)S(1)} %pad_maximum_fusion.w0.t0, ...), custom_call_target="tpu_custom_call" | custom-call | flops 1207959552 | bytes 7000000 | tf_op jit(solution)/shard_map/pallas_call | solution.py:163
  76.2 5.0 %collective-permute-done.2.far_ref = bf16[128,2432]{1,0:T(8,128)(2,1)} collective-permute-done((bf16[128,2432]{1,0:T(8,128)(2,1)}, bf16[128,2432]{1,0:T(8,128)(2,1)}, u32[]{:S(2)}, u32[]{:S(2)}) %collective-permute-start.2) | collective-permute-done | bytes 622624 | tf_op jit(solution)/shard_map/ppermute | solution.py:30
  81.2 0.0 collective-permute-done.5.w3.own3_ref.t3
  81.2 0.0 copy-start.5
  81.2 7.0 %shard_map.83 = f32[4,2,32,256]{3,2,1,0:T(8,128)} custom-call(s32[7]{0:T(128)S(1)} %stack.47.where_ref, bf16[128,2432]{1,0:T(8,128)(2,1)} %collective-permute-done.near_ref, bf16[128,2432]{1,0:T(8,128)(2,1)} %collective-permute-done.2.far_ref, bf16[4800,256]{1,0:T(8,128)(2,1)S(1)} %pad_maximum_fusion.w0.t0, bf16[4800,256]{1,0:T(8,128)(2,1)} %collective-permute-done.3.w1.t1, ...), custom_call_target="tpu_custom_call" | custom-call | flops 1207959552 | bytes 7000000 | tf_op jit(solution)/shard_map/pallas_call | solution.py:178
  88.2 0.0 copy-start.2
  88.2 5.0 %all-to-all-start.1 = ((f32[32,8,256]{2,1,0:T(8,128)}), f32[32,8,256]{2,1,0:T(8,128)S(1)}, u32[]{:S(2)}, u32[]{:S(2)}) async-start(f32[32,8,256]{2,1,0:T(8,128)} %bitcast.12), calls=%async_computation.1 | async-start | bytes 524288 | tf_op jit(solution)/shard_map/all_to_all | solution.py:20
  93.2 0.0 all-gather.3.cloned.1.call-done
  93.3 0.0 copy-start.1
  93.3 10.4 %all-to-all-done.1.parts_ref = f32[32,8,256]{2,1,0:T(8,128)S(1)} async-done(((f32[32,8,256]{2,1,0:T(8,128)}), f32[32,8,256]{2,1,0:T(8,128)S(1)}, u32[]{:S(2)}, u32[]{:S(2)}) %all-to-all-start.1) | async-done | bytes 262176 | tf_op jit(solution)/shard_map/all_to_all | solution.py:20
  103.7 0.7 copy-done.3
  104.4 1.9 %shard_map.84 = f32[32,8,256]{2,1,0:T(8,128)} custom-call(f32[32,8,256]{2,1,0:T(8,128)} %copy-done.3), custom_call_target="tpu_custom_call" | custom-call | flops 300000 | bytes 600000 | tf_op jit(solution)/shard_map/pallas_call | solution.py:241
  106.3 7.8 %all-to-all-start.2 = ((f32[32,8,256]{2,1,0:T(8,128)}), f32[32,8,256]{2,1,0:T(8,128)S(1)}, u32[]{:S(2)}, u32[]{:S(2)}) async-start(f32[32,8,256]{2,1,0:T(8,128)} %shard_map.84), calls=%async_computation.2 | async-start | bytes 524288 | tf_op jit(solution)/shard_map/all_to_all | solution.py:20
  114.0 0.0 copy-done.5
  114.1 0.0 copy-done
  114.1 1.4 %fusion.8 = f32[64,64]{1,0:T(8,128)S(1)} fusion(bf16[64,4608]{1,0:T(8,128)(2,1)} %param.8, bf16[4608,64]{0,1:T(8,128)(2,1)S(1)} %copy-done), kind=kOutput, calls=%fused_computation.28 | convolution fusion | flops 37748736 | bytes 1196032 | tf_op jit(solution)/shard_map/dot_general | solution.py:235
  115.5 0.1 copy.16.mapped_ref
  115.5 10.4 %all-to-all-done.2 = f32[32,8,256]{2,1,0:T(8,128)S(1)} async-done(((f32[32,8,256]{2,1,0:T(8,128)}), f32[32,8,256]{2,1,0:T(8,128)S(1)}, u32[]{:S(2)}, u32[]{:S(2)}) %all-to-all-start.2) | async-done | bytes 262176 | tf_op jit(solution)/shard_map/all_to_all | solution.py:20
  126.0 0.0 copy-done.2
  126.0 0.0 copy-done.1
  126.0 1.6 %shard_map.85 = f32[8,16]{1,0:T(8,128)} custom-call(f32[2,4,4,8,256]{4,3,2,1,0:T(8,128)S(1)} %bitcast.35, f32[64,64]{1,0:T(8,128)S(1)} %copy.16.mapped_ref, f32[32,64]{1,0:T(8,128)S(1)} %slice.6.even_ref, f32[32,64]{1,0:T(8,128)S(1)} %slice.7.odd_ref, f32[64,64]{1,0:T(8,128)S(1)} %copy-done.2, f32[128,4096]{1,0:T(8,128)S(1)} %bitcast.34), custom_call_target="tpu_custom_call" | custom-call | flops 2000000 | bytes 2500000 | tf_op jit(solution)/shard_map/pallas_call | solution.py:248
  (7 shorter events, 0.1 us)
Async XLA Ops:
  6.5 107.5 %copy-start = (bf16[4608,64]{0,1:T(8,128)(2,1)S(1)}, bf16[4608,64]{0,1:T(8,128)(2,1)}, u32[]{:S(2)}) copy-start(bf16[4608,64]{0,1:T(8,128)(2,1)} %param.11) | copy-start | bytes 1769476
  7.5 7.9 %copy-start.6 = (s32[64]{0:T(128)S(1)}, s32[64]{0:T(128)}, u32[]{:S(2)}) copy-start(s32[64]{0:T(128)} %param.9) | copy-start | bytes 772
  7.5 22.4 %copy-start.4 = (f32[1,8,4096]{2,1,0:T(8,128)S(1)}, f32[1,8,4096]{2,1,0:T(8,128)}, u32[]{:S(2)}) copy-start(f32[1,8,4096]{2,1,0:T(8,128)} %param.15) | copy-start | bytes 393220
  9.4 56.5 %collective-permute-start.3 = (bf16[4800,256]{1,0:T(8,128)(2,1)S(1)}, bf16[4800,256]{1,0:T(8,128)(2,1)}, u32[]{:S(2)}, u32[]{:S(2)}) collective-permute-start(bf16[4800,256]{1,0:T(8,128)(2,1)S(1)} %pad_maximum_fusion.w0.t0), channel_id=1, source_target_pairs={{0,2},{2,4},{4,6},{6,8},{8,10},{10,12},{12,14},{14,0},{1,15},{3,1}... | collective-permute-start | bytes 7372808 | tf_op jit(solution)/shard_map/ppermute | solution.py:30
  17.3 32.7 %all-to-all-start = ((bf16[8,16,2432]{2,1,0:T(8,128)(2,1)}), bf16[8,16,2432]{2,1,0:T(8,128)(2,1)}, u32[]{:S(2)}, u32[]{:S(2)}) async-start(bf16[8,16,2432]{2,1,0:T(8,128)(2,1)} %broadcast_in_dim.4), calls=%async_computation | async-start | bytes 1245184 | tf_op jit(solution)/shard_map/all_to_all | solution.py:20
  29.8 63.4 %all-gather.3.cloned.1.call-start = ((), (), s32[]{:S(2)}) async-start(), calls=%async_computation.3 | async-start | bytes 2359296 | tf_op jit(solution)/shard_map/all_gather | solution.py:221
  50.1 11.6 %collective-permute-start.1 = (bf16[128,2432]{1,0:T(8,128)(2,1)}, bf16[128,2432]{1,0:T(8,128)(2,1)}, u32[]{:S(2)}, u32[]{:S(2)}) collective-permute-start(bf16[128,2432]{1,0:T(8,128)(2,1)} %bitcast.10.near_ref.near_digits.near3_ref), channel_id=1, source_target_pairs={{0,64},{64,128},{128,192},{192,256},{256,320},{320,384},{384,448},... | collective-permute-start | bytes 1867784 | tf_op jit(solution)/shard_map/ppermute | solution.py:30
  54.3 11.6 %collective-permute-start = (bf16[128,2432]{1,0:T(8,128)(2,1)}, bf16[128,2432]{1,0:T(8,128)(2,1)}, u32[]{:S(2)}, u32[]{:S(2)}) collective-permute-start(bf16[128,2432]{1,0:T(8,128)(2,1)} %bitcast.10.near_ref.near_digits.near3_ref), channel_id=1, source_target_pairs={{0,16},{16,32},{32,48},{48,0},{1,49},{17,1},{33,17},{49,33},{2,18}... | collective-permute-start | bytes 1867784 | tf_op jit(solution)/shard_map/ppermute | solution.py:30
  56.3 15.3 %collective-permute-start.4 = (bf16[4800,256]{1,0:T(8,128)(2,1)S(1)}, bf16[4800,256]{1,0:T(8,128)(2,1)}, u32[]{:S(2)}, u32[]{:S(2)}) collective-permute-start(bf16[4800,256]{1,0:T(8,128)(2,1)S(1)} %pad_maximum_fusion.w0.t0), channel_id=1, source_target_pairs={{0,1},{1,0},{2,3},{3,2},{4,5},{5,4},{6,7},{7,6},{8,9},{9,8},{10,11... | collective-permute-start | bytes 7372808 | tf_op jit(solution)/shard_map/ppermute | solution.py:222
  65.9 15.3 %collective-permute-start.5 = (bf16[4800,256]{1,0:T(8,128)(2,1)}, bf16[4800,256]{1,0:T(8,128)(2,1)}, u32[]{:S(2)}, u32[]{:S(2)}) collective-permute-start(bf16[4800,256]{1,0:T(8,128)(2,1)} %collective-permute-done.3.w1.t1), channel_id=1, source_target_pairs={{0,1},{1,0},{2,3},{3,2},{4,5},{5,4},{6,7},{7,6},{8,9},{9,8},{10,11... | collective-permute-start | bytes 7372808 | tf_op jit(solution)/shard_map/ppermute | solution.py:224
  69.6 11.6 %collective-permute-start.2 = (bf16[128,2432]{1,0:T(8,128)(2,1)}, bf16[128,2432]{1,0:T(8,128)(2,1)}, u32[]{:S(2)}, u32[]{:S(2)}) collective-permute-start(bf16[128,2432]{1,0:T(8,128)(2,1)} %collective-permute-done.1.far_ref.far_digits.far3_ref), channel_id=1, source_target_pairs={{0,16},{16,32},{32,48},{48,0},{1,49},{17,1},{33,17},{49,33},{2,18}... | collective-permute-start | bytes 1867784 | tf_op jit(solution)/shard_map/ppermute | solution.py:30
  81.2 32.8 %copy-start.5 = (f32[64,64]{1,0:T(8,128)S(1)}, f32[64,64]{1,0:T(8,128)}, u32[]{:S(2)}) copy-start(f32[64,64]{1,0:T(8,128)} %param.13) | copy-start | bytes 49156
  88.2 37.7 %copy-start.2 = (f32[64,64]{1,0:T(8,128)S(1)}, f32[64,64]{1,0:T(8,128)}, u32[]{:S(2)}) copy-start(f32[64,64]{1,0:T(8,128)} %right_ref.1) | copy-start | bytes 49156
  88.2 15.5 %all-to-all-start.1 = ((f32[32,8,256]{2,1,0:T(8,128)}), f32[32,8,256]{2,1,0:T(8,128)S(1)}, u32[]{:S(2)}, u32[]{:S(2)}) async-start(f32[32,8,256]{2,1,0:T(8,128)} %bitcast.12), calls=%async_computation.1 | async-start | bytes 524288 | tf_op jit(solution)/shard_map/all_to_all | solution.py:20
  93.3 32.7 %copy-start.1 = (f32[16,8,4096]{2,1,0:T(8,128)S(1)}, f32[16,8,4096]{2,1,0:T(8,128)}, u32[]{:S(2)}) copy-start(f32[16,8,4096]{2,1,0:T(8,128)} %all-gather.3.cloned.1.call-done) | copy-start | bytes 6291460
  103.7 0.7 copy-start.3
  106.3 19.7 %all-to-all-start.2 = ((f32[32,8,256]{2,1,0:T(8,128)}), f32[32,8,256]{2,1,0:T(8,128)S(1)}, u32[]{:S(2)}, u32[]{:S(2)}) async-start(f32[32,8,256]{2,1,0:T(8,128)} %shard_map.84), calls=%async_computation.2 | async-start | bytes 524288 | tf_op jit(solution)/shard_map/all_to_all | solution.py:20
Sparse Core Ops, SparseCore 0:
  56.4 35.2 all-gather.2
